TPU v7x, 32 devices: a whole 2x2x4 slice. The times are simulated.
32 devices in a mesh: expert: 8 (over y, x, core), tensor: 4 (over z).
Axes of the slice: x: 2, y: 2, z: 4, core: 2. Of those that a mesh axis runs over, the one named last changes fastest.
Arguments:
- tokens: bfloat16 [12608, 512], P(('expert', 'tensor')), may hold values from -6 to 6
- norm1_gain: float32 [512], replicated, may hold values from 0.1 to 1.9
- w_qkv: bfloat16 [512, 3, 512], P(None, None, 'tensor'), may hold values from -0.25 to 0.25
- w_out: bfloat16 [512, 512], P('tensor'), may hold values from -1.5 to 1.5
- norm2_gain: float32 [512], replicated, may hold values from 0.1 to 1.9
- w_router: bfloat16 [512, 8], replicated, may hold values from -0.125 to 0.125
- noise: float32 [12608, 8], P(('expert', 'tensor')), may hold values from -3 to 3
- routes: int32 [12608, 2], P(('expert', 'tensor')), may hold values from 0 to 7, all different within a row; in each aligned block of 394 rows (0 to 393, 394 to 787, ...) at most 197 rows name the same one
- w_in: bfloat16 [8, 512, 2048], P('expert', None, 'tensor'), may hold values from -0.25 to 0.25
- w_back: bfloat16 [8, 2048, 512], P('expert', 'tensor'), may hold values from -3 to 3
- cotangent: bfloat16 [12608, 512], P(('expert', 'tensor')), may hold values from -6 to 6
Outputs:
- output: bfloat16 [12608, 512], P(('expert', 'tensor'))
- grad_tokens: float32 [12608, 512], P(('expert', 'tensor'))
- grad_norm1: float32 [512], replicated
- grad_qkv: float32 [512, 3, 512], P(None, None, 'tensor')
- grad_out: float32 [512, 512], P('tensor')
- grad_norm2: float32 [512], replicated
- grad_router: float32 [512, 8], replicated
- grad_in: float32 [8, 512, 2048], P('expert', None, 'tensor')
- grad_back: float32 [8, 2048, 512], P('expert', 'tensor')
Inputs may be any that keep to these rules, and one draw needn't show every extreme that they name: `routes`: within the rows of one device (aligned blocks of 394 rows) no expert is named by more than 197 rows, a bound that some block reaches; a row names two different experts.
All inputs are finite; a program needn't handle non-finite values.
Results may differ from a plain program's by a relative error of at most 0.023.
Values may be sent and summed in bfloat16 or wider, within the bound.
A program may use at most 192 MiB of HBM per device.

v0:
```python
import jax
import jax.numpy as jnp
from jax import lax
from jax.sharding import PartitionSpec as P

D = 512
HD = 64
TOP = 2
SEQ = 197


epsilon = 1e-06


def gelu_exact(values):
    return jax.nn.gelu(values, approximate=False)


def layer_norm(values, gain_vec):
    center = values - jnp.mean(values, -1, keepdims=True)
    spread = jnp.mean(center * center, -1, keepdims=True)
    inverse = lax.rsqrt(spread + epsilon)
    normed = center * inverse
    return (normed * gain_vec, normed, inverse)


def norm_back(grad_rows, normed, inverse, gain_vec):
    scaled = grad_rows * gain_vec
    inner = (
        scaled
        - jnp.mean(scaled, -1, keepdims=True)
        - normed * jnp.mean(scaled * normed, -1, keepdims=True)
    )
    return (inverse * inner, jnp.sum(grad_rows * normed, axis=0))


def dispatch(buffer):
    experts, capacity, features = buffer.shape
    copies = lax.all_gather(buffer, "tensor", axis=0, tiled=True)
    copies = copies.reshape(lax.axis_size("tensor"), experts, capacity, features)
    arrived = lax.all_to_all(copies, "expert", split_axis=1, concat_axis=1, tiled=True)
    return arrived.reshape(-1, features)


def collect(term_fn, row_count, layout):
    summed = lax.psum_scatter(
        term_fn(jnp.int32(0), row_count * lax.axis_size("tensor")).astype(jnp.bfloat16),
        "tensor",
        scatter_dimension=0,
        tiled=True,
    )
    arrived = lax.all_to_all(
        summed.reshape(layout), "expert", split_axis=0, concat_axis=0, tiled=True
    )
    return arrived.reshape(row_count, layout[2])


def per_device(
    tokens, norm1_gain, w_qkv, w_out, norm2_gain, w_router, noise, routes, w_in, w_back, cotangent
):
    inputs = tokens.astype(jnp.float32)
    own_rows = inputs.shape[0]
    experts = noise.shape[1]
    capacity = (2 * own_rows * TOP + experts - 1) // experts
    local_width = w_out.shape[0]
    local_heads = local_width // HD
    scaling = HD ** (-0.5)
    layout = (experts, capacity, D)
    slot_count = experts * capacity
    first_proj, second_proj = (w_in[0], w_back[0])
    normed1_f, unit1, inverse1 = layer_norm(inputs, norm1_gain)
    normed1 = normed1_f.astype(jnp.bfloat16)
    qkv_matrix = w_qkv.reshape(D, 3 * local_width)
    projected = jnp.dot(
        lax.all_gather(normed1, "tensor", axis=0, tiled=True),
        qkv_matrix,
        preferred_element_type=jnp.float32,
    ).astype(jnp.bfloat16)
    all_rows = projected.shape[0]
    images = all_rows // SEQ
    split_heads = projected.reshape(images, SEQ, 3, local_heads, HD)
    queries = split_heads[:, :, 0]
    key_rows = split_heads[:, :, 1]
    value_rows = split_heads[:, :, 2]
    scores = (
        jnp.einsum("bqhd,bkhd->bhqk", queries, key_rows, preferred_element_type=jnp.float32)
        * scaling
    )
    row_max = jnp.max(scores, -1, keepdims=True)
    log_norm = row_max + jnp.log(jnp.sum(jnp.exp(scores - row_max), -1, keepdims=True))
    attend_low = jnp.exp(scores - log_norm).astype(jnp.bfloat16)
    mixed = jnp.einsum(
        "bhqk,bkhd->bqhd", attend_low, value_rows, preferred_element_type=jnp.float32
    )
    mixed = mixed.astype(jnp.bfloat16).reshape(all_rows, local_width)
    attention = lax.psum_scatter(
        jnp.dot(mixed, w_out, preferred_element_type=jnp.float32),
        "tensor",
        scatter_dimension=0,
        tiled=True,
    )
    residual = inputs + attention
    normed2_f, unit2, inverse2 = layer_norm(residual, norm2_gain)
    normed2 = normed2_f.astype(jnp.bfloat16)
    normed2_wide = normed2.astype(jnp.float32)
    router_matrix = w_router.astype(jnp.float32)
    logits = jnp.dot(normed2, w_router, preferred_element_type=jnp.float32) + noise
    router = jax.nn.softmax(logits, axis=-1)
    gate_vals = jnp.take_along_axis(router, routes, axis=1)
    picked = routes.reshape(-1)
    one_hot = (picked[:, None] == jnp.arange(experts, dtype=jnp.int32)[None, :]).astype(jnp.int32)
    places = jnp.sum(one_hot * (jnp.cumsum(one_hot, axis=0) - 1), axis=1)
    slot_ids = picked * capacity + places
    owners = (
        jnp.zeros((slot_count,), jnp.int32)
        .at[slot_ids]
        .set(jnp.arange(picked.shape[0], dtype=jnp.int32) + 1)
    )
    filled = (owners > 0)[:, None]
    pair_index = jnp.maximum(owners - 1, 0)
    send_rows = jnp.where(
        filled, jnp.take(normed2, pair_index // TOP, axis=0), jnp.zeros((), jnp.bfloat16)
    )
    send_rows = send_rows.reshape(layout)
    routed = dispatch(send_rows)
    pre_act = jnp.dot(routed, first_proj, preferred_element_type=jnp.float32)
    activated, gelu_pull = jax.vjp(gelu_exact, pre_act)
    act_low = activated.astype(jnp.bfloat16)

    def out_term(offset, row_count):
        return jnp.dot(act_low, second_proj, preferred_element_type=jnp.float32)

    returned = collect(out_term, slot_count, layout)
    paired = jnp.take(returned, slot_ids, axis=0).astype(jnp.float32).reshape(own_rows, TOP, D)
    output = (residual + jnp.sum(gate_vals[:, :, None] * paired, axis=1)).astype(jnp.bfloat16)
    upstream = cotangent.astype(jnp.float32)
    d_gates = jnp.sum(upstream[:, None, :] * paired, axis=-1)
    grad_pairs = (gate_vals[:, :, None] * upstream[:, None, :]).astype(jnp.bfloat16).reshape(-1, D)
    send_grads = jnp.where(
        filled, jnp.take(grad_pairs, pair_index, axis=0), jnp.zeros((), jnp.bfloat16)
    )
    grad_rows = dispatch(send_grads.reshape(layout))
    routed_back = dispatch(send_rows)
    pre_back = jnp.dot(routed_back, first_proj, preferred_element_type=jnp.float32)
    act_back, pull_back = jax.vjp(gelu_exact, pre_back)
    act_back = act_back.astype(jnp.bfloat16)
    grad_back = jnp.einsum("rf,rd->fd", act_back, grad_rows, preferred_element_type=jnp.float32)
    d_act = jnp.einsum("rd,fd->rf", grad_rows, second_proj, preferred_element_type=jnp.float32)
    d_pre = pull_back(d_act)[0].astype(jnp.bfloat16)
    grad_in = jnp.einsum("rd,rf->df", routed_back, d_pre, preferred_element_type=jnp.float32)

    def in_term(offset, row_count):
        return jnp.einsum("rf,df->rd", d_pre, first_proj, preferred_element_type=jnp.float32)

    returned_grads = collect(in_term, slot_count, layout)
    d_routed = (
        jnp.take(returned_grads, slot_ids, axis=0).astype(jnp.float32).reshape(own_rows, TOP, D)
    )
    chosen = (routes[:, :, None] == jnp.arange(experts, dtype=jnp.int32)[None, None, :]).astype(
        jnp.float32
    )
    d_router = jnp.sum(chosen * d_gates[:, :, None], axis=1)
    d_logits = router * (d_router - jnp.sum(router * d_router, -1, keepdims=True))
    grad_router = jnp.einsum("sd,se->de", normed2_wide, d_logits, precision=lax.Precision.HIGHEST)
    d_normed2 = jnp.sum(d_routed, axis=1) + jnp.dot(
        d_logits, router_matrix.T, precision=lax.Precision.HIGHEST
    )
    d_norm2_rows, grad_norm2 = norm_back(d_normed2, unit2, inverse2, norm2_gain)
    d_residual = upstream + d_norm2_rows
    d_attention = lax.all_gather(d_residual.astype(jnp.bfloat16), "tensor", axis=0, tiled=True)
    grad_out = jnp.einsum("tc,td->cd", mixed, d_attention, preferred_element_type=jnp.float32)
    d_mixed = jnp.einsum("td,cd->tc", d_attention, w_out, preferred_element_type=jnp.float32)
    d_mixed = d_mixed.astype(jnp.bfloat16).reshape(images, SEQ, local_heads, HD)
    scores_again = (
        jnp.einsum("bqhd,bkhd->bhqk", queries, key_rows, preferred_element_type=jnp.float32)
        * scaling
    )
    attend_again = jnp.exp(scores_again - log_norm)
    d_values = jnp.einsum(
        "bhqk,bqhd->bkhd",
        attend_again.astype(jnp.bfloat16),
        d_mixed,
        preferred_element_type=jnp.float32,
    ).astype(jnp.bfloat16)
    d_attend = jnp.einsum(
        "bqhd,bkhd->bhqk", d_mixed, value_rows, preferred_element_type=jnp.float32
    )
    d_scores = attend_again * (d_attend - jnp.sum(attend_again * d_attend, -1, keepdims=True))
    d_scores = d_scores.astype(jnp.bfloat16)
    d_queries = (
        jnp.einsum("bhqk,bkhd->bqhd", d_scores, key_rows, preferred_element_type=jnp.float32)
        * scaling
    ).astype(jnp.bfloat16)
    d_keys = (
        jnp.einsum("bhqk,bqhd->bkhd", d_scores, queries, preferred_element_type=jnp.float32)
        * scaling
    ).astype(jnp.bfloat16)
    grad_qkv_rows = jnp.stack([d_queries, d_keys, d_values], axis=2).reshape(
        all_rows, 3 * local_width
    )
    grad_qkv_local = jnp.einsum(
        "td,tc->dc",
        lax.all_gather(normed1, "tensor", axis=0, tiled=True),
        grad_qkv_rows,
        preferred_element_type=jnp.float32,
    )
    d_normed1 = lax.psum_scatter(
        jnp.einsum(
            "tc,dc->td", grad_qkv_rows, qkv_matrix, preferred_element_type=jnp.float32
        ).astype(jnp.bfloat16),
        "tensor",
        scatter_dimension=0,
        tiled=True,
    ).astype(jnp.float32)
    d_norm1_rows, grad_norm1 = norm_back(d_normed1, unit1, inverse1, norm1_gain)
    grad_tokens = d_residual + d_norm1_rows
    grad_qkv_sum, grad_out_sum = (
        lax.psum(grad_qkv_local.astype(jnp.bfloat16), "expert").astype(jnp.float32),
        lax.psum(grad_out.astype(jnp.bfloat16), "expert").astype(jnp.float32),
    )
    router_sum, norm1_sum, norm2_sum = lax.psum(
        (grad_router, grad_norm1, grad_norm2), ("expert", "tensor")
    )
    return (
        output,
        grad_tokens,
        norm1_sum,
        grad_qkv_sum.reshape(D, 3, local_width),
        grad_out_sum,
        norm2_sum,
        router_sum,
        grad_in[None],
        grad_back[None],
    )


def solution(mesh):
    placed = (
        P(("expert", "tensor"), None),
        P(),
        P(None, None, "tensor"),
        P("tensor", None),
        P(),
        P(),
        P(("expert", "tensor"), None),
        P(("expert", "tensor"), None),
        P("expert", None, "tensor"),
        P("expert", "tensor", None),
        P(("expert", "tensor"), None),
    )
    return jax.shard_map(
        per_device,
        mesh=mesh,
        in_specs=placed,
        out_specs=(
            P(("expert", "tensor"), None),
            P(("expert", "tensor"), None),
            P(),
            P(None, None, "tensor"),
            P("tensor", None),
            P(),
            P(),
            P("expert", None, "tensor"),
            P("expert", "tensor", None),
        ),
        check_vma=False,
    )
```

profile of v0, /device:TPU:0, one launch (start us, length us, event | category | flops | bytes accessed | tf_op | source)
XLA Modules:
  0.0 1154.8 jit_solution(15634142382134725678)
XLA Ops:
  18.1 5.3 scatter_custom_fusion
  23.4 29.9 %all-gather.11.cloned.1.call-done = bf16[4,394,512]{2,1,0:T(8,128)(2,1)} async-done(((bf16[1,394,512]{2,1,0:T(8,128)(2,1)}), bf16[4,394,512]{2,1,0:T(8,128)(2,1)}) %all-gather.11.cloned.1.call-update) | async-done | bytes 1613840 | tf_op jit(solution)/shard_map/all_gather | solution.py:75
  58.4 4.5 reshape.320
  70.7 2.7 copy.161
  79.8 61.4 %fusion = f32[400,512]{1,0:T(8,128)S(1)} fusion(f32[1576,512]{1,0:T(8,128)} %fusion.64), kind=kCustom, calls=%all-reduce-scatter | all-reduce-scatter fusion | flops 819201 | bytes 4047360
  144.4 3.4 concatenate.3
  150.4 6.0 gather_fusion
  160.7 118.0 %all-gather.7.cloned.1.call-done = bf16[32,197,512]{2,0,1:T(8,128)(2,1)} async-done(((bf16[8,197,512]{2,0,1:T(8,128)(2,1)}), bf16[32,197,512]{2,0,1:T(8,128)(2,1)}) %all-gather.7.cloned.1.call-update) | async-done | bytes 6455312 | tf_op jit(solution)/shard_map/all_gather | solution.py:39
  278.6 8.8 copy.136
  287.5 77.0 %all_to_all.21 = bf16[4,8,197,512]{3,0,2,1:T(4,128)(2,1)S(1)} all-to-all(bf16[4,8,197,512]{3,0,2,1:T(4,128)(2,1)} %copy.136), channel_id=1, replica_groups=mesh['expert'=8,'tensor'=4] {'expert'}, dimensions={1} | all-to-all | bytes 12910592 | tf_op jit(solution)/shard_map/all_to_all | solution.py:41
  364.5 4.1 copy.137
  368.5 6.7 reshape.238
  375.2 33.6 %multiply_convert_fusion = (bf16[6304,512]{1,0:T(8,128)(2,1)S(1)}, f32[6304,512]{1,0:T(8,128)}, f32[6304,512]{1,0:T(8,128)}) fusion(bf16[6304,512]{1,0:T(8,128)(2,1)} %reshape.238, bf16[1,512,512]{2,1,0:T(8,128)(2,1)S(1)} %copy-done), kind=kOutput, calls=%fused_computation.9 | convolution fusion | flops 3514908672 | bytes 39256064 | tf_op jit(solution)/shard_map/dot_general | solution.py:126
  411.5 5.4 convolution_convert_fusion.1
  416.9 109.9 %reduce-scatter.7.cloned.1.call-done = bf16[1576,512]{1,0:T(8,128)(2,1)} async-done(((bf16[6304,512]{1,0:T(8,128)(2,1)}), bf16[1576,512]{1,0:T(8,128)(2,1)}) %reduce-scatter.7.cloned.1.call-update) | async-done | bytes 1613840 | tf_op jit(solution)/shard_map/reduce_scatter | solution.py:46
  526.8 3.1 reshape.239
  529.9 4.3 all-to-all-start.1
  538.2 17.8 %all-to-all-done.1 = bf16[8,197,512]{2,1,0:T(8,128)(2,1)} async-done(((bf16[8,197,512]{2,1,0:T(8,128)(2,1)}), bf16[8,197,512]{2,1,0:T(8,128)(2,1)}, u32[]{:S(2)}, u32[]{:S(2)}) %all-to-all-start.1) | async-done | bytes 1613856 | tf_op jit(solution)/shard_map/all_to_all | solution.py:52
  557.9 3.4 gather_fusion.3
  563.9 8.1 gather_fusion.2
  573.5 6.0 gather_fusion.1
  583.8 116.9 %all-gather.9.cloned.1.call-done = bf16[32,197,512]{2,0,1:T(8,128)(2,1)} async-done(((bf16[8,197,512]{2,0,1:T(8,128)(2,1)}), bf16[32,197,512]{2,0,1:T(8,128)(2,1)}) %all-gather.9.cloned.1.call-update) | async-done | bytes 6455312 | tf_op jit(solution)/shard_map/all_gather | solution.py:39
  700.7 8.9 copy.140
  709.5 77.2 %all_to_all.22 = bf16[4,8,197,512]{3,0,2,1:T(4,128)(2,1)S(1)} all-to-all(bf16[4,8,197,512]{3,0,2,1:T(4,128)(2,1)} %copy.140), channel_id=1, replica_groups=mesh['expert'=8,'tensor'=4] {'expert'}, dimensions={1} | all-to-all | bytes 12910592 | tf_op jit(solution)/shard_map/all_to_all | solution.py:41
  786.7 4.1 copy.141
  790.8 6.7 reshape.243
  797.5 15.0 %add_convert_fusion = bf16[6304,512]{1,0:T(8,128)(2,1)} fusion(f32[6304,512]{1,0:T(8,128)} %get-tuple-element.28, f32[6304,512]{1,0:T(8,128)} %get-tuple-element.43, bf16[6304,512]{1,0:T(8,128)(2,1)} %reshape.243, bf16[1,512,512]{2,1,0:T(8,128)(2,1)S(1)} %copy-done.45), kind=kOutput, calls=%fused_computation.8 | convolution fusion | flops 3350298624 | bytes 39256064 | tf_op jit(solution)/shard_map/rd,fd->rf/dot_general | solution.py:148
  812.5 8.3 convolution_convert_fusion
  820.9 109.9 %reduce-scatter.9.cloned.1.call-done = bf16[1576,512]{1,0:T(8,128)(2,1)} async-done(((bf16[6304,512]{1,0:T(8,128)(2,1)}), bf16[1576,512]{1,0:T(8,128)(2,1)}) %reduce-scatter.9.cloned.1.call-update) | async-done | bytes 1613840 | tf_op jit(solution)/shard_map/reduce_scatter | solution.py:46
  930.9 3.1 reshape.244
  934.0 26.3 %all_to_all.23 = bf16[8,197,512]{2,1,0:T(8,128)(2,1)} all-to-all(bf16[8,197,512]{2,1,0:T(8,128)(2,1)} %reshape.244), channel_id=1, replica_groups=mesh['expert'=8,'tensor'=4] {'expert'}, dimensions={0} | all-to-all | bytes 3227648 | tf_op jit(solution)/shard_map/all_to_all | solution.py:52
  962.2 3.9 gather_fusion.4
  966.2 3.1 select_convert_fusion
  971.6 3.1 reshape.241
  974.7 4.5 multiply_reduce_fusion.3
  979.2 3.0 reduce_sum.182
  984.3 2.8 convert_bitcast_fusion
  987.7 9.3 convolution_bitcast_fusion
  996.9 9.3 convolution_bitcast_fusion.1
  1006.2 17.9 %all-gather.13.cloned.1.call-done = bf16[4,394,512]{2,1,0:T(8,128)(2,1)} async-done(((bf16[1,394,512]{2,1,0:T(8,128)(2,1)}), bf16[4,394,512]{2,1,0:T(8,128)(2,1)}) %all-gather.13.cloned.1.call-update) | async-done | bytes 1613840 | tf_op jit(solution)/shard_map/all_gather | solution.py:170
  1027.8 3.3 copy.144
  1031.1 2.9 fusion.12
  1040.7 4.0 reshape.249
  1044.7 3.5 convolution_convert_fusion.7
  1048.2 3.6 convolution_convert_fusion.2
  1051.8 34.4 %fusion.1 = bf16[400,512]{1,0:T(8,128)(2,1)S(1)} fusion(bf16[1576,512]{1,0:T(8,128)(2,1)} %convolution_convert_fusion.2), kind=kCustom, calls=%all-reduce-scatter.1 | all-reduce-scatter fusion | flops 819201 | bytes 2023936
  1092.8 39.8 %all-reduce.5 = (f32[512]{0:T(512)}, f32[512]{0:T(512)}, f32[512,8]{0,1:T(8,128)}) all-reduce(f32[512]{0:T(512)S(1)} %get-tuple-element.12, f32[512]{0:T(512)S(1)} %get-tuple-element.10, f32[512,8]{0,1:T(8,128)S(1)} %fusion.53), channel_id=1, replica_groups=mesh['expert'=8,'tensor'=4] {'expert','tensor'}, use_global_device_ids=true, to_apply=%region_27.29 | all-reduce | flops 5120 | bytes 40960 | tf_op jit(solution)/shard_map/psum | solution.py:221
  1135.1 8.8 all-reduce.9.cloned.1.call-done
  (211 shorter events, 85.6 us)
Async XLA Ops:
  7.2 368.1 %copy-start = (bf16[1,512,512]{2,1,0:T(8,128)(2,1)S(1)}, bf16[1,512,512]{2,1,0:T(8,128)(2,1)}, u32[]{:S(2)}) copy-start(bf16[1,512,512]{2,1,0:T(8,128)(2,1)} %param.21) | copy-start | bytes 1572868
  7.2 46.1 %all-gather.11.cloned.1.call-start = ((), (), s32[]{:S(2)}) async-start(), calls=%async_computation.10 | async-start | bytes 2048000 | tf_op jit(solution)/shard_map/all_gather | solution.py:75
  12.3 266.3 %all-gather.7.cloned.1.call-start = ((), (), s32[]{:S(2)}) async-start(), calls=%async_computation.6 | async-start | bytes 8069120 | tf_op jit(solution)/shard_map/all_gather | solution.py:39
  18.0 37.2 %copy-start.25 = (bf16[512,3,128]{0,2,1:T(8,128)(2,1)}, bf16[512,3,128]{0,2,1:T(8,128)(2,1)S(1)}, u32[]{:S(2)}) copy-start(bf16[512,3,128]{0,2,1:T(8,128)(2,1)S(1)} %copy.121) | copy-start | bytes 1179652
  68.0 6.8 copy-start.10
  70.7 5.9 copy-start.14
  73.4 3.6 copy-start.12
  73.4 4.1 copy-start.21
  75.9 67.3 %copy-start.43 = (u32[32]{0:T(128)S(1)}, u32[32]{0:T(128)}, u32[]{:S(2)}) copy-start(u32[32]{0:T(128)} %constant.196) | copy-start | bytes 388
  76.6 71.3 %copy-start.5 = (bf16[394,512]{1,0:T(8,128)(2,1)S(1)}, bf16[394,512]{1,0:T(8,128)(2,1)}, u32[]{:S(2)}) copy-start(bf16[394,512]{1,0:T(8,128)(2,1)} %param.13) | copy-start | bytes 1210372
  77.5 72.9 %copy-start.16 = (bf16[1576,128]{0,1:T(8,128)(2,1)}, bf16[1576,128]{0,1:T(8,128)(2,1)S(1)}, u32[]{:S(2)}) copy-start(bf16[1576,128]{0,1:T(8,128)(2,1)S(1)} %reshape.233) | copy-start | bytes 1210372
  77.5 72.7 %copy-start.39 = (f32[512]{0:T(512)S(1)}, f32[512]{0:T(512)}, u32[]{:S(2)}) copy-start(f32[512]{0:T(512)} %param.17) | copy-start | bytes 6148
  141.2 3.3 collective-permute-start
  143.1 15.2 %copy-start.37 = (pred[8,197]{1,0:T(8,128)(4,1)}, pred[8,197]{1,0:T(8,128)(4,1)S(1)}, u32[]{:S(2)}) copy-start(pred[8,197]{1,0:T(8,128)(4,1)S(1)} %broadcast_in_dim.92) | copy-start | bytes 4732
  150.1 6.3 copy-start.35
  160.6 366.2 %reduce-scatter.7.cloned.1.call-start = ((), (), s32[]{:S(2)}) async-start(), calls=%async_computation.7 | async-start | bytes 8069120 | tf_op jit(solution)/shard_map/reduce_scatter | solution.py:46
  375.2 36.2 %copy-start.44 = (bf16[1,512,512]{2,1,0:T(8,128)(2,1)S(1)}, bf16[1,512,512]{2,1,0:T(8,128)(2,1)}, u32[]{:S(2)}) copy-start(bf16[1,512,512]{2,1,0:T(8,128)(2,1)} %param.22) | copy-start | bytes 1572868
  408.8 2.7 copy-start.46
  416.9 117.8 %copy-start.27 = (s32[394,2]{0,1:T(2,128)S(1)}, s32[394,2]{0,1:T(2,128)}, u32[]{:S(2)}) copy-start(s32[394,2]{0,1:T(2,128)} %param.20) | copy-start | bytes 9460
  416.9 118.3 %copy-start.19 = (bf16[394,512]{1,0:T(8,128)(2,1)S(1)}, bf16[394,512]{1,0:T(8,128)(2,1)}, u32[]{:S(2)}) copy-start(bf16[394,512]{1,0:T(8,128)(2,1)} %param.23) | copy-start | bytes 1210372
  416.9 121.0 %copy-start.32 = (bf16[512,8]{0,1:T(8,128)(2,1)S(1)}, bf16[512,8]{0,1:T(8,128)(2,1)}, u32[]{:S(2)}) copy-start(bf16[512,8]{0,1:T(8,128)(2,1)} %param.18) | copy-start | bytes 24580
  416.9 121.0 %copy-start.42 = (f32[394,8]{0,1:T(8,128)S(1)}, f32[394,8]{0,1:T(8,128)}, u32[]{:S(2)}) copy-start(f32[394,8]{0,1:T(8,128)} %param.19) | copy-start | bytes 37828
  529.9 26.1 %all-to-all-start.1 = ((bf16[8,197,512]{2,1,0:T(8,128)(2,1)}), bf16[8,197,512]{2,1,0:T(8,128)(2,1)}, u32[]{:S(2)}, u32[]{:S(2)}) async-start(bf16[8,197,512]{2,1,0:T(8,128)(2,1)} %reshape.239), calls=%async_computation.2 | async-start | bytes 3276800 | tf_op jit(solution)/shard_map/all_to_all | solution.py:52
  534.2 166.4 %all-gather.9.cloned.1.call-start = ((), (), s32[]{:S(2)}) async-start(), calls=%async_computation.8 | async-start | bytes 8069120 | tf_op jit(solution)/shard_map/all_gather | solution.py:39
  561.3 2.5 copy-start.8
  563.8 9.4 copy-start.7
  573.5 7.9 copy-start.38
  583.7 347.1 %reduce-scatter.9.cloned.1.call-start = ((), (), s32[]{:S(2)}) async-start(), calls=%async_computation.9 | async-start | bytes 8069120 | tf_op jit(solution)/shard_map/reduce_scatter | solution.py:46
  790.8 6.7 copy-start.45
  820.9 203.2 %all-gather.13.cloned.1.call-start = ((), (), s32[]{:S(2)}) async-start(), calls=%async_computation.11 | async-start | bytes 2048000 | tf_op jit(solution)/shard_map/all_gather | solution.py:170
  934.0 32.2 %copy-start.9 = (bf16[788,512]{1,0:T(8,128)(2,1)S(1)}, bf16[788,512]{1,0:T(8,128)(2,1)}, u32[]{:S(2)}) copy-start(bf16[788,512]{1,0:T(8,128)(2,1)} %copy-done.8) | copy-start | bytes 2420740
  969.3 12.9 %copy-start.4 = (f32[394,512]{1,0:T(8,128)S(1)}, f32[394,512]{1,0:T(8,128)}, u32[]{:S(2)}) copy-start(f32[394,512]{1,0:T(8,128)} %copy-done.3) | copy-start | bytes 2420740
  969.3 12.9 %copy-start.31 = (f32[394]{0:T(512)S(1)}, f32[394]{0:T(512)}, u32[]{:S(2)}) copy-start(f32[394]{0:T(512)} %copy-done.30) | copy-start | bytes 4732
  969.3 12.9 %copy-start.36 = (f32[394]{0:T(512)S(1)}, f32[394]{0:T(512)}, u32[]{:S(2)}) copy-start(f32[394]{0:T(512)} %copy-done.35) | copy-start | bytes 4732
  969.3 12.9 %copy-start.40 = (f32[512]{0:T(512)S(1)}, f32[512]{0:T(512)}, u32[]{:S(2)}) copy-start(f32[512]{0:T(512)} %param.17) | copy-start | bytes 6148
  987.1 156.8 %all-reduce.9.cloned.1.call-start = ((), (), s32[]{:S(2)}) async-start(), calls=%async_computation.12 | async-start | bytes 1048576 | tf_op jit(solution)/shard_map/psum | solution.py:218
  996.9 29.0 %copy-start.22 = (bf16[128,512]{1,0:T(8,128)(2,1)S(1)}, bf16[128,512]{1,0:T(8,128)(2,1)}, u32[]{:S(2)}) copy-start(bf16[128,512]{1,0:T(8,128)(2,1)} %param.16) | copy-start | bytes 393220
  1006.2 24.9 %copy-start.24 = (f32[2,8,197]{2,1,0:T(8,128)S(1)}, f32[2,8,197]{2,1,0:T(8,128)}, u32[]{:S(2)}) copy-start(f32[2,8,197]{2,1,0:T(8,128)} %copy-done.23) | copy-start | bytes 37828
  1006.2 27.8 %copy-start.15 = (bf16[8,197,1,2,64]{1,4,3,0,2:T(8,128)(2,1)S(1)}, bf16[8,197,1,2,64]{1,4,3,0,2:T(8,128)(2,1)}, u32[]{:S(2)}) copy-start(bf16[8,197,1,2,64]{1,4,3,0,2:T(8,128)(2,1)} %copy-done.14) | copy-start | bytes 1210372
  1031.1 3.1 copy-start.2
  1034.2 3.0 copy-start.11
  1038.3 9.9 copy-start.26
  1044.7 43.1 %copy-start.17 = (bf16[1576,128]{0,1:T(8,128)(2,1)S(1)}, bf16[1576,128]{0,1:T(8,128)(2,1)}, u32[]{:S(2)}) copy-start(bf16[1576,128]{0,1:T(8,128)(2,1)} %copy-done.16) | copy-start | bytes 1210372
  1048.2 44.0 %copy-start.6 = (bf16[394,512]{1,0:T(8,128)(2,1)S(1)}, bf16[394,512]{1,0:T(8,128)(2,1)}, u32[]{:S(2)}) copy-start(bf16[394,512]{1,0:T(8,128)(2,1)} %param.13) | copy-start | bytes 1210372
  1048.2 44.0 %copy-start.29 = (f32[394]{0:T(512)S(1)}, f32[394]{0:T(512)}, u32[]{:S(2)}) copy-start(f32[394]{0:T(512)} %copy-done.28) | copy-start | bytes 4732
  1048.2 44.0 %copy-start.34 = (f32[394]{0:T(512)S(1)}, f32[394]{0:T(512)}, u32[]{:S(2)}) copy-start(f32[394]{0:T(512)} %copy-done.33) | copy-start | bytes 4732
  1048.2 44.0 %copy-start.41 = (f32[512]{0:T(512)S(1)}, f32[512]{0:T(512)}, u32[]{:S(2)}) copy-start(f32[512]{0:T(512)} %param.14) | copy-start | bytes 6148
  1086.2 4.7 collective-permute-start.1
  (9 other events, 10.1 us)
Sparse Core Ops, SparseCore 0:
  12.4 40.8 all-gather.10
  160.8 117.8 all-gather.6
  417.0 109.7 reduce-scatter.6
  583.9 116.7 all-gather.8
  821.0 109.8 reduce-scatter.8
  987.2 36.8 all-gather.12
  1091.0 52.8 all-reduce.8
where the time goes:
time: 1160 us; the launch traced here: 1150 us
  waiting for transfers between devices  529 us (46%)
  blocking collectives  316 us (27%)
  local copies, waits for them, and re-layouts  146 us (13%)
  matrix products  104 us (9%)
  other arithmetic  34.8 us (3%)
  between operations  16.2 us (1%)
    all_gather x2, waiting for transfers between devices, dispatch(): copies = lax.all_gather(buffer, 'tensor', axis=0, tiled=True)  235 us
    reduce_scatter x2, waiting for transfers between devices, collect(): lax.psum_scatter(term_fn(jnp.int32(0), row_count * lax.axis_size('tensor'...  220 us
    all_to_all x2, blocking collectives, dispatch(): lax.all_to_all(copies, 'expert', split_axis=1, concat_axis=1, tiled=True)  154 us
    unnamed x2, blocking collectives  95.8 us
    psum x1, blocking collectives, per_device(): lax.psum((grad_router, grad_norm1, grad_norm2), ('expert', 'tensor'))  39.8 us
    dot_general x1, matrix products, per_device(): pre_act = jnp.dot(routed, first_proj, preferred_element_type=jnp.float32)  33.6 us
    all_gather x1, waiting for transfers between devices, per_device(): lax.all_gather(normed1, 'tensor', axis=0, tiled=True)  29.9 us
    all_to_all x1, blocking collectives, collect(): lax.all_to_all(summed.reshape(layout), 'expert', split_axis=0, concat_axi...  26.3 us
  transfers between devices with their start and end apart: 10, of which 8 were waited for; matrix products, arithmetic and copies ran while one was open for 4% of the time, Pallas kernels for 0%

commit v1 on v0

v1 whole, which is shorter than its diff:
```python
import functools

import jax
import jax.numpy as jnp
from jax import lax
from jax.experimental import pallas as pl
from jax.experimental.pallas import tpu as pltpu
from jax.sharding import PartitionSpec as P

D = 512
HD = 64
TOP = 2
SEQ = 197
LANES = 128
TILE = 16
CHUNK = 256
EPSILON = 1e-06
BF = jnp.bfloat16
F32 = jnp.float32
VMEM_BYTES = 56 * 1024 * 1024

NN = (((1,), (0,)), ((), ()))
NT = (((1,), (1,)), ((), ()))
TN = (((0,), (0,)), ((), ()))


def up(value, unit):
    return (value + unit - 1) // unit * unit


SP = up(SEQ, TILE)


def mm(a, b, dims=NN):
    return lax.dot_general(a, b, dims, preferred_element_type=F32)


def call(body, out_shape, scratch=(), flops=0, moved=0, prefetch=None, **more):
    params = pltpu.CompilerParams(vmem_limit_bytes=VMEM_BYTES, **more)
    vmem = pl.BlockSpec(memory_space=pltpu.VMEM)
    cost = pl.CostEstimate(flops=flops, bytes_accessed=moved, transcendentals=0)

    def run(*args):
        specs = [vmem] * len(args)
        for place in prefetch or ():
            specs[place] = pl.BlockSpec(memory_space=pltpu.SMEM)
        return pl.pallas_call(
            body,
            out_shape=out_shape,
            in_specs=specs,
            out_specs=jax.tree.map(lambda _: vmem, out_shape),
            scratch_shapes=list(scratch),
            compiler_params=params,
            cost_estimate=cost,
        )(*args)

    return run


def shape(dims, dtype=BF):
    return jax.ShapeDtypeStruct(dims, dtype)


def unit_norm(values):
    center = values - jnp.mean(values, -1, keepdims=True)
    spread = jnp.mean(center * center, -1, keepdims=True)
    inverse = lax.rsqrt(spread + EPSILON)
    return center * inverse, inverse


def norm_back(grad_rows, normed, inverse, gain):
    scaled = grad_rows * gain
    inner = (
        scaled
        - jnp.mean(scaled, -1, keepdims=True)
        - normed * jnp.mean(scaled * normed, -1, keepdims=True)
    )
    return inverse * inner, jnp.sum(grad_rows * normed, axis=0, keepdims=True)


def ids(shape_of, dim):
    return lax.broadcasted_iota(jnp.int32, shape_of, dim)


def slots_by_lane(routes_t, experts):
    rows = routes_t.shape[1]
    which = ids((experts, rows), 0)
    named = (routes_t[0:1] == which) | (routes_t[1:2] == which)
    before = (ids((rows, rows), 0) < ids((rows, rows), 1)).astype(F32).astype(BF)
    rank = mm(named.astype(F32).astype(BF), before)
    return jnp.where(named, rank, -1.0)


def slots_by_row(routes, experts):
    rows = routes.shape[0]
    which = ids((rows, experts), 1)
    named = (routes[:, 0:1] == which) | (routes[:, 1:2] == which)
    before = (ids((rows, rows), 1) < ids((rows, rows), 0)).astype(F32).astype(BF)
    rank = mm(before, named.astype(F32).astype(BF))
    return jnp.where(named, rank, -1.0)


def send_rows(slots, rows, out_ref, experts):
    count = out_ref.shape[1]
    place = ids((count, rows.shape[0]), 0).astype(F32)
    for e in range(experts):
        pick = (place == slots[e : e + 1, :]).astype(F32).astype(BF)
        out_ref[e] = mm(pick, rows).astype(BF)


def take_rows(slots, in_ref, experts):
    count = in_ref.shape[1]
    rows = slots.shape[0]
    place = ids((rows, count), 1).astype(F32)
    total = None
    for e in range(experts):
        pick = (place == slots[:, e : e + 1]).astype(F32).astype(BF)
        part = mm(pick, in_ref[e])
        total = part if total is None else total + part
    return total


def early_kernel(experts, routes_t_ref, cot_ref, noise_ref, out_ref):
    lane = ids(noise_ref.shape, 1)
    noise = noise_ref[...]
    high = noise.astype(BF)
    rest = noise - high.astype(F32)
    middle = rest.astype(BF)
    low = (rest - middle.astype(F32)).astype(BF)
    parts = jnp.where(
        lane < experts,
        high.astype(F32),
        jnp.where(
            lane < 2 * experts,
            middle.astype(F32),
            jnp.where(lane < 3 * experts, low.astype(F32), noise),
        ),
    ).astype(BF)
    slots = slots_by_lane(routes_t_ref[...], experts)
    send_rows(slots, jnp.concatenate([cot_ref[...], parts], axis=1), out_ref, experts)


def attend_kernel(
    experts, images, routes_t_ref, x_ref, gain1_ref, w_qkv_ref, w_out_ref, gain2_ref,
    qkv_ref, attend_ref, mixed_ref, residual_ref, send_ref,
):
    groups, _, wide = w_qkv_ref.shape
    width = wide // 3
    heads = width // HD
    x = x_ref[...].astype(F32)
    unit1, _ = unit_norm(x)
    normed1 = (unit1 * gain1_ref[...]).astype(BF)
    lane = ids((SP, width), 1) // HD
    live = ids((SP, SP), 1) < SEQ
    for t in range(groups):
        qkv_ref[t] = mm(normed1, w_qkv_ref[t]).astype(BF)
        for i in range(images):
            rows = slice(i * SP, (i + 1) * SP)
            q = qkv_ref[t, rows, 0:width]
            k = qkv_ref[t, rows, width : 2 * width]
            v = qkv_ref[t, rows, 2 * width : 3 * width]
            mixed = None
            for j in range(heads):
                q_j = q if heads == 1 else jnp.where(lane == j, q, jnp.zeros_like(q))
                scores = mm(q_j, k, NT) * HD ** (-0.5)
                scores = jnp.where(live, scores, -1e30)
                power = jnp.exp(scores - jnp.max(scores, -1, keepdims=True))
                attend = (power / jnp.sum(power, -1, keepdims=True)).astype(BF)
                attend_ref[i, t * heads + j] = attend
                part = mm(attend, v)
                mixed = part if mixed is None else jnp.where(lane == j, part, mixed)
            mixed_ref[rows, t * width : (t + 1) * width] = mixed.astype(BF)
    residual = x + mm(mixed_ref[...], w_out_ref[...])
    residual_ref[...] = residual
    unit2, _ = unit_norm(residual)
    normed2 = (unit2 * gain2_ref[...]).astype(BF)
    send_rows(slots_by_lane(routes_t_ref[...], experts), normed2, send_ref, experts)


def gelu_parts(pre):
    density = jnp.exp(pre * pre * -0.5)
    size = jnp.abs(pre) * (0.5**0.5)
    t = 1.0 / (1.0 + 0.3275911 * size)
    series = t * (
        0.254829592
        + t * (-0.284496736 + t * (1.421413741 + t * (-1.453152027 + t * 1.061405429)))
    )
    tail = 0.5 * series * density
    return jnp.where(pre < 0, tail, 1.0 - tail), density * 0.3989422804014327


def expert_kernel(
    experts, own_ref, count_ref, x_in, early_in, w_router_ref, w_in_ref, w_back_ref,
    out_ref, back_ref, grads_ref, router_grad_ref,
    xs, es, dexp, hidden, dpre, outs, backs, total,
):
    sources, slots, _ = x_in.shape
    parts = w_in_ref.shape[0]
    width = w_in_ref.shape[2]
    own = own_ref[0]

    base = jnp.int32(0)
    for s in range(sources):
        tiles = (count_ref[s] + TILE - 1) // TILE

        def copy_in(j, _, s=s, base=base):
            to = pl.ds(pl.multiple_of((base + j) * TILE, TILE), TILE)
            at = pl.ds(pl.multiple_of(j * TILE, TILE), TILE)
            xs[to, :] = x_in[s, at, :]
            es[to, :] = early_in[s, at, :]
            return 0

        lax.fori_loop(0, tiles, copy_in, 0)
        base = base + tiles
    per = CHUNK // TILE
    chunks = (base + per - 1) // per

    def clear(j, _):
        to = pl.ds(pl.multiple_of(j * TILE, TILE), TILE)
        xs[to, :] = jnp.zeros((TILE, xs.shape[1]), BF)
        es[to, :] = jnp.zeros((TILE, es.shape[1]), BF)
        return 0

    lax.fori_loop(base, chunks * per, clear, 0)

    lane = ids((CHUNK, LANES), 1)
    fold_from, fold_to = ids((LANES, LANES), 0), ids((LANES, LANES), 1)
    fold = (
        (fold_from < 3 * experts) & (lax.rem(fold_from, experts) == fold_to)
    ).astype(F32).astype(BF)
    router_grad_ref[...] = jnp.zeros_like(router_grad_ref)

    def rows_of(c):
        return pl.ds(pl.multiple_of(c * CHUNK, CHUNK), CHUNK)

    def forward(c, _):
        rows = rows_of(c)
        x = xs[rows, :]
        cot = es[rows, 0:D].astype(F32)
        logits = mm(x, w_router_ref[...]) + mm(es[rows, D : D + LANES], fold)
        logits = jnp.where(lane < experts, logits, -1e30)
        power = jnp.exp(logits - jnp.max(logits, -1, keepdims=True))
        router = power / jnp.sum(power, -1, keepdims=True)
        mine = lane == own
        gate = jnp.sum(jnp.where(mine, router, 0.0), -1, keepdims=True)
        d_exp = (gate * cot).astype(BF)
        dexp[rows, :] = d_exp
        out = jnp.zeros((CHUNK, D), F32)
        back = jnp.zeros((CHUNK, D), F32)
        for f in range(parts):
            pre = mm(x, w_in_ref[f])
            normal, density = gelu_parts(pre)
            low = (pre * normal).astype(BF)
            hidden[f, rows, :] = low
            w_b = w_back_ref[f]
            out = out + mm(low, w_b)
            d_pre = (mm(d_exp, w_b, NT) * (normal + pre * density)).astype(BF)
            dpre[f, rows, :] = d_pre
            back = back + mm(d_pre, w_in_ref[f], NT)
        out = out.astype(BF).astype(F32)
        outs[rows, :] = (gate * out).astype(BF)
        d_gate = jnp.sum(cot * out, -1, keepdims=True)
        d_logits = (d_gate * gate * (mine.astype(F32) - router)).astype(BF)
        backs[rows, :] = (back + mm(d_logits, w_router_ref[...], NT)).astype(BF)
        router_grad_ref[...] += mm(x, d_logits, TN)
        return 0

    lax.fori_loop(0, chunks, forward, 0)

    def grads(f, _):
        def add_in(c, _):
            total[0] += mm(xs[rows_of(c), :], dpre[f, rows_of(c), :], TN)
            total[1] += mm(dexp[rows_of(c), :], hidden[f, rows_of(c), :], TN)
            return 0

        total[...] = jnp.zeros_like(total)
        lax.fori_loop(0, chunks, add_in, 0)
        grads_ref[f] = total[...].astype(BF)
        return 0

    lax.fori_loop(0, parts, grads, 0)

    base = jnp.int32(0)
    for s in range(sources):
        tiles = (count_ref[s] + TILE - 1) // TILE

        def copy_out(j, _, s=s, base=base):
            at = pl.ds(pl.multiple_of((base + j) * TILE, TILE), TILE)
            to = pl.ds(pl.multiple_of(j * TILE, TILE), TILE)
            out_ref[s, to, :] = outs[at, :]
            back_ref[s, to, :] = backs[at, :]
            return 0

        def clear_out(j, _, s=s):
            to = pl.ds(pl.multiple_of(j * TILE, TILE), TILE)
            out_ref[s, to, :] = jnp.zeros((TILE, D), BF)
            back_ref[s, to, :] = jnp.zeros((TILE, D), BF)
            return 0

        lax.fori_loop(0, tiles, copy_out, 0)
        lax.fori_loop(tiles, slots // TILE, clear_out, 0)
        base = base + tiles


def backward_kernel(
    experts, images, routes_ref, back_ref, residual_ref, cot_ref, x_ref, gain1_ref, gain2_ref,
    w_qkv_ref, w_out_ref, qkv_ref, attend_ref, mixed_ref,
    tokens_grad_ref, qkv_grad_ref, out_grad_ref, norm1_ref, norm2_ref, d_mixed_ref, d_qkv_ref,
):
    groups, _, wide = w_qkv_ref.shape
    width = wide // 3
    heads = width // HD
    slots = slots_by_row(routes_ref[...], experts)
    d_normed2 = take_rows(slots, back_ref, experts)
    unit2, inverse2 = unit_norm(residual_ref[...])
    d_rows, norm2 = norm_back(d_normed2, unit2, inverse2, gain2_ref[...])
    norm2_ref[...] = norm2
    d_residual = cot_ref[...].astype(F32) + d_rows
    tokens_grad_ref[...] = d_residual
    d_attention = d_residual.astype(BF)
    out_grad = mm(mixed_ref[...], d_attention, TN).astype(BF)
    for t in range(groups):
        out_grad_ref[t] = out_grad[t * width : (t + 1) * width]
    d_mixed = mm(d_attention, w_out_ref[...], NT).astype(BF)
    for t in range(groups):
        d_mixed_ref[t] = d_mixed[:, t * width : (t + 1) * width]
    x = x_ref[...].astype(F32)
    unit1, inverse1 = unit_norm(x)
    normed1 = (unit1 * gain1_ref[...]).astype(BF)
    lane = ids((SP, width), 1) // HD
    scaling = HD ** (-0.5)
    d_normed1 = None
    for t in range(groups):
        for i in range(images):
            rows = slice(i * SP, (i + 1) * SP)
            q = qkv_ref[t, rows, 0:width]
            k = qkv_ref[t, rows, width : 2 * width]
            v = qkv_ref[t, rows, 2 * width : 3 * width]
            do = d_mixed_ref[t, rows, :]
            dq = dk = dv = None
            for j in range(heads):
                own = lane == j
                do_j = do if heads == 1 else jnp.where(own, do, jnp.zeros_like(do))
                q_j = q if heads == 1 else jnp.where(own, q, jnp.zeros_like(q))
                attend_low = attend_ref[i, t * heads + j]
                attend = attend_low.astype(F32)
                part_v = mm(attend_low, do_j, TN)
                d_attend = mm(do_j, v, NT)
                inner = jnp.sum(attend * d_attend, -1, keepdims=True)
                ds = (attend * (d_attend - inner)).astype(BF)
                part_q = mm(ds, k) * scaling
                part_k = mm(ds, q_j, TN) * scaling
                dq = part_q if dq is None else jnp.where(own, part_q, dq)
                dk = part_k if dk is None else dk + part_k
                dv = part_v if dv is None else dv + part_v
            d_qkv_ref[t, rows, 0:width] = dq.astype(BF)
            d_qkv_ref[t, rows, width : 2 * width] = dk.astype(BF)
            d_qkv_ref[t, rows, 2 * width : 3 * width] = dv.astype(BF)
        d_t = d_qkv_ref[t]
        qkv_grad_ref[t] = mm(normed1, d_t, TN).astype(BF)
        part = mm(d_t, w_qkv_ref[t], NT)
        d_normed1 = part if d_normed1 is None else d_normed1 + part
    d_rows, norm1 = norm_back(d_normed1, unit1, inverse1, gain1_ref[...])
    norm1_ref[...] = norm1
    tokens_grad_ref[...] += d_rows


def output_kernel(experts, routes_ref, out_in, residual_ref, output_ref):
    slots = slots_by_row(routes_ref[...], experts)
    output_ref[...] = (residual_ref[...] + take_rows(slots, out_in, experts)).astype(BF)


def per_device(
    tokens, norm1_gain, w_qkv, w_out, norm2_gain, w_router, noise, routes, w_in, w_back, cotangent
):
    own_rows = tokens.shape[0]
    experts = noise.shape[1]
    tensor = lax.axis_size("tensor")
    images = own_rows // SEQ
    rows = images * SP
    capacity = (2 * own_rows * TOP + experts - 1) // experts
    slots = up(capacity, TILE)
    width = w_out.shape[0]
    hidden = w_in.shape[2]

    def padded(a, fill=0):
        a = a.reshape(images, SEQ, a.shape[1])
        a = jnp.pad(a, ((0, 0), (0, SP - SEQ), (0, 0)), constant_values=fill)
        return a.reshape(rows, a.shape[2])

    def own(a):
        return a.reshape(images, SP, a.shape[1])[:, :SEQ].reshape(own_rows, a.shape[1])

    w_qkv_all = lax.all_gather(w_qkv.reshape(D, 3 * width), "tensor", axis=0)
    w_out_all = lax.all_gather(w_out, "tensor", axis=0, tiled=True)
    w_in_all = lax.all_gather(w_in[0], "tensor", axis=0)
    w_back_all = lax.all_gather(w_back[0], "tensor", axis=0)

    x = padded(tokens)
    cot = padded(cotangent)
    routes_p = padded(routes, -1)
    routes_t = routes_p.T
    spread = jnp.concatenate(
        [noise] * 3
        + [jnp.ones((own_rows, 1), F32), jnp.zeros((own_rows, LANES - 3 * experts - 1), F32)],
        axis=1,
    )
    early = call(
        functools.partial(early_kernel, experts), shape((experts, slots, D + LANES))
    )(routes_t, cot, padded(spread))
    early = lax.all_to_all(early, "expert", split_axis=0, concat_axis=0, tiled=True)
    counts = jnp.sum(early[:, :, D + 3 * experts].astype(F32), axis=1).astype(jnp.int32)

    gain1, gain2 = norm1_gain.reshape(1, D), norm2_gain.reshape(1, D)
    heads = tensor * width // HD
    qkv, attend, mixed, residual, send = call(
        functools.partial(attend_kernel, experts, images),
        (
            shape((tensor, rows, 3 * width)),
            shape((images, heads, SP, SP)),
            shape((rows, D)),
            shape((rows, D), F32),
            shape((experts, slots, D)),
        ),
        flops=2 * rows * D * D * 4,
        moved=10_000_000,
    )(routes_t, x, gain1, w_qkv_all, w_out_all, gain2)
    routed = lax.all_to_all(send, "expert", split_axis=0, concat_axis=0, tiled=True)

    w_router_wide = jnp.pad(w_router, ((0, 0), (0, LANES - experts)))
    most = up(experts * slots, CHUNK)
    own_expert = lax.axis_index("expert").astype(jnp.int32).reshape(1)
    outs, backs, grads, router_grad = call(
        functools.partial(expert_kernel, experts),
        (
            shape((experts, slots, D)),
            shape((experts, slots, D)),
            shape((tensor, 2, D, hidden)),
            shape((D, LANES), F32),
        ),
        scratch=(
            pltpu.VMEM((most, D), BF),
            pltpu.VMEM((most, D + LANES), BF),
            pltpu.VMEM((most, D), BF),
            pltpu.VMEM((tensor, most, hidden), BF),
            pltpu.VMEM((tensor, most, hidden), BF),
            pltpu.VMEM((most, D), BF),
            pltpu.VMEM((most, D), BF),
            pltpu.VMEM((2, D, hidden), F32),
        ),
        flops=12 * experts * slots * D * tensor * hidden,
        moved=20_000_000,
        prefetch=(0, 1),
    )(own_expert, counts, routed, early, w_router_wide, w_in_all, w_back_all)

    returned = lax.all_to_all(backs, "expert", split_axis=0, concat_axis=0, tiled=True)
    returned_out = lax.all_to_all(outs, "expert", split_axis=0, concat_axis=0, tiled=True)
    grads = lax.psum_scatter(grads, "tensor", scatter_dimension=0, tiled=True)[0]

    grad_tokens, qkv_grad, out_grad, norm1, norm2 = call(
        functools.partial(backward_kernel, experts, images),
        (
            shape((rows, D), F32),
            shape((tensor, D, 3 * width)),
            shape((tensor, width, D)),
            shape((1, D), F32),
            shape((1, D), F32),
        ),
        scratch=(
            pltpu.VMEM((tensor, rows, width), BF),
            pltpu.VMEM((tensor, rows, 3 * width), BF),
        ),
        flops=2 * rows * D * D * 10,
        moved=10_000_000,
    )(
        routes_p, returned, residual, cot, x, gain1, gain2,
        w_qkv_all, w_out_all, qkv, attend, mixed,
    )
    output = call(functools.partial(output_kernel, experts), shape((rows, D)))(
        routes_p, returned_out, residual
    )
    both = jnp.concatenate(
        [qkv_grad.reshape(tensor, 3 * width, D), out_grad.reshape(tensor, width, D)], axis=1
    )
    both = lax.psum_scatter(both, "tensor", scatter_dimension=0, tiled=True)[0]
    both = lax.psum(both, "expert").astype(F32)
    router_grad, norm1, norm2 = lax.psum(
        (router_grad[:, :experts], norm1, norm2), ("expert", "tensor")
    )
    return (
        own(output),
        own(grad_tokens),
        norm1.reshape(D),
        both[: 3 * width].reshape(D, 3, width),
        both[3 * width :],
        norm2.reshape(D),
        router_grad,
        grads[0].astype(F32)[None],
        grads[1].T.astype(F32)[None],
    )


def solution(mesh):
    rows = P(("expert", "tensor"), None)
    placed = (
        rows,
        P(),
        P(None, None, "tensor"),
        P("tensor", None),
        P(),
        P(),
        rows,
        rows,
        P("expert", None, "tensor"),
        P("expert", "tensor", None),
        rows,
    )
    return jax.shard_map(
        per_device,
        mesh=mesh,
        in_specs=placed,
        out_specs=(
            rows,
            rows,
            P(),
            P(None, None, "tensor"),
            P("tensor", None),
            P(),
            P(),
            P("expert", None, "tensor"),
            P("expert", "tensor", None),
        ),
        check_vma=False,
    )
```

time: 1160 us -> 433 us (0.37)
  waiting for transfers between devices: 529 us -> 189 us
  blocking collectives: 316 us -> 122 us
  local copies, waits for them, and re-layouts: 146 us -> 18.8 us
  matrix products: 104 us -> 0 us
  Pallas kernels: 0 us -> 73.2 us
  other arithmetic: 34.8 us -> 4.75 us
    all_gather x4 -> x3, waiting for transfers between devices: 283 us -> 90 us  [the longest x1 46.3 us: per_device(): w_back_all = lax.all_gather(w_back[0], 'tensor', axis=0)]
    all_to_all x3 -> x2, blocking collectives: 181 us -> 55.4 us  [the longest x1 28.7 us: per_device(): lax.all_to_all(outs, 'expert', split_axis=0, concat_axis=0, tiled=True)]
    reduce_scatter x2, waiting for transfers between devices: 220 us -> 97.1 us  [the longest x1 53 us: per_device(): lax.psum_scatter(grads, 'tensor', scatter_dimension=0, tiled=True)[0]]
    dot_general x21 -> x0, matrix products: 104 us -> none  [the longest x1 33.6 us: per_device(): pre_act = jnp.dot(routed, first_proj, preferred_element_type=jnp.float32)]
    unnamed x2 -> x0, blocking collectives: 95.8 us -> none
    pallas_call x0 -> x5, Pallas kernels: none -> 73.2 us  [run(): pl.pallas_call(body, out_shape=out_shape, in_specs=specs, out_specs=jax.t...]
    reshape x16 -> x9, local copies, waits for them, and re-layouts: 61.9 us -> 5.56 us  [the longest x1 2.99 us: per_device(): qkv_grad.reshape(tensor, 3 * width, D)]
    gather x11 -> x0, local copies, waits for them, and re-layouts: 31.9 us -> none  [the longest x5 8.68 us: per_device(): gate_vals = jnp.take_along_axis(router, routes, axis=1)]
  transfers between devices with their start and end apart: 10 -> 8, of which waited for: 8 -> 5; matrix products, arithmetic and copies ran while one was open for 4% -> 3% of each run, Pallas kernels for 0% -> 4%
where the time goes in v1:
time: 433 us; the launch traced here: 432 us
  waiting for transfers between devices  189 us (44%)
  blocking collectives  122 us (28%)
  Pallas kernels  73.2 us (17%)
  local copies, waits for them, and re-layouts  18.8 us (4%)
  between operations  14.4 us (3%)
  starting transfers between devices  9.86 us (2%)
  other arithmetic  4.75 us (1%)
    pallas_call x5, Pallas kernels, run(): pl.pallas_call(body, out_shape=out_shape, in_specs=specs, out_specs=jax.t...  73.2 us
    reduce_scatter x1, waiting for transfers between devices, per_device(): lax.psum_scatter(grads, 'tensor', scatter_dimension=0, tiled=True)[0]  53 us
    all_gather x1, waiting for transfers between devices, per_device(): w_back_all = lax.all_gather(w_back[0], 'tensor', axis=0)  46.3 us
    reduce_scatter x1, waiting for transfers between devices, per_device(): both = lax.psum_scatter(both, 'tensor', scatter_dimension=0, tiled=True)[0]  44.1 us
    psum x1, blocking collectives, per_device(): lax.psum((router_grad[:, :experts], norm1, norm2), ('expert', 'tensor'))  43.5 us
    all_gather x1, waiting for transfers between devices, per_device(): w_in_all = lax.all_gather(w_in[0], 'tensor', axis=0)  32.8 us
    all_to_all x1, blocking collectives, per_device(): lax.all_to_all(outs, 'expert', split_axis=0, concat_axis=0, tiled=True)  28.7 us
    all_to_all x1, blocking collectives, per_device(): lax.all_to_all(backs, 'expert', split_axis=0, concat_axis=0, tiled=True)  26.7 us
  transfers between devices with their start and end apart: 8, of which 5 were waited for; matrix products, arithmetic and copies ran while one was open for 3% of the time, Pallas kernels for 4%

profile of v1, /device:TPU:0, one launch (start us, length us, event | category | flops | bytes accessed | tf_op | source)
XLA Modules:
  0.0 432.3 jit_solution(2660995881329665648)
XLA Ops:
  7.2 1.2 copy.47
  8.4 0.9 copy.48
  9.4 0.7 all-gather.6.cloned.1.call-update
  10.1 0.1 reshape.94
  10.2 0.1 copy.42
  10.4 0.7 copy.46.routes_t_ref
  11.1 0.1 copy.43
  11.3 0.3 concatenate.6
  11.6 0.7 pad.21
  12.3 0.1 reshape.97
  12.4 0.8 pad.20
  13.2 4.1 shard_map.178
  17.3 5.3 %all-to-all-start = ((bf16[8,208,640]{2,1,0:T(8,128)(2,1)}), bf16[8,208,640]{2,1,0:T(8,128)(2,1)S(1)}, u32[]{:S(2)}, u32[]{:S(2)}) async-start(bf16[8,208,640]{2,1,0:T(8,128)(2,1)} %shard_map.178), calls=%async_computation | async-start | bytes 4259840 | tf_op jit(solution)/shard_map/all_to_all | solution.py:411
  22.6 0.7 all-gather.8.cloned.1.call-update
  23.3 0.1 reshape.101
  23.4 0.8 pad.22
  24.2 23.3 %all_gather.13.w_out_ref = bf16[512,512]{1,0:T(8,128)(2,1)} all-gather(bf16[128,512]{1,0:T(8,128)(2,1)S(1)} %copy-done.9), channel_id=1, replica_groups=mesh['expert'=8,'tensor'=4] {'tensor'}, dimensions={0}, use_global_device_ids=true | all-gather | bytes 655360 | tf_op jit(solution)/shard_map/all_gather | solution.py:395
  47.5 10.9 %all-gather.4.cloned.1.call-done.w_qkv_ref = bf16[4,512,384]{2,1,0:T(8,128)(2,1)} async-done(((bf16[1,512,384]{2,1,0:T(8,128)(2,1)}), bf16[4,512,384]{2,1,0:T(8,128)(2,1)}) %all-gather.4.cloned.1.call-update) | async-done | bytes 1572880 | tf_op jit(solution)/shard_map/all_gather | solution.py:394
  58.4 7.5 %shard_map.179 = (bf16[4,416,384]{2,1,0:T(8,128)(2,1)}, bf16[2,8,208,208]{3,2,1,0:T(8,128)(2,1)}, bf16[416,512]{1,0:T(8,128)(2,1)}, f32[416,512]{1,0:T(8,128)}, bf16[8,208,512]{2,1,0:T(8,128)(2,1)}) custom-call(s32[2,416]{1,0:T(2,128)} %copy.46.routes_t_ref, bf16[416,512]{1,0:T(8,128)(2,1)} %bitcast.37, f32[1,512]{1,0:T(1,128)} %bitcast.47, ...), custom_call_target="tpu_custom_call" | custom-call | flops 872415232 | bytes 10000000 | tf_op jit(solution)/shard_map/pallas_call | solution.py:47
  66.0 4.3 %all-to-all-start.1 = ((bf16[8,208,512]{2,1,0:T(8,128)(2,1)}), bf16[8,208,512]{2,1,0:T(8,128)(2,1)}, u32[]{:S(2)}, u32[]{:S(2)}) async-start(bf16[8,208,512]{2,1,0:T(8,128)(2,1)} %get-tuple-element.23), calls=%async_computation.1 | async-start | bytes 3407872 | tf_op jit(solution)/shard_map/all_to_all | solution.py:428
  70.4 0.2 copy.50
  70.5 0.7 pad.23.w_router_ref
  71.2 0.3 convert_reduce_fusion
  71.5 0.5 convert_element_type.38.count_ref
  72.0 32.8 %all-gather.6.cloned.1.call-done.w_in_ref = bf16[4,512,512]{2,1,0:T(8,128)(2,1)} async-done(((bf16[1,512,512]{2,1,0:T(8,128)(2,1)}), bf16[4,512,512]{2,1,0:T(8,128)(2,1)}) %all-gather.6.cloned.1.call-update) | async-done | bytes 2097168 | tf_op jit(solution)/shard_map/all_gather | solution.py:396
  104.8 46.3 %all-gather.8.cloned.1.call-done.w_back_ref = bf16[4,512,512]{2,1,0:T(8,128)(2,1)} async-done(((bf16[1,512,512]{2,1,0:T(8,128)(2,1)}), bf16[4,512,512]{2,1,0:T(8,128)(2,1)}) %all-gather.8.cloned.1.call-update) | async-done | bytes 2097168 | tf_op jit(solution)/shard_map/all_gather | solution.py:397
  151.1 40.4 %shard_map.180 = (bf16[8,208,512]{2,1,0:T(8,128)(2,1)}, bf16[8,208,512]{2,1,0:T(8,128)(2,1)}, bf16[4,2,512,512]{3,2,1,0:T(8,128)(2,1)}, f32[512,128]{1,0:T(8,128)}) custom-call(s32[1]{0:T(128)} %bitcast.1.own_ref, s32[8]{0:T(128)} %convert_element_type.38.count_ref, bf16[8,208,512]{2,1,0:T(8,128)(2,1)} %all-to-all-done.1.x_in, ...), custom_call_target="tpu_custom_call" | custom-call | flops 20937965568 | bytes 20000000 | tf_op jit(solution)/shard_map/pallas_call | solution.py:47
  191.5 26.7 %all_to_all.20.back_ref = bf16[8,208,512]{2,1,0:T(8,128)(2,1)} all-to-all(bf16[8,208,512]{2,1,0:T(8,128)(2,1)} %get-tuple-element.26), channel_id=1, replica_groups=mesh['expert'=8,'tensor'=4] {'expert'}, dimensions={0} | all-to-all | bytes 3407872 | tf_op jit(solution)/shard_map/all_to_all | solution.py:456
  218.2 17.0 %shard_map.182 = (f32[416,512]{1,0:T(8,128)}, bf16[4,512,384]{2,1,0:T(8,128)(2,1)}, bf16[4,128,512]{2,1,0:T(8,128)(2,1)}, f32[1,512]{1,0:T(1,128)}, f32[1,512]{1,0:T(1,128)}) custom-call(s32[416,2]{1,0:T(8,128)} %bitcast.35, bf16[8,208,512]{2,1,0:T(8,128)(2,1)} %all_to_all.20.back_ref, f32[416,512]{1,0:T(8,128)} %get-tuple-element.25.residual_ref, ...), custom_call_target="tpu_custom_call" | custom-call | flops 2181038080 | bytes 10000000 | tf_op jit(solution)/shard_map/pallas_call | solution.py:47
  235.3 3.0 reshape.110
  238.3 1.5 pad_maximum_fusion
  239.8 44.1 %reduce-scatter.3.cloned.1.call-done = bf16[1,512,512]{2,1,0:T(8,128)(2,1)} async-done(((bf16[4,512,512]{2,1,0:T(8,128)(2,1)}), bf16[1,512,512]{2,1,0:T(8,128)(2,1)}) %reduce-scatter.3.cloned.1.call-update) | async-done | bytes 524304 | tf_op jit(solution)/shard_map/reduce_scatter | solution.py:485
  284.0 0.5 reduce-scatter.5.cloned.1.call-update
  284.5 0.9 copy-done.3
  285.5 28.7 %all_to_all.21.out_in = bf16[8,208,512]{2,1,0:T(8,128)(2,1)} all-to-all(bf16[8,208,512]{2,1,0:T(8,128)(2,1)S(1)} %copy-done.3), channel_id=1, replica_groups=mesh['expert'=8,'tensor'=4] {'expert'}, dimensions={0} | all-to-all | bytes 3407872 | tf_op jit(solution)/shard_map/all_to_all | solution.py:457
  314.2 4.1 shard_map.181
  318.4 1.0 slice.35
  319.4 0.8 reshape.106
  320.3 1.0 reshape.108
  321.3 43.5 %all-reduce.5 = (f32[512]{0:T(512)}, f32[512]{0:T(512)}, f32[512,8]{1,0:T(8,128)S(1)}) all-reduce(f32[512]{0:T(512)S(1)} %bitcast.45, f32[512]{0:T(512)S(1)} %bitcast.46, f32[512,8]{1,0:T(8,128)S(1)} %bitcast.44), channel_id=1, replica_groups=mesh['expert'=8,'tensor'=4] {'expert','tensor'}, use_global_device_ids=true, to_apply=%region_1.2 | all-reduce | flops 5120 | bytes 40960 | tf_op jit(solution)/shard_map/psum | solution.py:487
  364.8 0.7 copy.52
  365.5 1.1 slice.37
  366.6 0.4 reshape.111
  367.0 0.9 copy.51
  367.9 0.7 slice.38
  368.7 53.0 %reduce-scatter.5.cloned.1.call-done = bf16[1,2,512,512]{3,2,1,0:T(8,128)(2,1)} async-done(((bf16[4,2,512,512]{3,2,1,0:T(8,128)(2,1)}), bf16[1,2,512,512]{3,2,1,0:T(8,128)(2,1)}) %reduce-scatter.5.cloned.1.call-update) | async-done | bytes 1048592 | tf_op jit(solution)/shard_map/reduce_scatter | solution.py:458
  421.7 2.5 convert_bitcast_fusion
  424.1 1.3 copy.53
  (46 shorter events, 0.5 us)
Async XLA Ops:
  7.2 3.0 copy-start.12
  7.2 3.9 copy-start.10
  7.2 51.2 %all-gather.4.cloned.1.call-start = ((), (), s32[]{:S(2)}) async-start(), calls=%async_computation.6 | async-start | bytes 1966080 | tf_op jit(solution)/shard_map/all_gather | solution.py:394
  9.4 3.0 copy-start.6
  9.4 95.4 %all-gather.6.cloned.1.call-start = ((), (), s32[]{:S(2)}) async-start(), calls=%async_computation.7 | async-start | bytes 2621440 | tf_op jit(solution)/shard_map/all_gather | solution.py:396
  10.4 2.8 copy-start
  17.3 6.0 %copy-start.7 = (bf16[394,512]{1,0:T(8,128)(2,1)S(1)}, bf16[394,512]{1,0:T(8,128)(2,1)}, u32[]{:S(2)}) copy-start(bf16[394,512]{1,0:T(8,128)(2,1)} %param.11) | copy-start | bytes 1210372
  17.3 48.7 %all-to-all-start = ((bf16[8,208,640]{2,1,0:T(8,128)(2,1)}), bf16[8,208,640]{2,1,0:T(8,128)(2,1)S(1)}, u32[]{:S(2)}, u32[]{:S(2)}) async-start(bf16[8,208,640]{2,1,0:T(8,128)(2,1)} %shard_map.178), calls=%async_computation | async-start | bytes 4259840 | tf_op jit(solution)/shard_map/all_to_all | solution.py:411
  22.6 1.6 copy-start.9
  22.6 128.5 %all-gather.8.cloned.1.call-start = ((), (), s32[]{:S(2)}) async-start(), calls=%async_computation.8 | async-start | bytes 2621440 | tf_op jit(solution)/shard_map/all_gather | solution.py:397
  65.9 4.4 %copy-start.11 = (bf16[512,8]{0,1:T(8,128)(2,1)S(1)}, bf16[512,8]{0,1:T(8,128)(2,1)}, u32[]{:S(2)}) copy-start(bf16[512,8]{0,1:T(8,128)(2,1)} %param.16) | copy-start | bytes 24580
  66.0 5.5 %copy-start.1 = (bf16[8,208,640]{2,1,0:T(8,128)(2,1)}, bf16[8,208,640]{2,1,0:T(8,128)(2,1)S(1)}, u32[]{:S(2)}) copy-start(bf16[8,208,640]{2,1,0:T(8,128)(2,1)S(1)} %all-to-all-done.early_in) | copy-start | bytes 6389764
  66.0 85.1 %all-to-all-start.1 = ((bf16[8,208,512]{2,1,0:T(8,128)(2,1)}), bf16[8,208,512]{2,1,0:T(8,128)(2,1)}, u32[]{:S(2)}, u32[]{:S(2)}) async-start(bf16[8,208,512]{2,1,0:T(8,128)(2,1)} %get-tuple-element.23), calls=%async_computation.1 | async-start | bytes 3407872 | tf_op jit(solution)/shard_map/all_to_all | solution.py:428
  70.3 213.6 %reduce-scatter.3.cloned.1.call-start = ((), (), s32[]{:S(2)}) async-start(), calls=%async_computation.9 | async-start | bytes 2621440 | tf_op jit(solution)/shard_map/reduce_scatter | solution.py:485
  235.3 3.0 copy-start.5
  239.8 125.7 %all-reduce.8.cloned.1.call-start = ((), (), s32[]{:S(2)}) async-start(), calls=%async_computation.10 | async-start | bytes 1048576 | tf_op jit(solution)/shard_map/psum | solution.py:486
  284.0 137.7 %reduce-scatter.5.cloned.1.call-start = ((), (), s32[]{:S(2)}) async-start(), calls=%async_computation.11 | async-start | bytes 5242880 | tf_op jit(solution)/shard_map/reduce_scatter | solution.py:458
  284.0 1.5 copy-start.3
  314.2 6.1 %copy-start.4 = (f32[416,512]{1,0:T(8,128)S(1)}, f32[416,512]{1,0:T(8,128)}, u32[]{:S(2)}) copy-start(f32[416,512]{1,0:T(8,128)} %get-tuple-element.30) | copy-start | bytes 2555908
  319.4 1.9 copy-start.8
  319.4 1.9 copy-start.13
  319.4 1.9 copy-start.14
  366.6 1.3 copy-start.2
Sparse Core Ops, SparseCore 0:
  10.2 48.2 all-gather.3
  60.0 44.7 all-gather.5
  106.4 44.6 all-gather.7
  239.9 43.9 reduce-scatter.2
  287.2 55.9 all-reduce.7
  345.3 76.3 reduce-scatter.4

commit v2 on v1

--- a/solution.py
+++ b/solution.py
@@ -35,20 +35,23 @@
     return lax.dot_general(a, b, dims, preferred_element_type=F32)
 
 
-def call(body, out_shape, scratch=(), flops=0, moved=0, prefetch=None, **more):
+def call(
+    body, out_shape, scratch=(), flops=0, moved=0, prefetch=(), far_in=(), far_out=(), **more
+):
     params = pltpu.CompilerParams(vmem_limit_bytes=VMEM_BYTES, **more)
-    vmem = pl.BlockSpec(memory_space=pltpu.VMEM)
     cost = pl.CostEstimate(flops=flops, bytes_accessed=moved, transcendentals=0)
 
+    def spec(place, far, scalar=()):
+        if place in scalar:
+            return pl.BlockSpec(memory_space=pltpu.SMEM)
+        return pl.BlockSpec(memory_space=pl.ANY if place in far else pltpu.VMEM)
+
     def run(*args):
-        specs = [vmem] * len(args)
-        for place in prefetch or ():
-            specs[place] = pl.BlockSpec(memory_space=pltpu.SMEM)
         return pl.pallas_call(
             body,
             out_shape=out_shape,
-            in_specs=specs,
-            out_specs=jax.tree.map(lambda _: vmem, out_shape),
+            in_specs=[spec(place, far_in, prefetch) for place in range(len(args))],
+            out_specs=tuple(spec(place, far_out) for place in range(len(out_shape))),
             scratch_shapes=list(scratch),
             compiler_params=params,
             cost_estimate=cost,
@@ -120,7 +123,137 @@
     return total
 
 
-def early_kernel(experts, routes_t_ref, cot_ref, noise_ref, out_ref):
+MESH = pl.DeviceIdType.MESH
+
+
+def greet(axes):
+    barrier = pltpu.get_barrier_semaphore()
+    for name, size in axes:
+        me = lax.axis_index(name)
+
+        def hello(d, _, name=name, size=size, me=me):
+            pl.semaphore_signal(
+                barrier, inc=1, device_id={name: lax.rem(me + d, size)}, device_id_type=MESH
+            )
+            return 0
+
+        lax.fori_loop(1, size, hello, 0)
+    pl.semaphore_wait(barrier, sum(size - 1 for _, size in axes))
+
+
+def remote(src, dst, send_sem, recv_sem, name, to):
+    return pltpu.make_async_remote_copy(
+        src_ref=src,
+        dst_ref=dst,
+        send_sem=send_sem,
+        recv_sem=recv_sem,
+        device_id={name: to},
+        device_id_type=MESH,
+    )
+
+
+def each(size, step):
+    def body(d, _):
+        step(d)
+        return 0
+
+    lax.fori_loop(1, size, body, 0)
+
+
+class Line:
+    def __init__(self, size, own, everyone, send_sem, recv_sem):
+        self.size, self.own, self.all = size, own, everyone
+        self.send_sem, self.recv_sem = send_sem, recv_sem
+        self.me = lax.axis_index("tensor")
+
+    def copy(self, way, step, arriving):
+        toward = 1 if way == 0 else -1
+        owner = self.me - toward * (step + (1 if arriving else 0))
+        src = self.own if step == 0 else self.all.at[owner]
+        return remote(
+            src, self.all.at[owner], self.send_sem.at[way, step], self.recv_sem.at[way, step],
+            "tensor", self.me + toward,
+        )
+
+    def sends(self, way, step):
+        last = self.size - 1
+        if way == 0:
+            return (self.me >= step) & (self.me < last)
+        return (self.me <= last - step) & (self.me > 0)
+
+    def receives(self, way, step):
+        if way == 0:
+            return self.me >= step + 1
+        return self.me <= self.size - 2 - step
+
+    def start(self, step):
+        for way in (0, 1):
+            pl.when(self.sends(way, step))(lambda way=way: self.copy(way, step, False).start())
+
+    def arrive(self, step):
+        for way in (0, 1):
+            pl.when(self.receives(way, step))(
+                lambda way=way: self.copy(way, step, True).wait_recv()
+            )
+
+    def finish(self):
+        for step in range(self.size - 1):
+            for way in (0, 1):
+                pl.when(self.sends(way, step))(
+                    lambda way=way, step=step: self.copy(way, step, False).wait_send()
+                )
+
+
+def forward_kernel(
+    experts, tensor, images, routes_t_ref, x_ref, cot_ref, noise_ref, gain1_ref, gain2_ref,
+    w_own_ref, w_in_own, w_back_own,
+    w_ref, qkv_ref, attend_ref, mixed_ref, residual_ref, routed_ref, early_ref, w_in_all, w_back_all,
+    slots_ref, send_ref, early_send, own_sem, piece_sems, plane_sems, early_sems, route_sems,
+    in_sems, back_sems,
+):
+    wide = w_own_ref.shape[1]
+    width = wide // 4
+    heads = width // HD
+    me_e, me_t = lax.axis_index("expert"), lax.axis_index("tensor")
+    piece = D // experts
+    mine = pl.ds(pl.multiple_of(me_e * piece, piece), piece)
+
+    def piece_copy(d, arriving):
+        owner = lax.rem(me_t + tensor - d, tensor) if arriving else me_t
+        return remote(
+            w_own_ref.at[mine], w_ref.at[owner, mine], piece_sems.at[0, d], piece_sems.at[1, d],
+            "tensor", lax.rem(me_t + d, tensor),
+        )
+
+    def plane_copy(z, d, arriving):
+        owner = lax.rem(me_t + tensor - z, tensor)
+        other = lax.rem(me_e + experts - d, experts) if arriving else me_e
+        rows = pl.ds(pl.multiple_of(other * piece, piece), piece)
+        block = w_ref.at[owner, rows]
+        return remote(
+            block, block, plane_sems.at[0, z, d], plane_sems.at[1, z, d],
+            "expert", lax.rem(me_e + d, experts),
+        )
+
+    def swap_copy(src, dst, sems, d, arriving):
+        to = lax.rem(me_e + d, experts)
+        place = lax.rem(me_e + experts - d, experts) if arriving else me_e
+        return remote(src.at[to], dst.at[place], sems.at[0, d], sems.at[1, d], "expert", to)
+
+    greet((("expert", experts), ("tensor", tensor)))
+    each(tensor, lambda d: piece_copy(d, False).start())
+    line_in = Line(tensor, w_in_own, w_in_all, in_sems.at[0], in_sems.at[1])
+    line_back = Line(tensor, w_back_own, w_back_all, back_sems.at[0], back_sems.at[1])
+    line_in.start(0)
+    line_back.start(0)
+    keep = [
+        pltpu.make_async_copy(w_own_ref, w_ref.at[me_t], own_sem.at[0]),
+        pltpu.make_async_copy(w_in_own, w_in_all.at[me_t], own_sem.at[1]),
+        pltpu.make_async_copy(w_back_own, w_back_all.at[me_t], own_sem.at[2]),
+    ]
+    for copy in keep:
+        copy.start()
+
     lane = ids(noise_ref.shape, 1)
     noise = noise_ref[...]
     high = noise.astype(BF)
@@ -136,24 +269,43 @@
             jnp.where(lane < 3 * experts, low.astype(F32), noise),
         ),
     ).astype(BF)
-    slots = slots_by_lane(routes_t_ref[...], experts)
-    send_rows(slots, jnp.concatenate([cot_ref[...], parts], axis=1), out_ref, experts)
-
-
-def attend_kernel(
-    experts, images, routes_t_ref, x_ref, gain1_ref, w_qkv_ref, w_out_ref, gain2_ref,
-    qkv_ref, attend_ref, mixed_ref, residual_ref, send_ref,
-):
-    groups, _, wide = w_qkv_ref.shape
-    width = wide // 3
-    heads = width // HD
+    slots_ref[...] = slots_by_lane(routes_t_ref[...], experts)
+    count = send_ref.shape[1]
+    place = ids((count, slots_ref.shape[1]), 0).astype(F32)
+
+    def pick_rows(rows, out_ref, dst, sems, own_copy):
+        for d in range(1, experts + 1):
+            e = lax.rem(me_e + d, experts)
+            pick = (place == slots_ref[pl.ds(e, 1), :]).astype(F32).astype(BF)
+            out_ref[e] = mm(pick, rows).astype(BF)
+            if d < experts:
+                swap_copy(out_ref, dst, sems, d, False).start()
+            else:
+                own_copy.start()
+
+    def forward_piece(z):
+        piece_copy(z, True).wait_recv()
+        each(experts, lambda d: plane_copy(z, d, False).start())
+
+    each(tensor, forward_piece)
+    own_early = pltpu.make_async_copy(early_send.at[me_e], early_ref.at[me_e], own_sem.at[3])
+    pick_rows(
+        jnp.concatenate([cot_ref[...], parts], axis=1), early_send, early_ref, early_sems, own_early
+    )
     x = x_ref[...].astype(F32)
     unit1, _ = unit_norm(x)
     normed1 = (unit1 * gain1_ref[...]).astype(BF)
+    line_in.arrive(0)
+    line_in.start(1)
+    line_back.arrive(0)
+    line_back.start(1)
+    keep[0].wait()
+    each(tensor, lambda z: each(experts, lambda d: plane_copy(z, d, True).wait_recv()))
+
     lane = ids((SP, width), 1) // HD
     live = ids((SP, SP), 1) < SEQ
-    for t in range(groups):
-        qkv_ref[t] = mm(normed1, w_qkv_ref[t]).astype(BF)
+    for t in range(tensor):
+        qkv_ref[t] = mm(normed1, w_ref[t, :, 0 : 3 * width]).astype(BF)
         for i in range(images):
             rows = slice(i * SP, (i + 1) * SP)
             q = qkv_ref[t, rows, 0:width]
@@ -169,12 +321,35 @@
                 attend_ref[i, t * heads + j] = attend
                 part = mm(attend, v)
                 mixed = part if mixed is None else jnp.where(lane == j, part, mixed)
-            mixed_ref[rows, t * width : (t + 1) * width] = mixed.astype(BF)
-    residual = x + mm(mixed_ref[...], w_out_ref[...])
+            mixed_ref[t, rows, :] = mixed.astype(BF)
+    residual = x
+    for t in range(tensor):
+        residual = residual + mm(mixed_ref[t], w_ref[t, :, 3 * width : wide], NT)
     residual_ref[...] = residual
     unit2, _ = unit_norm(residual)
     normed2 = (unit2 * gain2_ref[...]).astype(BF)
-    send_rows(slots_by_lane(routes_t_ref[...], experts), normed2, send_ref, experts)
+    own_route = pltpu.make_async_copy(send_ref.at[me_e], routed_ref.at[me_e], own_sem.at[4])
+    pick_rows(normed2, send_ref, routed_ref, route_sems, own_route)
+
+    for step in range(1, tensor - 1):
+        for line in (line_in, line_back):
+            line.arrive(step)
+            if step + 1 < tensor - 1:
+                line.start(step + 1)
+    each(tensor, lambda d: piece_copy(d, False).wait_send())
+    each(tensor, lambda z: each(experts, lambda d: plane_copy(z, d, False).wait_send()))
+
+    def swapped(d):
+        swap_copy(early_send, early_ref, early_sems, d, False).wait_send()
+        swap_copy(early_send, early_ref, early_sems, d, True).wait_recv()
+        swap_copy(send_ref, routed_ref, route_sems, d, False).wait_send()
+        swap_copy(send_ref, routed_ref, route_sems, d, True).wait_recv()
+
+    each(experts, swapped)
+    line_in.finish()
+    line_back.finish()
+    for copy in [keep[1], keep[2], own_early, own_route]:
+        copy.wait()
 
 
 def gelu_parts(pre):
@@ -304,11 +479,11 @@
 
 def backward_kernel(
     experts, images, routes_ref, back_ref, residual_ref, cot_ref, x_ref, gain1_ref, gain2_ref,
-    w_qkv_ref, w_out_ref, qkv_ref, attend_ref, mixed_ref,
-    tokens_grad_ref, qkv_grad_ref, out_grad_ref, norm1_ref, norm2_ref, d_mixed_ref, d_qkv_ref,
+    w_ref, qkv_ref, attend_ref, mixed_ref,
+    tokens_grad_ref, w_grad_ref, norm1_ref, norm2_ref, d_qkv_ref,
 ):
-    groups, _, wide = w_qkv_ref.shape
-    width = wide // 3
+    groups, _, wide = w_ref.shape
+    width = wide // 4
     heads = width // HD
     slots = slots_by_row(routes_ref[...], experts)
     d_normed2 = take_rows(slots, back_ref, experts)
@@ -318,12 +493,6 @@
     d_residual = cot_ref[...].astype(F32) + d_rows
     tokens_grad_ref[...] = d_residual
     d_attention = d_residual.astype(BF)
-    out_grad = mm(mixed_ref[...], d_attention, TN).astype(BF)
-    for t in range(groups):
-        out_grad_ref[t] = out_grad[t * width : (t + 1) * width]
-    d_mixed = mm(d_attention, w_out_ref[...], NT).astype(BF)
-    for t in range(groups):
-        d_mixed_ref[t] = d_mixed[:, t * width : (t + 1) * width]
     x = x_ref[...].astype(F32)
     unit1, inverse1 = unit_norm(x)
     normed1 = (unit1 * gain1_ref[...]).astype(BF)
@@ -331,12 +500,14 @@
     scaling = HD ** (-0.5)
     d_normed1 = None
     for t in range(groups):
+        w_grad_ref[t, :, 3 * width : wide] = mm(d_attention, mixed_ref[t], TN).astype(BF)
+        d_mixed = mm(d_attention, w_ref[t, :, 3 * width : wide]).astype(BF)
         for i in range(images):
             rows = slice(i * SP, (i + 1) * SP)
             q = qkv_ref[t, rows, 0:width]
             k = qkv_ref[t, rows, width : 2 * width]
             v = qkv_ref[t, rows, 2 * width : 3 * width]
-            do = d_mixed_ref[t, rows, :]
+            do = d_mixed[rows]
             dq = dk = dv = None
             for j in range(heads):
                 own = lane == j
@@ -353,12 +524,12 @@
                 dq = part_q if dq is None else jnp.where(own, part_q, dq)
                 dk = part_k if dk is None else dk + part_k
                 dv = part_v if dv is None else dv + part_v
-            d_qkv_ref[t, rows, 0:width] = dq.astype(BF)
-            d_qkv_ref[t, rows, width : 2 * width] = dk.astype(BF)
-            d_qkv_ref[t, rows, 2 * width : 3 * width] = dv.astype(BF)
-        d_t = d_qkv_ref[t]
-        qkv_grad_ref[t] = mm(normed1, d_t, TN).astype(BF)
-        part = mm(d_t, w_qkv_ref[t], NT)
+            d_qkv_ref[rows, 0:width] = dq.astype(BF)
+            d_qkv_ref[rows, width : 2 * width] = dk.astype(BF)
+            d_qkv_ref[rows, 2 * width : 3 * width] = dv.astype(BF)
+        d_t = d_qkv_ref[...]
+        w_grad_ref[t, :, 0 : 3 * width] = mm(normed1, d_t, TN).astype(BF)
+        part = mm(d_t, w_ref[t, :, 0 : 3 * width], NT)
         d_normed1 = part if d_normed1 is None else d_normed1 + part
     d_rows, norm1 = norm_back(d_normed1, unit1, inverse1, gain1_ref[...])
     norm1_ref[...] = norm1
@@ -391,11 +562,7 @@
     def own(a):
         return a.reshape(images, SP, a.shape[1])[:, :SEQ].reshape(own_rows, a.shape[1])
 
-    w_qkv_all = lax.all_gather(w_qkv.reshape(D, 3 * width), "tensor", axis=0)
-    w_out_all = lax.all_gather(w_out, "tensor", axis=0, tiled=True)
-    w_in_all = lax.all_gather(w_in[0], "tensor", axis=0)
-    w_back_all = lax.all_gather(w_back[0], "tensor", axis=0)
-
+    w_own = jnp.concatenate([w_qkv.reshape(D, 3 * width), w_out.T], axis=1)
     x = padded(tokens)
     cot = padded(cotangent)
     routes_p = padded(routes, -1)
@@ -405,27 +572,42 @@
         + [jnp.ones((own_rows, 1), F32), jnp.zeros((own_rows, LANES - 3 * experts - 1), F32)],
         axis=1,
     )
-    early = call(
-        functools.partial(early_kernel, experts), shape((experts, slots, D + LANES))
-    )(routes_t, cot, padded(spread))
-    early = lax.all_to_all(early, "expert", split_axis=0, concat_axis=0, tiled=True)
-    counts = jnp.sum(early[:, :, D + 3 * experts].astype(F32), axis=1).astype(jnp.int32)
-
     gain1, gain2 = norm1_gain.reshape(1, D), norm2_gain.reshape(1, D)
     heads = tensor * width // HD
-    qkv, attend, mixed, residual, send = call(
-        functools.partial(attend_kernel, experts, images),
+    dma = pltpu.SemaphoreType.DMA
+    w_all, qkv, attend, mixed, residual, routed, early, w_in_all, w_back_all = call(
+        functools.partial(forward_kernel, experts, tensor, images),
         (
+            shape((tensor, D, 4 * width)),
             shape((tensor, rows, 3 * width)),
             shape((images, heads, SP, SP)),
-            shape((rows, D)),
+            shape((tensor, rows, width)),
             shape((rows, D), F32),
             shape((experts, slots, D)),
+            shape((experts, slots, D + LANES)),
+            shape((tensor, D, hidden)),
+            shape((tensor, hidden, D)),
+        ),
+        scratch=(
+            pltpu.VMEM((experts, rows), F32),
+            pltpu.VMEM((experts, slots, D), BF),
+            pltpu.VMEM((experts, slots, D + LANES), BF),
+            dma((5,)),
+            dma((2, tensor)),
+            dma((2, tensor, experts)),
+            dma((2, experts)),
+            dma((2, experts)),
+            dma((2, 2, tensor - 1)),
+            dma((2, 2, tensor - 1)),
         ),
         flops=2 * rows * D * D * 4,
-        moved=10_000_000,
-    )(routes_t, x, gain1, w_qkv_all, w_out_all, gain2)
-    routed = lax.all_to_all(send, "expert", split_axis=0, concat_axis=0, tiled=True)
+        moved=20_000_000,
+        far_in=(6, 7, 8),
+        far_out=(5, 6, 7, 8),
+        collective_id=0,
+        has_side_effects=True,
+    )(routes_t, x, cot, padded(spread), gain1, gain2, w_own, w_in[0], w_back[0])
+    counts = jnp.sum(early[:, :, D + 3 * experts].astype(F32), axis=1).astype(jnp.int32)
 
     w_router_wide = jnp.pad(w_router, ((0, 0), (0, LANES - experts)))
     most = up(experts * slots, CHUNK)
@@ -457,33 +639,23 @@
     returned_out = lax.all_to_all(outs, "expert", split_axis=0, concat_axis=0, tiled=True)
     grads = lax.psum_scatter(grads, "tensor", scatter_dimension=0, tiled=True)[0]
 
-    grad_tokens, qkv_grad, out_grad, norm1, norm2 = call(
+    grad_tokens, w_grad, norm1, norm2 = call(
         functools.partial(backward_kernel, experts, images),
         (
             shape((rows, D), F32),
-            shape((tensor, D, 3 * width)),
-            shape((tensor, width, D)),
+            shape((tensor, D, 4 * width)),
             shape((1, D), F32),
             shape((1, D), F32),
         ),
-        scratch=(
-            pltpu.VMEM((tensor, rows, width), BF),
-            pltpu.VMEM((tensor, rows, 3 * width), BF),
-        ),
+        scratch=(pltpu.VMEM((rows, 3 * width), BF),),
         flops=2 * rows * D * D * 10,
         moved=10_000_000,
-    )(
-        routes_p, returned, residual, cot, x, gain1, gain2,
-        w_qkv_all, w_out_all, qkv, attend, mixed,
-    )
-    output = call(functools.partial(output_kernel, experts), shape((rows, D)))(
+    )(routes_p, returned, residual, cot, x, gain1, gain2, w_all, qkv, attend, mixed)
+    (output,) = call(functools.partial(output_kernel, experts), (shape((rows, D)),))(
         routes_p, returned_out, residual
     )
-    both = jnp.concatenate(
-        [qkv_grad.reshape(tensor, 3 * width, D), out_grad.reshape(tensor, width, D)], axis=1
-    )
-    both = lax.psum_scatter(both, "tensor", scatter_dimension=0, tiled=True)[0]
-    both = lax.psum(both, "expert").astype(F32)
+    w_grad = lax.psum_scatter(w_grad, "tensor", scatter_dimension=0, tiled=True)[0]
+    w_grad = lax.psum(w_grad, "expert").astype(F32)
     router_grad, norm1, norm2 = lax.psum(
         (router_grad[:, :experts], norm1, norm2), ("expert", "tensor")
     )
@@ -491,8 +663,8 @@
         own(output),
         own(grad_tokens),
         norm1.reshape(D),
-        both[: 3 * width].reshape(D, 3, width),
-        both[3 * width :],
+        w_grad[:, : 3 * width].reshape(D, 3, width),
+        w_grad[:, 3 * width :].T,
         norm2.reshape(D),
         router_grad,
         grads[0].astype(F32)[None],

time: 433 us -> 380 us (0.88)
  waiting for transfers between devices: 189 us -> 100 us
  Pallas kernels: 73.2 us -> 146 us
  blocking collectives: 122 us -> 98.1 us
  starting transfers between devices: 9.86 us -> 0.12 us
    all_gather x3 -> x0, waiting for transfers between devices: 90 us -> none  [the longest x1 46.3 us: per_device(): w_back_all = lax.all_gather(w_back[0], 'tensor', axis=0)]
    pallas_call x5 -> x4, Pallas kernels: 73.2 us -> 146 us  [run(): pl.pallas_call(body, out_shape=out_shape, in_specs=[spec(place, far_in, p...]
    all_gather x1 -> x0, blocking collectives: 23.3 us -> none  [per_device(): w_out_all = lax.all_gather(w_out, 'tensor', axis=0, tiled=True)]
    all_to_all x2 -> x0, starting transfers between devices: 9.62 us -> none  [the longest x1 5.3 us: per_device(): lax.all_to_all(early, 'expert', split_axis=0, concat_axis=0, tiled=True)]
  transfers between devices with their start and end apart: 8 -> 3, of which waited for: 5 -> 2; matrix products, arithmetic and copies ran while one was open for 3% -> 2% of each run, Pallas kernels for 4% -> 1%
where the time goes in v2:
time: 380 us; the launch traced here: 381 us
  Pallas kernels  146 us (38%)
  waiting for transfers between devices  100 us (26%)
  blocking collectives  98.1 us (26%)
  local copies, waits for them, and re-layouts  17.4 us (5%)
  between operations  14 us (4%)
  other arithmetic  5.22 us (1%)
    pallas_call x4, Pallas kernels, run(): pl.pallas_call(body, out_shape=out_shape, in_specs=[spec(place, far_in, p...  146 us
    reduce_scatter x1, waiting for transfers between devices, per_device(): lax.psum_scatter(grads, 'tensor', scatter_dimension=0, tiled=True)[0]  54.2 us
    reduce_scatter x1, waiting for transfers between devices, per_device(): lax.psum_scatter(w_grad, 'tensor', scatter_dimension=0, tiled=True)[0]  45.3 us
    psum x1, blocking collectives, per_device(): lax.psum((router_grad[:, :experts], norm1, norm2), ('expert', 'tensor'))  43.3 us
    all_to_all x1, blocking collectives, per_device(): lax.all_to_all(outs, 'expert', split_axis=0, concat_axis=0, tiled=True)  28.2 us
    all_to_all x1, blocking collectives, per_device(): lax.all_to_all(backs, 'expert', split_axis=0, concat_axis=0, tiled=True)  26.7 us
    unnamed x28, local copies, waits for them, and re-layouts  7.76 us
  transfers between devices with their start and end apart: 3, of which 2 were waited for; matrix products, arithmetic and copies ran while one was open for 2% of the time, Pallas kernels for 1%

profile of v2, /device:TPU:0, one launch (start us, length us, event | category | flops | bytes accessed | tf_op | source)
XLA Modules:
  0.0 380.9 jit_solution(1753809234248129520)
XLA Ops:
  7.2 0.0 reduce-scatter.3.cloned.1.call-start
  7.2 0.8 reshape.94
  8.0 1.0 copy.37
  9.1 0.9 copy.40
  9.9 0.1 copy.32
  10.1 0.0 copy-start
  10.1 0.7 copy.39.routes_t_ref
  10.8 0.9 copy.33
  11.8 0.3 concatenate.6
  12.1 0.7 pad.22
  12.8 0.2 copy.36
  13.0 0.2 copy.38
  13.2 0.1 reshape.97
  13.3 0.7 pad.23.w_router_ref
  14.0 0.8 pad.20
  14.8 0.1 reshape.99
  14.9 0.8 pad.21
  15.7 0.8 pad_maximum_fusion.w_own_ref
  16.5 83.8 %shard_map.178 = (bf16[4,512,512]{2,1,0:T(8,128)(2,1)}, bf16[4,416,384]{2,1,0:T(8,128)(2,1)}, bf16[2,8,208,208]{3,2,1,0:T(8,128)(2,1)}, bf16[4,416,128]{2,1,0:T(...) custom-call(s32[2,416]{1,0:T(2,128)} %copy.39.routes_t_ref, ...), custom_call_target="tpu_custom_call" | custom-call | flops 872415232 | bytes 20000000 | tf_op jit(solution)/shard_map/pallas_call | solution.py:50
  100.4 1.3 convert_reduce_fusion
  101.7 0.5 convert_element_type.38.count_ref
  102.2 40.5 %shard_map.179 = (bf16[8,208,512]{2,1,0:T(8,128)(2,1)}, bf16[8,208,512]{2,1,0:T(8,128)(2,1)}, bf16[4,2,512,512]{3,2,1,0:T(8,128)(2,1)}, f32[512,128]{1,0:T(8,128)}) custom-call(s32[1]{0:T(128)} %bitcast.1.own_ref, s32[8]{0:T(128)} %convert_element_type.38.count_ref, bf16[8,208,512]{2,1,0:T(8,128)(2,1)} %get-tuple-element.27.x_in, ...), custom_call_target="tpu_custom_call" | custom-call | flops 20937965568 | bytes 20000000 | tf_op jit(solution)/shard_map/pallas_call | solution.py:50
  142.6 26.7 %all_to_all.10.back_ref = bf16[8,208,512]{2,1,0:T(8,128)(2,1)} all-to-all(bf16[8,208,512]{2,1,0:T(8,128)(2,1)} %get-tuple-element.32), channel_id=1, replica_groups=mesh['expert'=8,'tensor'=4] {'expert'}, dimensions={0} | all-to-all | bytes 3407872 | tf_op jit(solution)/shard_map/all_to_all | solution.py:638
  169.3 17.3 %shard_map.181 = (f32[416,512]{1,0:T(8,128)}, bf16[4,512,512]{2,1,0:T(8,128)(2,1)}, f32[1,512]{1,0:T(1,128)}, f32[1,512]{1,0:T(1,128)}) custom-call(s32[416,2]{1,0:T(8,128)} %bitcast.39, bf16[8,208,512]{2,1,0:T(8,128)(2,1)} %all_to_all.10.back_ref, f32[416,512]{1,0:T(8,128)} %get-tuple-element.31.residual_ref, bf16[416,512]{1,0:T(8,128)(2,1)} %bitcast.45, ...), custom_call_target="tpu_custom_call" | custom-call | flops 2181038080 | bytes 10000000 | tf_op jit(solution)/shard_map/pallas_call | solution.py:50
  186.7 0.0 reduce-scatter.3.cloned.1.call-update
  186.7 0.0 all-reduce.8.cloned.1.call-start
  186.7 45.3 %reduce-scatter.3.cloned.1.call-done = bf16[1,512,512]{2,1,0:T(8,128)(2,1)} async-done(((bf16[4,512,512]{2,1,0:T(8,128)(2,1)}), bf16[1,512,512]{2,1,0:T(8,128)(2,1)}) %reduce-scatter.3.cloned.1.call-update) | async-done | bytes 524304 | tf_op jit(solution)/shard_map/reduce_scatter | solution.py:657
  232.0 0.0 all-reduce.8.cloned.1.call-update
  232.1 0.0 reduce-scatter.5.cloned.1.call-start
  232.1 0.7 reduce-scatter.5.cloned.1.call-update
  232.8 0.8 copy-done.2
  233.6 28.2 %all_to_all.11.out_in = bf16[8,208,512]{2,1,0:T(8,128)(2,1)} all-to-all(bf16[8,208,512]{2,1,0:T(8,128)(2,1)S(1)} %copy-done.2), channel_id=1, replica_groups=mesh['expert'=8,'tensor'=4] {'expert'}, dimensions={0} | all-to-all | bytes 3407872 | tf_op jit(solution)/shard_map/all_to_all | solution.py:639
  261.8 4.2 %shard_map.180 = bf16[416,512]{1,0:T(8,128)(2,1)} custom-call(s32[416,2]{1,0:T(8,128)} %bitcast.40, bf16[8,208,512]{2,1,0:T(8,128)(2,1)} %all_to_all.11.out_in, f32[416,512]{1,0:T(8,128)} %get-tuple-element.31.residual_ref), custom_call_target="tpu_custom_call" | custom-call | tf_op jit(solution)/shard_map/pallas_call | solution.py:50
  265.9 1.0 slice.34
  267.0 0.0 copy-start.9
  267.0 0.8 reshape.107
  267.8 0.1 slice.35
  267.9 1.0 reshape.109
  268.9 43.3 %all-reduce.5 = (f32[512]{0:T(512)}, f32[512]{0:T(512)}, f32[512,8]{1,0:T(8,128)S(1)}) all-reduce(f32[512]{0:T(512)S(1)} %bitcast.53, f32[512]{0:T(512)S(1)} %bitcast.54, f32[512,8]{1,0:T(8,128)S(1)} %bitcast.51), channel_id=1, replica_groups=mesh['expert'=8,'tensor'=4] {'expert','tensor'}, use_global_device_ids=true, to_apply=%region_1.2 | all-reduce | flops 5120 | bytes 40960 | tf_op jit(solution)/shard_map/psum | solution.py:659
  312.1 0.7 copy.44
  312.9 1.1 slice.36
  314.0 0.3 copy.41
  314.2 1.1 copy.42
  315.4 0.1 convert_element_type.39
  315.6 0.8 copy.43
  316.4 54.2 %reduce-scatter.5.cloned.1.call-done = bf16[1,2,512,512]{3,2,1,0:T(8,128)(2,1)} async-done(((bf16[4,2,512,512]{3,2,1,0:T(8,128)(2,1)}), bf16[1,2,512,512]{3,2,1,0:T(8,128)(2,1)}) %reduce-scatter.5.cloned.1.call-update) | async-done | bytes 1048592 | tf_op jit(solution)/shard_map/reduce_scatter | solution.py:640
  370.6 2.5 convert_bitcast_fusion
  373.1 1.3 copy.45
  (23 shorter events, 0.1 us)
Async XLA Ops:
  7.2 5.6 %copy-start.6 = (bf16[512,3,128]{2,0,1:T(8,128)(2,1)S(1)}, bf16[512,3,128]{2,0,1:T(8,128)(2,1)}, u32[]{:S(2)}) copy-start(bf16[512,3,128]{2,0,1:T(8,128)(2,1)} %param.13) | copy-start | bytes 1179652
  7.2 224.8 %reduce-scatter.3.cloned.1.call-start = ((), (), s32[]{:S(2)}) async-start(), calls=%async_computation.4 | async-start | bytes 2621440 | tf_op jit(solution)/shard_map/reduce_scatter | solution.py:657
  10.1 3.1 copy-start
  10.8 2.4 copy-start.4
  12.1 2.7 copy-start.5
  186.7 126.2 %all-reduce.8.cloned.1.call-start = ((), (), s32[]{:S(2)}) async-start(), calls=%async_computation.5 | async-start | bytes 1048576 | tf_op jit(solution)/shard_map/psum | solution.py:658
  232.1 138.6 %reduce-scatter.5.cloned.1.call-start = ((), (), s32[]{:S(2)}) async-start(), calls=%async_computation.6 | async-start | bytes 5242880 | tf_op jit(solution)/shard_map/reduce_scatter | solution.py:640
  232.1 1.5 copy-start.2
  261.8 6.1 %copy-start.3 = (f32[416,512]{1,0:T(8,128)S(1)}, f32[416,512]{1,0:T(8,128)}, u32[]{:S(2)}) copy-start(f32[416,512]{1,0:T(8,128)} %get-tuple-element.37) | copy-start | bytes 2555908
  267.0 1.9 copy-start.7
  267.0 1.9 copy-start.8
  267.0 1.9 copy-start.9
  312.8 2.5 copy-start.1
Sparse Core Ops, SparseCore 0:
  186.8 45.1 reduce-scatter.2
  235.4 56.7 all-reduce.7
  294.5 76.0 reduce-scatter.4

commit v3 on v2

--- a/solution.py
+++ b/solution.py
@@ -437,7 +437,7 @@
         d_gate = jnp.sum(cot * out, -1, keepdims=True)
         d_logits = (d_gate * gate * (mine.astype(F32) - router)).astype(BF)
         backs[rows, :] = (back + mm(d_logits, w_router_ref[...], NT)).astype(BF)
-        router_grad_ref[...] += mm(x, d_logits, TN)
+        router_grad_ref[...] += mm(d_logits, x, TN)
         return 0
 
     lax.fori_loop(0, chunks, forward, 0)
@@ -477,29 +477,176 @@
         base = base + tiles
 
 
+class Sums:
+    def __init__(self, size, own, held, send_sem, recv_sem):
+        self.size, self.own, self.held = size, own, held
+        self.send_sem, self.recv_sem = send_sem, recv_sem
+        self.me = lax.axis_index("tensor")
+
+    def hops(self, way):
+        return self.me if way == 0 else self.size - 1 - self.me
+
+    def block(self, way, step):
+        ahead = self.size - 1 + self.hops(way) - step
+        return ahead if way == 0 else self.size - 1 - ahead
+
+    def copy(self, way, step, part, first):
+        toward = 1 if way == 0 else -1
+        if first:
+            src = self.own.at[self.block(way, step), part]
+        else:
+            src = self.held.at[way, max(step - 1, 0), part]
+        return remote(
+            src, self.held.at[way, step, part],
+            self.send_sem.at[way, step, part], self.recv_sem.at[way, step, part],
+            "tensor", self.me + toward,
+        )
+
+    def start_first(self):
+        for step in range(self.size - 1):
+            for part in (0, 1):
+                for way in (0, 1):
+                    pl.when(self.hops(way) == 0)(
+                        lambda way=way, step=step, part=part: self.copy(
+                            way, step, part, True
+                        ).start()
+                    )
+
+    def middle(self, way, step):
+        hops = self.hops(way)
+        return (hops >= 1) & (hops <= step) & (hops < self.size - 1)
+
+    def forward(self, step, part):
+        for way in (0, 1):
+
+            def go(way=way):
+                self.copy(way, step - 1, part, False).wait_recv()
+                held = self.held.at[way, step - 1, part]
+                mine = self.own.at[self.block(way, step), part]
+                add_into(held, mine)
+                self.copy(way, step, part, False).start()
+
+            pl.when(self.middle(way, step))(go)
+
+    def last(self, part):
+        for way in (0, 1):
+            pl.when(self.hops(way) >= 1)(
+                lambda way=way: self.copy(way, self.size - 2, part, False).wait_recv()
+            )
+
+    def finish(self):
+        for part in (0, 1):
+            for step in range(self.size - 1):
+                for way in (0, 1):
+                    sends = (self.hops(way) == 0) | self.middle(way, step)
+                    pl.when(sends)(
+                        lambda way=way, step=step, part=part: self.copy(
+                            way, step, part, False
+                        ).wait_send()
+                    )
+
+
+def add_into(held, mine):
+    rows = held.shape[0]
+    block = min(rows, 128)
+
+    def body(r, _):
+        at = pl.ds(pl.multiple_of(r * block, block), block)
+        held[at, :] = (held[at, :].astype(F32) + mine[at, :].astype(F32)).astype(BF)
+        return 0
+
+    lax.fori_loop(0, rows // block, body, 0)
+
+
 def backward_kernel(
-    experts, images, routes_ref, back_ref, residual_ref, cot_ref, x_ref, gain1_ref, gain2_ref,
-    w_ref, qkv_ref, attend_ref, mixed_ref,
-    tokens_grad_ref, w_grad_ref, norm1_ref, norm2_ref, d_qkv_ref,
+    experts, tensor, images, routes_ref, residual_ref, cot_ref, x_ref, gain1_ref, gain2_ref,
+    w_ref, qkv_ref, attend_ref, mixed_ref, grads_ref, router_ref, back_own, out_own,
+    tokens_grad_ref, output_ref, w_sum_ref, small_sum_ref, in_grad_ref, back_grad_ref,
+    d_qkv_ref, back_ref, out_ref, w_grad_ref, held, pieces, piece_send, piece_line,
+    final_ref, small_ref, small_plane, small_line_send, small_line,
+    own_sem, back_sems, out_sems, sum_send, sum_recv, w_sems, piece_sems, final_sems,
+    small_sems, small_line_sems,
 ):
-    groups, _, wide = w_ref.shape
+    wide = w_ref.shape[2]
     width = wide // 4
     heads = width // HD
+    me_e, me_t = lax.axis_index("expert"), lax.axis_index("tensor")
+    piece = D // experts
+    mine = pl.ds(pl.multiple_of(me_e * piece, piece), piece)
+
+    def place(d, arriving):
+        return lax.rem(me_e + experts - d, experts) if arriving else me_e
+
+    def swap_copy(src, dst, sems, d, arriving):
+        to = lax.rem(me_e + d, experts)
+        return remote(
+            src.at[to], dst.at[place(d, arriving)], sems.at[0, d], sems.at[1, d], "expert", to
+        )
+
+    def w_copy(t, d, arriving):
+        to = lax.rem(me_e + d, experts)
+        rows = pl.ds(pl.multiple_of(to * piece, piece), piece)
+        return remote(
+            w_grad_ref.at[t, rows], pieces.at[place(d, arriving), t],
+            w_sems.at[0, t, d], w_sems.at[1, t, d], "expert", to,
+        )
+
+    def line_copy(src, dst, sems, d, arriving):
+        owner = lax.rem(me_t + tensor - d, tensor) if arriving else me_t
+        return remote(
+            src, dst.at[owner], sems.at[0, d], sems.at[1, d],
+            "tensor", lax.rem(me_t + d, tensor),
+        )
+
+    def piece_copy(d, arriving):
+        src = piece_send.at[lax.rem(me_t + d, tensor)]
+        return line_copy(src, piece_line, piece_sems, d, arriving)
+
+    def final_copy(d, arriving):
+        rows = pl.ds(pl.multiple_of(place(d, arriving) * piece, piece), piece)
+        block = final_ref.at[rows]
+        return remote(
+            block, block, final_sems.at[0, d], final_sems.at[1, d],
+            "expert", lax.rem(me_e + d, experts),
+        )
+
+    def small_copy(d, arriving):
+        return remote(
+            small_ref, small_plane.at[place(d, arriving)], small_sems.at[0, d],
+            small_sems.at[1, d], "expert", lax.rem(me_e + d, experts),
+        )
+
+    def small_line_copy(d, arriving):
+        return line_copy(small_line_send, small_line, small_line_sems, d, arriving)
+
+    greet((("expert", experts), ("tensor", tensor)))
+    each(experts, lambda d: swap_copy(back_own, back_ref, back_sems, d, False).start())
+    keep_back = pltpu.make_async_copy(back_own.at[me_e], back_ref.at[me_e], own_sem.at[0])
+    keep_back.start()
+    sums = Sums(tensor, grads_ref, held, sum_send, sum_recv)
+    sums.start_first()
+
     slots = slots_by_row(routes_ref[...], experts)
+    unit2, inverse2 = unit_norm(residual_ref[...])
+    x = x_ref[...].astype(F32)
+    unit1, inverse1 = unit_norm(x)
+    normed1 = (unit1 * gain1_ref[...]).astype(BF)
+
+    keep_back.wait()
+    each(experts, lambda d: swap_copy(back_own, back_ref, back_sems, d, True).wait_recv())
     d_normed2 = take_rows(slots, back_ref, experts)
-    unit2, inverse2 = unit_norm(residual_ref[...])
     d_rows, norm2 = norm_back(d_normed2, unit2, inverse2, gain2_ref[...])
-    norm2_ref[...] = norm2
+    small_ref[...] = jnp.zeros_like(small_ref)
+    small_ref[0:experts, :] = router_ref[0:experts, :]
+    small_ref[experts + 1 : experts + 2, :] = norm2
     d_residual = cot_ref[...].astype(F32) + d_rows
     tokens_grad_ref[...] = d_residual
     d_attention = d_residual.astype(BF)
-    x = x_ref[...].astype(F32)
-    unit1, inverse1 = unit_norm(x)
-    normed1 = (unit1 * gain1_ref[...]).astype(BF)
     lane = ids((SP, width), 1) // HD
     scaling = HD ** (-0.5)
     d_normed1 = None
-    for t in range(groups):
+    line_steps = [(step, part) for step in range(1, tensor - 1) for part in (0, 1)]
+    for t in range(tensor):
         w_grad_ref[t, :, 3 * width : wide] = mm(d_attention, mixed_ref[t], TN).astype(BF)
         d_mixed = mm(d_attention, w_ref[t, :, 3 * width : wide]).astype(BF)
         for i in range(images):
@@ -524,21 +671,91 @@
                 dq = part_q if dq is None else jnp.where(own, part_q, dq)
                 dk = part_k if dk is None else dk + part_k
                 dv = part_v if dv is None else dv + part_v
-            d_qkv_ref[rows, 0:width] = dq.astype(BF)
-            d_qkv_ref[rows, width : 2 * width] = dk.astype(BF)
-            d_qkv_ref[rows, 2 * width : 3 * width] = dv.astype(BF)
-        d_t = d_qkv_ref[...]
-        w_grad_ref[t, :, 0 : 3 * width] = mm(normed1, d_t, TN).astype(BF)
-        part = mm(d_t, w_ref[t, :, 0 : 3 * width], NT)
+            d_qkv_ref[t, rows, 0:width] = dq.astype(BF)
+            d_qkv_ref[t, rows, width : 2 * width] = dk.astype(BF)
+            d_qkv_ref[t, rows, 2 * width : 3 * width] = dv.astype(BF)
+        w_grad_ref[t, :, 0 : 3 * width] = mm(normed1, d_qkv_ref[t], TN).astype(BF)
+        each(experts, lambda d, t=t: w_copy(t, d, False).start())
+        if t in (0, tensor // 2) and line_steps:
+            sums.forward(*line_steps.pop(0))
+    each(experts, lambda d: swap_copy(out_own, out_ref, out_sems, d, False).start())
+    keep_out = pltpu.make_async_copy(out_own.at[me_e], out_ref.at[me_e], own_sem.at[1])
+    keep_out.start()
+    for t in range(tensor):
+        part = mm(d_qkv_ref[t], w_ref[t, :, 0 : 3 * width], NT)
         d_normed1 = part if d_normed1 is None else d_normed1 + part
     d_rows, norm1 = norm_back(d_normed1, unit1, inverse1, gain1_ref[...])
-    norm1_ref[...] = norm1
     tokens_grad_ref[...] += d_rows
-
-
-def output_kernel(experts, routes_ref, out_in, residual_ref, output_ref):
-    slots = slots_by_row(routes_ref[...], experts)
-    output_ref[...] = (residual_ref[...] + take_rows(slots, out_in, experts)).astype(BF)
+    small_ref[experts : experts + 1, :] = norm1
+    each(experts, lambda d: small_copy(d, False).start())
+    small_plane[me_e] = small_ref[...]
+
+    for t in range(tensor):
+        pieces[me_e, t] = w_grad_ref[t, mine, :]
+    for t in range(tensor):
+        each(experts, lambda d, t=t: w_copy(t, d, True).wait_recv())
+        total = pieces[0, t].astype(F32)
+        for e in range(1, experts):
+            total = total + pieces[e, t].astype(F32)
+        piece_send[t] = total.astype(BF)
+    each(tensor, lambda d: piece_copy(d, False).start())
+    piece_line[me_t] = piece_send[me_t]
+    each(experts, lambda d: small_copy(d, True).wait_recv())
+    total = small_plane[0]
+    for e in range(1, experts):
+        total = total + small_plane[e]
+    small_line_send[...] = total
+    each(tensor, lambda d: small_line_copy(d, False).start())
+    small_line[me_t] = total
+    if line_steps:
+        sums.forward(*line_steps.pop(0))
+    each(tensor, lambda d: piece_copy(d, True).wait_recv())
+    total = piece_line[0].astype(F32)
+    for t in range(1, tensor):
+        total = total + piece_line[t].astype(F32)
+    final_ref[mine, :] = total.astype(BF)
+    each(experts, lambda d: final_copy(d, False).start())
+    for step, part in line_steps:
+        sums.forward(step, part)
+
+    keep_out.wait()
+    each(experts, lambda d: swap_copy(out_own, out_ref, out_sems, d, True).wait_recv())
+    output_ref[...] = (residual_ref[...] + take_rows(slots, out_ref, experts)).astype(BF)
+    each(tensor, lambda d: small_line_copy(d, True).wait_recv())
+    total = small_line[0]
+    for t in range(1, tensor):
+        total = total + small_line[t]
+    small_sum_ref[...] = total
+    each(experts, lambda d: final_copy(d, True).wait_recv())
+    w_sum_ref[...] = final_ref[...].astype(F32)
+
+    for part in (0, 1):
+        sums.last(part)
+        total = grads_ref[me_t, part].astype(F32)
+        for way in (0, 1):
+            came = held[way, tensor - 2, part].astype(F32)
+            total = total + jnp.where(sums.hops(way) >= 1, came, jnp.zeros_like(came))
+        if part == 0:
+            in_grad_ref[...] = total
+        else:
+            back_grad_ref[...] = total.T
+    sums.finish()
+
+    def sent(d):
+        swap_copy(back_own, back_ref, back_sems, d, False).wait_send()
+        swap_copy(out_own, out_ref, out_sems, d, False).wait_send()
+        for t in range(tensor):
+            w_copy(t, d, False).wait_send()
+        final_copy(d, False).wait_send()
+        small_copy(d, False).wait_send()
+
+    each(experts, sent)
+
+    def sent_line(d):
+        piece_copy(d, False).wait_send()
+        small_line_copy(d, False).wait_send()
+
+    each(tensor, sent_line)
 
 
 def per_device(
@@ -618,7 +835,7 @@
             shape((experts, slots, D)),
             shape((experts, slots, D)),
             shape((tensor, 2, D, hidden)),
-            shape((D, LANES), F32),
+            shape((LANES, D), F32),
         ),
         scratch=(
             pltpu.VMEM((most, D), BF),
@@ -635,40 +852,62 @@
         prefetch=(0, 1),
     )(own_expert, counts, routed, early, w_router_wide, w_in_all, w_back_all)
 
-    returned = lax.all_to_all(backs, "expert", split_axis=0, concat_axis=0, tiled=True)
-    returned_out = lax.all_to_all(outs, "expert", split_axis=0, concat_axis=0, tiled=True)
-    grads = lax.psum_scatter(grads, "tensor", scatter_dimension=0, tiled=True)[0]
-
-    grad_tokens, w_grad, norm1, norm2 = call(
-        functools.partial(backward_kernel, experts, images),
+    small_rows = up(experts + 2, 8)
+    piece = D // experts
+    grad_tokens, output, w_sum, small, grad_in, grad_back = call(
+        functools.partial(backward_kernel, experts, tensor, images),
         (
             shape((rows, D), F32),
-            shape((tensor, D, 4 * width)),
-            shape((1, D), F32),
-            shape((1, D), F32),
+            shape((rows, D)),
+            shape((D, 4 * width), F32),
+            shape((small_rows, D), F32),
+            shape((D, hidden), F32),
+            shape((hidden, D), F32),
         ),
-        scratch=(pltpu.VMEM((rows, 3 * width), BF),),
+        scratch=(
+            pltpu.VMEM((tensor, rows, 3 * width), BF),
+            pltpu.VMEM((experts, slots, D), BF),
+            pltpu.VMEM((experts, slots, D), BF),
+            pltpu.VMEM((tensor, D, 4 * width), BF),
+            pltpu.VMEM((2, tensor - 1, 2, D, hidden), BF),
+            pltpu.VMEM((experts, tensor, piece, 4 * width), BF),
+            pltpu.VMEM((tensor, piece, 4 * width), BF),
+            pltpu.VMEM((tensor, piece, 4 * width), BF),
+            pltpu.VMEM((D, 4 * width), BF),
+            pltpu.VMEM((small_rows, D), F32),
+            pltpu.VMEM((experts, small_rows, D), F32),
+            pltpu.VMEM((small_rows, D), F32),
+            pltpu.VMEM((tensor, small_rows, D), F32),
+            dma((2,)),
+            dma((2, experts)),
+            dma((2, experts)),
+            dma((2, tensor - 1, 2)),
+            dma((2, tensor - 1, 2)),
+            dma((2, tensor, experts)),
+            dma((2, tensor)),
+            dma((2, experts)),
+            dma((2, experts)),
+            dma((2, tensor)),
+        ),
         flops=2 * rows * D * D * 10,
-        moved=10_000_000,
-    )(routes_p, returned, residual, cot, x, gain1, gain2, w_all, qkv, attend, mixed)
-    (output,) = call(functools.partial(output_kernel, experts), (shape((rows, D)),))(
-        routes_p, returned_out, residual
-    )
-    w_grad = lax.psum_scatter(w_grad, "tensor", scatter_dimension=0, tiled=True)[0]
-    w_grad = lax.psum(w_grad, "expert").astype(F32)
-    router_grad, norm1, norm2 = lax.psum(
-        (router_grad[:, :experts], norm1, norm2), ("expert", "tensor")
+        moved=20_000_000,
+        far_in=(12, 13),
+        collective_id=1,
+        has_side_effects=True,
+    )(
+        routes_p, residual, cot, x, gain1, gain2, w_all, qkv, attend, mixed, grads, router_grad,
+        backs, outs,
     )
     return (
         own(output),
         own(grad_tokens),
-        norm1.reshape(D),
-        w_grad[:, : 3 * width].reshape(D, 3, width),
-        w_grad[:, 3 * width :].T,
-        norm2.reshape(D),
-        router_grad,
-        grads[0].astype(F32)[None],
-        grads[1].T.astype(F32)[None],
+        small[experts],
+        w_sum[:, : 3 * width].reshape(D, 3, width),
+        w_sum[:, 3 * width :].T,
+        small[experts + 1],
+        small[:experts].T,
+        grad_in[None],
+        grad_back[None],
     )
 
 

time: 380 us -> 253 us (0.67); the launches traced: 381 us -> 250 us
  waiting for transfers between devices: 100 us -> 0 us
  blocking collectives: 98.1 us -> 0 us
  Pallas kernels: 146 us -> 229 us
  between operations: 14 us -> 0.86 us
    reduce_scatter x2 -> x0, waiting for transfers between devices: 99.5 us -> none  [the longest x1 54.2 us: per_device(): lax.psum_scatter(grads, 'tensor', scatter_dimension=0, tiled=True)[0]]
    pallas_call x4 -> x3, Pallas kernels: 146 us -> 229 us  [run(): pl.pallas_call(body, out_shape=out_shape, in_specs=[spec(place, far_in, p...]
    all_to_all x2 -> x0, blocking collectives: 54.9 us -> none  [the longest x1 28.2 us: per_device(): lax.all_to_all(outs, 'expert', split_axis=0, concat_axis=0, tiled=True)]
    psum x1 -> x0, blocking collectives: 43.3 us -> none  [per_device(): lax.psum((router_grad[:, :experts], norm1, norm2), ('expert', 'tensor'))]
    unnamed x28 -> x26, local copies, waits for them, and re-layouts: 7.76 us -> 6.91 us
  transfers between devices with their start and end apart: 3 -> 0, of which waited for: 2 -> 0; matrix products, arithmetic and copies ran while one was open for 2% -> 0% of each run, Pallas kernels for 1% -> 0%
where the time goes in v3:
time: 253 us; the launch traced here: 250 us
  Pallas kernels  229 us (91%)
  local copies, waits for them, and re-layouts  16.8 us (7%)
  other arithmetic  2.65 us (1%)
    pallas_call x3, Pallas kernels, run(): pl.pallas_call(body, out_shape=out_shape, in_specs=[spec(place, far_in, p...  229 us
    unnamed x26, local copies, waits for them, and re-layouts  6.91 us

profile of v3, /device:TPU:0, one launch (start us, length us, event | category | flops | bytes accessed | tf_op | source)
XLA Modules:
  0.0 249.5 jit_solution(18403368602554645628)
XLA Ops:
  0.6 0.8 reshape.70
  1.4 1.1 copy.35
  2.5 0.9 copy.38
  3.4 0.7 pad.23.w_router_ref
  4.1 0.1 copy.30
  4.2 0.0 copy-start
  4.2 0.7 copy.37.routes_t_ref
  4.9 0.8 copy.31
  5.8 0.0 copy-start.5
  5.8 0.3 concatenate.6
  6.2 0.7 pad.22
  6.9 0.0 copy-done.7
  6.9 0.2 copy.34
  7.1 0.2 copy.36
  7.3 0.0 copy-done
  7.3 0.8 pad_maximum_fusion.w_own_ref
  8.1 0.0 copy-done.5
  8.1 0.1 reshape.72
  8.2 0.8 pad.20
  9.0 0.0 copy-done.6
  9.0 0.1 reshape.74
  9.1 0.8 pad.21
  9.9 83.8 %shard_map.178 = (bf16[4,512,512]{2,1,0:T(8,128)(2,1)}, bf16[4,416,384]{2,1,0:T(8,128)(2,1)}, bf16[2,8,208,208]{3,2,1,0:T(8,128)(2,1)}, bf16[4,416,128]{2,1,0:T(...) custom-call(s32[2,416]{1,0:T(2,128)} %copy.37.routes_t_ref, ...), custom_call_target="tpu_custom_call" | custom-call | flops 872415232 | bytes 20000000 | tf_op jit(solution)/shard_map/pallas_call | solution.py:50
  93.6 1.3 convert_reduce_fusion
  94.9 0.5 convert_element_type.15.count_ref
  95.5 40.3 %shard_map.179 = (bf16[8,208,512]{2,1,0:T(8,128)(2,1)}, bf16[8,208,512]{2,1,0:T(8,128)(2,1)}, bf16[4,2,512,512]{3,2,1,0:T(8,128)(2,1)}, f32[128,512]{1,0:T(8,128)}) custom-call(s32[1]{0:T(128)} %bitcast.11.own_ref, s32[8]{0:T(128)} %convert_element_type.15.count_ref, bf16[8,208,512]{2,1,0:T(8,128)(2,1)} %get-tuple-element.34.x_in, ...), custom_call_target="tpu_custom_call" | custom-call | flops 20937965568 | bytes 20000000 | tf_op jit(solution)/shard_map/pallas_call | solution.py:50
  135.8 105.2 %shard_map.180 = (f32[416,512]{1,0:T(8,128)}, bf16[416,512]{1,0:T(8,128)(2,1)}, f32[512,512]{1,0:T(8,128)}, f32[16,512]{1,0:T(8,128)}, f32[512,512]{1,0:T(8,128)}, /*index=5*/f32[512,512]{1,0:T(8,128)}) custom-call(s32[416,2]{1,0:T(8,128)} %bitcast.28, f32[416,512]{1,0:T(8,128)} %get-tuple-element.28.residual_ref, bf16[416,512]{1,0:T(8,128)(2,1)} %bitcast.32, ...), custom_call_target="tpu_custom_call" | custom-call | flops 2181038080 | bytes 20000000 | tf_op jit(solution)/shard_map/pallas_call | solution.py:50
  241.0 0.0 copy-start.4
  241.0 1.1 slice.32
  242.1 0.0 copy-start.8
  242.1 0.0 copy-start.1
  242.1 0.8 reshape.83
  242.9 0.0 copy-done.4
  242.9 0.1 slice.33
  243.0 1.0 reshape.85
  244.0 0.0 copy-done.8
  244.0 0.6 fusion
  244.6 0.6 slice_bitcast_fusion.1
  245.2 0.0 copy-done.1
  245.2 0.1 slice.28
  245.3 0.3 copy.39
  245.5 0.0 copy-start.3
  245.6 1.1 copy.40
  246.7 0.8 copy.41
  247.6 0.0 copy-done.3
  247.6 1.0 copy.44
  248.5 0.0 copy-done.2
  248.5 1.0 copy.45
  (8 shorter events, 0.1 us)
Async XLA Ops:
  1.4 5.5 %copy-start.7 = (bf16[512,3,128]{2,0,1:T(8,128)(2,1)S(1)}, bf16[512,3,128]{2,0,1:T(8,128)(2,1)}, u32[]{:S(2)}) copy-start(bf16[512,3,128]{2,0,1:T(8,128)(2,1)} %param.13) | copy-start | bytes 1179652
  4.2 3.1 %copy-start = (s32[2,208,2]{2,1,0:T(8,128)}, s32[2,208,2]{2,1,0:T(8,128)S(1)}, u32[]{:S(2)}) copy-start(s32[2,208,2]{2,1,0:T(8,128)S(1)} %pad.19) | copy-start | bytes 9988
  5.8 2.3 copy-start.5
  6.9 2.1 copy-start.6
  241.0 2.0 copy-start.4
  242.1 1.9 copy-start.8
  242.1 3.1 %copy-start.1 = (f32[512,512]{1,0:T(8,128)S(1)}, f32[512,512]{1,0:T(8,128)}, u32[]{:S(2)}) copy-start(f32[512,512]{1,0:T(8,128)} %get-tuple-element.44) | copy-start | bytes 3145732
  245.5 2.0 copy-start.3
  245.6 3.0 %copy-start.2 = (f32[512,512]{1,0:T(8,128)S(1)}, f32[512,512]{1,0:T(8,128)}, u32[]{:S(2)}) copy-start(f32[512,512]{1,0:T(8,128)} %get-tuple-element.46) | copy-start | bytes 3145732

commit v4 on v3

v4 whole, which is shorter than its diff:
```python
import functools

import jax
import jax.numpy as jnp
from jax import lax
from jax.experimental import pallas as pl
from jax.experimental.pallas import tpu as pltpu
from jax.sharding import PartitionSpec as P

D = 512
HD = 64
TOP = 2
SEQ = 197
LANES = 128
TILE = 16
EPSILON = 1e-06
BF = jnp.bfloat16
F32 = jnp.float32
VMEM_BYTES = 62 * 1024 * 1024

NN = (((1,), (0,)), ((), ()))
NT = (((1,), (1,)), ((), ()))
TN = (((0,), (0,)), ((), ()))


def up(value, unit):
    return (value + unit - 1) // unit * unit


SP = up(SEQ, TILE)


def mm(a, b, dims=NN):
    return lax.dot_general(a, b, dims, preferred_element_type=F32)


def call(
    body, out_shape, scratch=(), flops=0, moved=0, prefetch=(), far_in=(), far_out=(), **more
):
    params = pltpu.CompilerParams(vmem_limit_bytes=VMEM_BYTES, **more)
    cost = pl.CostEstimate(flops=flops, bytes_accessed=moved, transcendentals=0)

    def spec(place, far, scalar=()):
        if place in scalar:
            return pl.BlockSpec(memory_space=pltpu.SMEM)
        return pl.BlockSpec(memory_space=pl.ANY if place in far else pltpu.VMEM)

    def run(*args):
        return pl.pallas_call(
            body,
            out_shape=out_shape,
            in_specs=[spec(place, far_in, prefetch) for place in range(len(args))],
            out_specs=tuple(spec(place, far_out) for place in range(len(out_shape))),
            scratch_shapes=list(scratch),
            compiler_params=params,
            cost_estimate=cost,
        )(*args)

    return run


def shape(dims, dtype=BF):
    return jax.ShapeDtypeStruct(dims, dtype)


def unit_norm(values):
    center = values - jnp.mean(values, -1, keepdims=True)
    spread = jnp.mean(center * center, -1, keepdims=True)
    inverse = lax.rsqrt(spread + EPSILON)
    return center * inverse, inverse


def norm_back(grad_rows, normed, inverse, gain):
    scaled = grad_rows * gain
    inner = (
        scaled
        - jnp.mean(scaled, -1, keepdims=True)
        - normed * jnp.mean(scaled * normed, -1, keepdims=True)
    )
    return inverse * inner, jnp.sum(grad_rows * normed, axis=0, keepdims=True)


def ids(shape_of, dim):
    return lax.broadcasted_iota(jnp.int32, shape_of, dim)


def slots_by_row(routes, experts):
    rows = routes.shape[0]
    which = ids((rows, experts), 1)
    named = (routes[:, 0:1] == which) | (routes[:, 1:2] == which)
    before = (ids((rows, rows), 1) < ids((rows, rows), 0)).astype(F32).astype(BF)
    rank = mm(before, named.astype(F32).astype(BF))
    return jnp.where(named, rank, -1.0)


def take_rows(slots, in_ref, experts):
    count = in_ref.shape[1]
    rows = slots.shape[0]
    place = ids((rows, count), 1).astype(F32)
    total = None
    for e in range(experts):
        pick = (place == slots[:, e : e + 1]).astype(F32).astype(BF)
        part = mm(pick, in_ref[e])
        total = part if total is None else total + part
    return total


MESH = pl.DeviceIdType.MESH


def greet(axes):
    barrier = pltpu.get_barrier_semaphore()
    for name, size in axes:
        me = lax.axis_index(name)

        def hello(d, _, name=name, size=size, me=me):
            pl.semaphore_signal(
                barrier, inc=1, device_id={name: lax.rem(me + d, size)}, device_id_type=MESH
            )
            return 0

        lax.fori_loop(1, size, hello, 0)
    pl.semaphore_wait(barrier, sum(size - 1 for _, size in axes))


def remote(src, dst, send_sem, recv_sem, name, to):
    return pltpu.make_async_remote_copy(
        src_ref=src,
        dst_ref=dst,
        send_sem=send_sem,
        recv_sem=recv_sem,
        device_id={name: to},
        device_id_type=MESH,
    )


def each(size, step):
    def body(d, _):
        step(d)
        return 0

    lax.fori_loop(1, size, body, 0)


class Line:
    def __init__(self, size, own, everyone, send_sem, recv_sem):
        self.size, self.own, self.all = size, own, everyone
        self.send_sem, self.recv_sem = send_sem, recv_sem
        self.me = lax.axis_index("tensor")

    def copy(self, way, step, arriving):
        toward = 1 if way == 0 else -1
        owner = self.me - toward * (step + (1 if arriving else 0))
        src = self.own if step == 0 else self.all.at[owner]
        return remote(
            src, self.all.at[owner], self.send_sem.at[way, step], self.recv_sem.at[way, step],
            "tensor", self.me + toward,
        )

    def sends(self, way, step):
        last = self.size - 1
        if way == 0:
            return (self.me >= step) & (self.me < last)
        return (self.me <= last - step) & (self.me > 0)

    def receives(self, way, step):
        if way == 0:
            return self.me >= step + 1
        return self.me <= self.size - 2 - step

    def start(self, step):
        for way in (0, 1):
            pl.when(self.sends(way, step))(lambda way=way: self.copy(way, step, False).start())

    def arrive(self, step):
        for way in (0, 1):
            pl.when(self.receives(way, step))(
                lambda way=way: self.copy(way, step, True).wait_recv()
            )

    def finish(self):
        for step in range(self.size - 1):
            for way in (0, 1):
                pl.when(self.sends(way, step))(
                    lambda way=way, step=step: self.copy(way, step, False).wait_send()
                )


def gelu_parts(pre):
    density = jnp.exp(pre * pre * -0.5)
    size = jnp.abs(pre) * (0.5**0.5)
    t = 1.0 / (1.0 + 0.3275911 * size)
    series = t * (
        0.254829592
        + t * (-0.284496736 + t * (1.421413741 + t * (-1.453152027 + t * 1.061405429)))
    )
    tail = 0.5 * series * density
    return jnp.where(pre < 0, tail, 1.0 - tail), density * 0.3989422804014327


class Sums:
    def __init__(self, size, own, held, send_sem, recv_sem):
        self.size, self.own, self.held = size, own, held
        self.send_sem, self.recv_sem = send_sem, recv_sem
        self.me = lax.axis_index("tensor")

    def hops(self, way):
        return self.me if way == 0 else self.size - 1 - self.me

    def block(self, way, step):
        ahead = self.size - 1 + self.hops(way) - step
        return ahead if way == 0 else self.size - 1 - ahead

    def copy(self, way, step, part, first):
        toward = 1 if way == 0 else -1
        if first:
            src = self.own(self.block(way, step), part)
        else:
            src = self.held.at[way, max(step - 1, 0), part]
        return remote(
            src, self.held.at[way, step, part],
            self.send_sem.at[way, step, part], self.recv_sem.at[way, step, part],
            "tensor", self.me + toward,
        )

    def start_first(self, way, step):
        for part in (0, 1):
            pl.when(self.hops(way) == 0)(
                lambda part=part: self.copy(way, step, part, True).start()
            )

    def middle(self, way, step):
        hops = self.hops(way)
        return (hops >= 1) & (hops <= step) & (hops < self.size - 1)

    def forward(self, step, part):
        for way in (0, 1):

            def go(way=way):
                self.copy(way, step - 1, part, False).wait_recv()
                held = self.held.at[way, step - 1, part]
                mine = self.own(self.block(way, step), part)
                add_into(held, mine)
                self.copy(way, step, part, False).start()

            pl.when(self.middle(way, step))(go)

    def last(self, part):
        for way in (0, 1):
            pl.when(self.hops(way) >= 1)(
                lambda way=way: self.copy(way, self.size - 2, part, False).wait_recv()
            )

    def finish(self):
        for part in (0, 1):
            for step in range(self.size - 1):
                for way in (0, 1):
                    sends = (self.hops(way) == 0) | self.middle(way, step)
                    pl.when(sends)(
                        lambda way=way, step=step, part=part: self.copy(
                            way, step, part, False
                        ).wait_send()
                    )


def add_into(held, mine):
    rows = held.shape[0]
    block = min(rows, 128)

    def body(r, _):
        at = pl.ds(pl.multiple_of(r * block, block), block)
        held[at, :] = (held[at, :].astype(F32) + mine[at, :].astype(F32)).astype(BF)
        return 0

    lax.fori_loop(0, rows // block, body, 0)


def block_kernel(
    experts, tensor, images, group,
    routes_ref, tokens_ref, cotangent_ref, noise_ref, gain1_ref, gain2_ref, w_router_ref,
    w_own_ref, w_in_own, w_back_own,
    output_ref, tokens_grad_ref, w_sum_ref, small_sum_ref, in_grad_ref, back_grad_ref,
    w_ref, w_in_all, w_back_all, narrow, x_ref, cot_ref, rows_ref, lanes_ref,
    qkv_ref, attend_ref, mixed_ref, residual_ref, d_qkv_ref,
    send_ref, routed_ref, early_send, early_ref, noise_send, noise_all, router_ref,
    hidden_ref, slope_ref, back_ref, out_ref, held,
    w_grad_ref, pieces, piece_send, piece_line,
    small_ref, small_plane, small_line_send, small_line,
    own_sem, first_sems, plane_sems, in_sems, in_back_sems, route_sems, early_sems, noise_sems,
    back_sems, out_sems, sum_send, sum_recv, w_sems, piece_sems, final_sems,
    small_sems, small_line_sems,
):
    own_rows = tokens_ref.shape[0]
    wide = w_own_ref.shape[1]
    width = wide // 4
    heads = width // HD
    slots = send_ref.shape[1]
    parts = w_in_all.shape[0]
    chunk = group * slots
    me_e, me_t = lax.axis_index("expert"), lax.axis_index("tensor")
    piece = D // experts

    def rows_at(e):
        return pl.ds(pl.multiple_of(e * piece, piece), piece)

    mine = rows_at(me_e)

    def after(d):
        return lax.rem(me_e + d, experts)

    def place(d, arriving):
        return lax.rem(me_e + experts - d, experts) if arriving else me_e

    def swap_copy(src, dst, sems, d, arriving):
        to = after(d)
        return remote(
            src.at[to], dst.at[place(d, arriving)], sems.at[0, d], sems.at[1, d], "expert", to
        )

    def line_copy(src, dst, sems, d, arriving):
        owner = lax.rem(me_t + tensor - d, tensor) if arriving else me_t
        return remote(
            src, dst(owner), sems.at[0, d], sems.at[1, d],
            "tensor", lax.rem(me_t + d, tensor),
        )

    def first_copy(d, arriving):
        return line_copy(
            w_own_ref.at[mine], lambda owner: w_ref.at[owner, mine], first_sems, d, arriving
        )

    def plane_copy(z, d, arriving):
        owner = lax.rem(me_t + tensor - z, tensor)
        block = w_ref.at[owner, rows_at(place(d, arriving))]
        return remote(
            block, block, plane_sems.at[0, z, d], plane_sems.at[1, z, d], "expert", after(d)
        )

    def route_copy(d, arriving):
        return swap_copy(send_ref, routed_ref, route_sems, d, arriving)

    def early_copy(d, arriving):
        return swap_copy(early_send, early_ref, early_sems, d, arriving)

    def noise_copy(d, arriving):
        return swap_copy(noise_send, noise_all, noise_sems, d, arriving)

    def back_copy(d, arriving):
        return swap_copy(early_send, back_ref, back_sems, d, arriving)

    def out_copy(d, arriving):
        return swap_copy(send_ref, out_ref, out_sems, d, arriving)

    def w_copy(t, d, arriving):
        return remote(
            w_grad_ref.at[t, rows_at(after(d))], pieces.at[place(d, arriving), t],
            w_sems.at[0, t, d], w_sems.at[1, t, d], "expert", after(d),
        )

    def piece_copy(d, arriving):
        src = piece_send.at[lax.rem(me_t + d, tensor)]
        return line_copy(src, lambda owner: piece_line.at[owner], piece_sems, d, arriving)

    def final_copy(d, arriving):
        block = w_sum_ref.at[rows_at(place(d, arriving))]
        return remote(block, block, final_sems.at[0, d], final_sems.at[1, d], "expert", after(d))

    def small_copy(d, arriving):
        return remote(
            small_ref, small_plane.at[place(d, arriving)], small_sems.at[0, d],
            small_sems.at[1, d], "expert", after(d),
        )

    def small_line_copy(d, arriving):
        return line_copy(
            small_line_send, lambda owner: small_line.at[owner], small_line_sems, d, arriving
        )

    greet((("expert", experts), ("tensor", tensor)))
    each(tensor, lambda d: first_copy(d, False).start())
    line_in = Line(tensor, w_in_own, w_in_all, in_sems.at[0], in_sems.at[1])
    line_back = Line(tensor, w_back_own, w_back_all, in_back_sems.at[0], in_back_sems.at[1])
    line_in.start(0)
    keep = [
        pltpu.make_async_copy(w_own_ref, w_ref.at[me_t], own_sem.at[0]),
        pltpu.make_async_copy(w_in_own, w_in_all.at[me_t], own_sem.at[1]),
        pltpu.make_async_copy(w_back_own, w_back_all.at[me_t], own_sem.at[2]),
    ]
    for copy in keep:
        copy.start()

    def spread(compact, to_ref, fill=0.0):
        columns = compact.shape[1]
        narrow[0:own_rows, 0:columns] = compact
        to_ref[...] = jnp.full(to_ref.shape, fill, F32)
        for i in range(images):
            to_ref[i * SP : i * SP + SEQ, 0:columns] = narrow[
                i * SEQ : (i + 1) * SEQ, 0:columns
            ]

    def compact(padded):
        for i in range(images):
            narrow[i * SEQ : (i + 1) * SEQ, :] = padded[i * SP : i * SP + SEQ, :]
        return narrow[0:own_rows, :]

    spread(noise_ref[...], rows_ref)
    noise = rows_ref[...].T[0:experts, :]
    high = noise.astype(BF).astype(F32)
    middle = (noise - high).astype(BF).astype(F32)
    low = noise - high - middle
    noise_parts = [high, middle, low]
    if noise_send.shape[1] > 3 * experts:
        noise_parts.append(jnp.zeros((noise_send.shape[1] - 3 * experts, noise.shape[1]), F32))
    noise = jnp.concatenate(noise_parts, axis=0).astype(BF)
    spread(slots_by_row(routes_ref[...], experts), rows_ref, -1.0)
    lanes_ref[...] = rows_ref[...].T[0:experts, :]
    spread(cotangent_ref[...].astype(F32), cot_ref)
    cot_low = cot_ref[...].astype(BF)
    spot = ids((slots, lanes_ref.shape[1]), 0).astype(F32)

    def pick_of(e):
        return (spot == lanes_ref[pl.ds(e, 1), :]).astype(F32).astype(BF)

    def forward_piece(z):
        first_copy(z, True).wait_recv()
        each(experts, lambda d: plane_copy(z, d, False).start())

    each(tensor, forward_piece)
    for d in range(1, experts + 1):
        e = after(d)
        pick = pick_of(e)
        rows_of_e = mm(pick, cot_low).astype(BF)
        noise_of_e = mm(noise, pick, NT).astype(BF)
        if d < experts:
            early_send[e] = rows_of_e
            noise_send[e] = noise_of_e
            early_copy(d, False).start()
            noise_copy(d, False).start()
        else:
            early_ref[e] = rows_of_e
            noise_all[e] = noise_of_e
    spread(tokens_ref[...].astype(F32), x_ref)
    x = x_ref[...]
    unit1, inverse1 = unit_norm(x)
    normed1 = (unit1 * gain1_ref[...]).astype(BF)
    line_in.arrive(0)
    if tensor > 2:
        line_in.start(1)
    line_back.start(0)
    keep[0].wait()
    each(tensor, lambda z: each(experts, lambda d: plane_copy(z, d, True).wait_recv()))

    lane = ids((SP, width), 1) // HD
    live = ids((SP, SP), 1) < SEQ
    for t in range(tensor):
        qkv_ref[t] = mm(normed1, w_ref[t, :, 0 : 3 * width]).astype(BF)
        for i in range(images):
            rows = slice(i * SP, (i + 1) * SP)
            q = qkv_ref[t, rows, 0:width]
            k = qkv_ref[t, rows, width : 2 * width]
            v = qkv_ref[t, rows, 2 * width : 3 * width]
            mixed = None
            for j in range(heads):
                q_j = q if heads == 1 else jnp.where(lane == j, q, jnp.zeros_like(q))
                scores = mm(q_j, k, NT) * HD ** (-0.5)
                scores = jnp.where(live, scores, -1e30)
                power = jnp.exp(scores - jnp.max(scores, -1, keepdims=True))
                attend = (power / jnp.sum(power, -1, keepdims=True)).astype(BF)
                attend_ref[i, t * heads + j] = attend
                part = mm(attend, v)
                mixed = part if mixed is None else jnp.where(lane == j, part, mixed)
            mixed_ref[t, rows, :] = mixed.astype(BF)
        if t == tensor // 2 - 1 and tensor > 3:
            line_in.arrive(1)
            line_in.start(2)
    residual = x
    for t in range(tensor):
        residual = residual + mm(mixed_ref[t], w_ref[t, :, 3 * width : wide], NT)
    residual_ref[...] = residual
    unit2, inverse2 = unit_norm(residual)
    normed2 = (unit2 * gain2_ref[...]).astype(BF)
    for d in range(1, experts + 1):
        e = after(d)
        rows_of_e = mm(pick_of(e), normed2).astype(BF)
        if d < experts:
            send_ref[e] = rows_of_e
            route_copy(d, False).start()
        else:
            routed_ref[e] = rows_of_e
    done_in, done_back = (2 if tensor > 3 else 1), 0
    for step in range(tensor - 1):
        if step >= done_in:
            line_in.arrive(step)
            if step + 1 < tensor - 1:
                line_in.start(step + 1)
        if step < tensor - 2:
            line_back.arrive(step)
            line_back.start(step + 1)
    if done_in > tensor - 2:
        line_in.arrive(tensor - 2)
    keep[1].wait()

    fold_from, fold_to = ids((noise_all.shape[1], LANES), 0), ids((noise_all.shape[1], LANES), 1)
    fold = (
        (fold_from < 3 * experts) & (lax.rem(fold_from, experts) == fold_to)
    ).astype(F32).astype(BF)
    expert_lane = ids((chunk, LANES), 1)
    groups = experts // group

    def block_rows(at):
        return pl.ds(pl.multiple_of(at * chunk, chunk), chunk)

    def all_slots(ref, at):
        if group == 1:
            return ref[at]
        return ref[pl.ds(at * group, group)].reshape(chunk, ref.shape[2])

    def hidden_units(turn, _):
        at = lax.rem(me_e // group + groups - turn, groups)
        for k in range(group):
            d = lax.rem(me_e + experts - (at * group + k), experts)

            @pl.when(d > 0)
            def _(d=d):
                route_copy(d, True).wait_recv()
                early_copy(d, True).wait_recv()
                noise_copy(d, True).wait_recv()

        rows = block_rows(at)
        came = all_slots(routed_ref, at)
        added = [mm(noise_all[at * group + k], fold, TN) for k in range(group)]
        added = added[0] if group == 1 else jnp.concatenate(added, axis=0)
        logits = jnp.where(expert_lane < experts, mm(came, w_router_ref[...]) + added, -1e30)
        power = jnp.exp(logits - jnp.max(logits, -1, keepdims=True))
        router_ref[rows, :] = power / jnp.sum(power, -1, keepdims=True)
        for f in range(parts):
            pre = mm(came, w_in_all[f])
            normal, density = gelu_parts(pre)
            hidden_ref[f, rows, :] = (pre * normal).astype(BF)
            slope_ref[f, rows, :] = (normal + pre * density).astype(BF)
        return 0

    lax.fori_loop(0, groups, hidden_units, 0)

    line_back.arrive(tensor - 2)
    keep[2].wait()

    def early_sent(d):
        early_copy(d, False).wait_send()
        route_copy(d, False).wait_send()

    each(experts, early_sent)

    small_ref[...] = jnp.zeros_like(small_ref)

    def expert_rows(turn, _):
        at = lax.rem(me_e // group + groups - turn, groups)
        rows = block_rows(at)
        came = all_slots(routed_ref, at)
        router = router_ref[rows, :]
        own_lane = expert_lane == me_e
        gate = jnp.sum(jnp.where(own_lane, router, 0.0), -1, keepdims=True)
        cot = all_slots(early_ref, at).astype(F32)
        d_exp = (gate * cot).astype(BF)
        out = jnp.zeros((chunk, D), F32)
        back = jnp.zeros((chunk, D), F32)
        for f in range(parts):
            w_b = w_back_all[f]
            out = out + mm(hidden_ref[f, rows, :], w_b)
            d_pre = (mm(d_exp, w_b, NT) * slope_ref[f, rows, :].astype(F32)).astype(BF)
            slope_ref[f, rows, :] = d_pre
            back = back + mm(d_pre, w_in_all[f], NT)
        out = out.astype(BF).astype(F32)
        d_gate = jnp.sum(cot * out, -1, keepdims=True)
        d_logits = (d_gate * gate * (own_lane.astype(F32) - router)).astype(BF)
        back = (back + mm(d_logits, w_router_ref[...], NT)).astype(BF)
        out = (gate * out).astype(BF)
        small_ref[0:experts, :] += mm(d_logits, came, TN)[0:experts]
        for k in range(group):
            e = at * group + k
            part = slice(k * slots, (k + 1) * slots)
            early_ref[e] = d_exp[part]
            d = lax.rem(e + experts - me_e, experts)

            @pl.when(d > 0)
            def _(d=d, e=e, part=part):
                send_ref[e] = out[part]
                early_send[e] = back[part]
                back_copy(d, False).start()

            @pl.when(d == 0)
            def _(e=e, part=part):
                out_ref[e] = out[part]
                back_ref[e] = back[part]

        return 0

    lax.fori_loop(0, groups, expert_rows, 0)

    def grads_at(block, part):
        return slope_ref.at[block, part * D : (part + 1) * D]

    sums = Sums(tensor, grads_at, held, sum_send, sum_recv)
    order = []
    for step in range(tensor):
        for f in (tensor - 1 - step, step):
            if f not in order:
                order.append(f)
    for f in order:
        for part, left, right in ((0, routed_ref, slope_ref), (1, early_ref, hidden_ref)):
            in_grad_ref[...] = jnp.zeros_like(in_grad_ref)

            def add_in(at, _, f=f, left=left, right=right):
                in_grad_ref[...] += mm(all_slots(left, at), right[f, block_rows(at), :], TN)
                return 0

            lax.fori_loop(0, groups, add_in, 0)
            grads_at(f, part)[...] = in_grad_ref[...].astype(BF)
        for step in range(tensor - 1):
            for way, block in ((0, tensor - 1 - step), (1, step)):
                if block == f:
                    sums.start_first(way, step)
    each(experts, lambda d: out_copy(d, False).start())

    each(experts, lambda d: back_copy(d, True).wait_recv())
    slots_of = rows_ref[:, 0:experts]
    d_normed2 = take_rows(slots_of, back_ref, experts)
    unit2, inverse2 = unit_norm(residual_ref[...])
    d_rows, norm2 = norm_back(d_normed2, unit2, inverse2, gain2_ref[...])
    small_ref[experts + 1 : experts + 2, :] = norm2
    d_residual = cot_ref[...] + d_rows
    cot_ref[...] = d_residual
    d_attention = d_residual.astype(BF)
    scaling = HD ** (-0.5)
    line_steps = [(step, part) for step in range(1, tensor - 1) for part in (0, 1)]
    unit1, inverse1 = unit_norm(x_ref[...])
    normed1 = (unit1 * gain1_ref[...]).astype(BF)
    for t in range(tensor):
        w_grad_ref[t, :, 3 * width : wide] = mm(d_attention, mixed_ref[t], TN).astype(BF)
        d_mixed = mm(d_attention, w_ref[t, :, 3 * width : wide]).astype(BF)
        for i in range(images):
            rows = slice(i * SP, (i + 1) * SP)
            q = qkv_ref[t, rows, 0:width]
            k = qkv_ref[t, rows, width : 2 * width]
            v = qkv_ref[t, rows, 2 * width : 3 * width]
            do = d_mixed[rows]
            dq = dk = dv = None
            for j in range(heads):
                own = lane == j
                do_j = do if heads == 1 else jnp.where(own, do, jnp.zeros_like(do))
                q_j = q if heads == 1 else jnp.where(own, q, jnp.zeros_like(q))
                attend_low = attend_ref[i, t * heads + j]
                attend = attend_low.astype(F32)
                part_v = mm(attend_low, do_j, TN)
                d_attend = mm(do_j, v, NT)
                inner = jnp.sum(attend * d_attend, -1, keepdims=True)
                ds = (attend * (d_attend - inner)).astype(BF)
                part_q = mm(ds, k) * scaling
                part_k = mm(ds, q_j, TN) * scaling
                dq = part_q if dq is None else jnp.where(own, part_q, dq)
                dk = part_k if dk is None else dk + part_k
                dv = part_v if dv is None else dv + part_v
            d_qkv_ref[t, rows, 0:width] = dq.astype(BF)
            d_qkv_ref[t, rows, width : 2 * width] = dk.astype(BF)
            d_qkv_ref[t, rows, 2 * width : 3 * width] = dv.astype(BF)
        w_grad_ref[t, :, 0 : 3 * width] = mm(normed1, d_qkv_ref[t], TN).astype(BF)
        each(experts, lambda d, t=t: w_copy(t, d, False).start())
        if t in (0, tensor // 2) and line_steps:
            sums.forward(*line_steps.pop(0))
    d_normed1 = None
    for t in range(tensor):
        part = mm(d_qkv_ref[t], w_ref[t, :, 0 : 3 * width], NT)
        d_normed1 = part if d_normed1 is None else d_normed1 + part
    d_rows, norm1 = norm_back(d_normed1, unit1, inverse1, gain1_ref[...])
    small_ref[experts : experts + 1, :] = norm1
    each(experts, lambda d: small_copy(d, False).start())
    small_plane[me_e] = small_ref[...]
    tokens_grad_ref[...] = compact(cot_ref[...] + d_rows)

    each(experts, lambda d: out_copy(d, True).wait_recv())
    output = residual_ref[...] + take_rows(slots_of, out_ref, experts)
    output_ref[...] = compact(output).astype(BF)

    for t in range(tensor):
        pieces[me_e, t] = w_grad_ref[t, mine, :]
    for t in range(tensor):
        each(experts, lambda d, t=t: w_copy(t, d, True).wait_recv())
        total = pieces[0, t].astype(F32)
        for e in range(1, experts):
            total = total + pieces[e, t].astype(F32)
        piece_send[t] = total.astype(BF)
    each(tensor, lambda d: piece_copy(d, False).start())
    piece_line[me_t] = piece_send[me_t]
    each(experts, lambda d: small_copy(d, True).wait_recv())
    total = small_plane[0]
    for e in range(1, experts):
        total = total + small_plane[e]
    small_line_send[...] = total
    each(tensor, lambda d: small_line_copy(d, False).start())
    small_line[me_t] = total
    if line_steps:
        sums.forward(*line_steps.pop(0))
    each(tensor, lambda d: piece_copy(d, True).wait_recv())
    total = piece_line[0].astype(F32)
    for t in range(1, tensor):
        total = total + piece_line[t].astype(F32)
    w_sum_ref[mine, :] = total.astype(BF)
    each(experts, lambda d: final_copy(d, False).start())
    for step, part in line_steps:
        sums.forward(step, part)

    each(tensor, lambda d: small_line_copy(d, True).wait_recv())
    total = small_line[0]
    for t in range(1, tensor):
        total = total + small_line[t]
    small_sum_ref[...] = total
    each(experts, lambda d: final_copy(d, True).wait_recv())

    for part in (0, 1):
        sums.last(part)
        total = grads_at(me_t, part)[...].astype(F32)
        for way in (0, 1):
            came = held[way, tensor - 2, part].astype(F32)
            total = total + jnp.where(sums.hops(way) >= 1, came, jnp.zeros_like(came))
        if part == 0:
            in_grad_ref[...] = total
        else:
            back_grad_ref[...] = total.T

    sums.finish()
    line_in.finish()
    line_back.finish()

    def sent(d):
        noise_copy(d, False).wait_send()
        back_copy(d, False).wait_send()
        out_copy(d, False).wait_send()
        for t in range(tensor):
            w_copy(t, d, False).wait_send()
        final_copy(d, False).wait_send()
        small_copy(d, False).wait_send()

    each(experts, sent)

    def sent_line(d):
        first_copy(d, False).wait_send()
        piece_copy(d, False).wait_send()
        small_line_copy(d, False).wait_send()
        each(experts, lambda k: plane_copy(d, k, False).wait_send())

    each(tensor, sent_line)


def per_device(
    tokens, norm1_gain, w_qkv, w_out, norm2_gain, w_router, noise, routes, w_in, w_back, cotangent
):
    own_rows = tokens.shape[0]
    experts = noise.shape[1]
    tensor = lax.axis_size("tensor")
    images = own_rows // SEQ
    rows = images * SP
    capacity = (2 * own_rows * TOP + experts - 1) // experts
    slots = up(capacity, TILE)
    group = max(1, 128 // slots)
    width = w_out.shape[0]
    hidden = w_in.shape[2]
    heads = tensor * width // HD
    piece = D // experts
    small_rows = up(experts + 2, 8)
    noise_rows = up(3 * experts, TILE)
    pairs = experts * slots
    dma = pltpu.SemaphoreType.DMA
    bf, f32 = (lambda *dims: pltpu.VMEM(dims, BF)), (lambda *dims: pltpu.VMEM(dims, F32))

    w_own = jnp.concatenate([w_qkv.reshape(D, 3 * width), w_out.T], axis=1)
    w_router_wide = jnp.pad(w_router, ((0, 0), (0, LANES - experts)))
    output, grad_tokens, w_sum, small, grad_in, grad_back = call(
        functools.partial(block_kernel, experts, tensor, images, group),
        (
            shape((own_rows, D)),
            shape((own_rows, D), F32),
            shape((D, 4 * width)),
            shape((small_rows, D), F32),
            shape((D, hidden), F32),
            shape((hidden, D), F32),
        ),
        scratch=(
            bf(tensor, D, 4 * width),
            bf(tensor, D, hidden),
            bf(tensor, hidden, D),
            f32(up(own_rows, TILE), D),
            f32(rows, D),
            f32(rows, D),
            f32(rows, LANES),
            f32(experts, rows),
            bf(tensor, rows, 3 * width),
            bf(images, heads, SP, SP),
            bf(tensor, rows, width),
            f32(rows, D),
            bf(tensor, rows, 3 * width),
            bf(experts, slots, D),
            bf(experts, slots, D),
            bf(experts, slots, D),
            bf(experts, slots, D),
            bf(experts, noise_rows, slots),
            bf(experts, noise_rows, slots),
            f32(pairs, LANES),
            bf(tensor, pairs, hidden),
            bf(tensor, max(pairs, 2 * D), hidden),
            bf(experts, slots, D),
            bf(experts, slots, D),
            bf(2, tensor - 1, 2, D, hidden),
            bf(tensor, D, 4 * width),
            bf(experts, tensor, piece, 4 * width),
            bf(tensor, piece, 4 * width),
            bf(tensor, piece, 4 * width),
            f32(small_rows, D),
            f32(experts, small_rows, D),
            f32(small_rows, D),
            f32(tensor, small_rows, D),
            dma((3,)),
            dma((2, tensor)),
            dma((2, tensor, experts)),
            dma((2, 2, tensor - 1)),
            dma((2, 2, tensor - 1)),
            dma((2, experts)),
            dma((2, experts)),
            dma((2, experts)),
            dma((2, experts)),
            dma((2, experts)),
            dma((2, tensor - 1, 2)),
            dma((2, tensor - 1, 2)),
            dma((2, tensor, experts)),
            dma((2, tensor)),
            dma((2, experts)),
            dma((2, experts)),
            dma((2, tensor)),
        ),
        far_in=(7, 8, 9),
        collective_id=0,
        has_side_effects=True,
    )(
        routes, tokens, cotangent, noise, norm1_gain.reshape(1, D), norm2_gain.reshape(1, D),
        w_router_wide, w_own, w_in[0], w_back[0],
    )
    w_sum = w_sum.astype(F32)
    return (
        output,
        grad_tokens,
        small[experts],
        w_sum[:, : 3 * width].reshape(D, 3, width),
        w_sum[:, 3 * width :].T,
        small[experts + 1],
        small[:experts].T,
        grad_in[None],
        grad_back[None],
    )


def solution(mesh):
    rows = P(("expert", "tensor"), None)
    placed = (
        rows,
        P(),
        P(None, None, "tensor"),
        P("tensor", None),
        P(),
        P(),
        rows,
        rows,
        P("expert", None, "tensor"),
        P("expert", "tensor", None),
        rows,
    )
    return jax.shard_map(
        per_device,
        mesh=mesh,
        in_specs=placed,
        out_specs=(
            rows,
            rows,
            P(),
            P(None, None, "tensor"),
            P("tensor", None),
            P(),
            P(),
            P("expert", None, "tensor"),
            P("expert", "tensor", None),
        ),
        check_vma=False,
    )
```

time: 253 us -> 220 us (0.87); the launches traced: 250 us -> 220 us
  Pallas kernels: 229 us -> 204 us
  local copies, waits for them, and re-layouts: 16.8 us -> 14.2 us
    pallas_call x3 -> x1, Pallas kernels: 229 us -> 204 us  [run(): pl.pallas_call(body, out_shape=out_shape, in_specs=[spec(place, far_in, p...]
    reshape x7 -> x0, local copies, waits for them, and re-layouts: 2.89 us -> none  [the longest x2 1.8 us: own(): a.reshape(images, SP, a.shape[1])[:, :SEQ].reshape(own_rows, a.shape[1])]
    unnamed x26 -> x29, local copies, waits for them, and re-layouts: 6.91 us -> 9.24 us
where the time goes in v4:
time: 220 us
  Pallas kernels  204 us (93%)
  local copies, waits for them, and re-layouts  14.2 us (6%)
    pallas_call x1, Pallas kernels, run(): pl.pallas_call(body, out_shape=out_shape, in_specs=[spec(place, far_in, p...  204 us
    unnamed x29, local copies, waits for them, and re-layouts  9.24 us

profile of v4, /device:TPU:0, one launch (start us, length us, event | category | flops | bytes accessed | tf_op | source)
XLA Modules:
  0.0 219.6 jit_solution(1002336753064154586)
XLA Ops:
  0.6 0.0 copy-start.7
  0.7 0.0 copy-start.6
  0.7 1.0 copy.29
  1.7 0.0 copy-done.7
  1.7 0.0 copy-start.5
  1.7 0.2 copy.27
  1.9 0.7 pad.4.w_router_ref
  2.6 0.0 copy-done.6
  2.6 0.0 copy-start.8
  2.6 0.8 copy.32.noise_ref
  3.4 0.0 copy-done.8
  3.4 0.8 copy.31.routes_ref
  4.2 0.0 copy-done.5
  4.2 0.2 copy.28
  4.4 0.2 copy.30
  4.6 0.8 pad_maximum_fusion.w_own_ref
  5.5 203.7 %shard_map.178 = (bf16[394,512]{1,0:T(8,128)(2,1)}, f32[394,512]{1,0:T(8,128)}, bf16[512,512]{1,0:T(8,128)(2,1)}, f32[16,512]{1,0:T(8,128)}, f32[512,512]{1,0:T(8,128)}, /*index=5*/f32[512,512]{1,0:T(8,128)}) custom-call(s32[394,2]{1,0:T(8,128)} %copy.31.routes_ref, bf16[394,512]{1,0:T(8,128)(2,1)} %tokens_ref.1, bf16[394,512]{1,0:T(8,128)(2,1)} %cotangent_ref.1, ...), custom_call_target="tpu_custom_call" | custom-call | tf_op jit(solution)/shard_map/pallas_call | solution.py:49
  209.1 1.4 fusion
  210.5 1.3 slice_bitcast_fusion.1
  211.8 1.0 slice.20
  212.9 0.3 copy.33
  213.2 0.0 copy-start
  213.2 1.1 copy.34
  214.3 0.0 copy-done
  214.3 0.0 copy-start.4
  214.3 0.1 convert_element_type.5
  214.4 0.0 copy-start.3
  214.5 0.8 copy.35
  215.3 0.0 copy-done.4
  215.3 0.0 copy-start.2
  215.3 0.8 copy.40
  216.1 0.0 copy-done.3
  216.1 0.9 copy.41
  217.0 0.0 copy-done.2
  217.0 0.0 copy-start.1
  217.0 1.0 copy.42
  218.0 0.6 copy-done.1
  218.6 1.0 copy.43
  (1 shorter events, 0.0 us)
Async XLA Ops:
  0.6 1.1 copy-start.7
  0.7 1.9 copy-start.6
  1.7 2.5 %copy-start.5 = (bf16[512,3,128]{2,0,1:T(8,128)(2,1)S(1)}, bf16[512,3,128]{2,0,1:T(8,128)(2,1)}, u32[]{:S(2)}) copy-start(bf16[512,3,128]{2,0,1:T(8,128)(2,1)} %param.13) | copy-start | bytes 1179652
  2.6 0.8 copy-start.8
  213.2 1.2 copy-start
  214.3 1.0 copy-start.4
  214.4 1.7 copy-start.3
  215.3 1.6 copy-start.2
  217.0 1.6 copy-start.1

commit v5 on v4

--- a/solution.py
+++ b/solution.py
@@ -9,6 +9,7 @@
 
 D = 512
 HD = 64
+CORES = 2
 TOP = 2
 SEQ = 197
 LANES = 128
@@ -94,13 +95,13 @@
 
 
 def take_rows(slots, in_ref, experts):
-    count = in_ref.shape[1]
+    count = in_ref.shape[0] // experts
     rows = slots.shape[0]
     place = ids((rows, count), 1).astype(F32)
     total = None
     for e in range(experts):
         pick = (place == slots[:, e : e + 1]).astype(F32).astype(BF)
-        part = mm(pick, in_ref[e])
+        part = mm(pick, in_ref[e * count : (e + 1) * count, :])
         total = part if total is None else total + part
     return total
 
@@ -223,11 +224,8 @@
             "tensor", self.me + toward,
         )
 
-    def start_first(self, way, step):
-        for part in (0, 1):
-            pl.when(self.hops(way) == 0)(
-                lambda part=part: self.copy(way, step, part, True).start()
-            )
+    def start_first(self, way, step, part):
+        pl.when(self.hops(way) == 0)(lambda: self.copy(way, step, part, True).start())
 
     def middle(self, way, step):
         hops = self.hops(way)
@@ -281,27 +279,42 @@
     w_own_ref, w_in_own, w_back_own,
     output_ref, tokens_grad_ref, w_sum_ref, small_sum_ref, in_grad_ref, back_grad_ref,
     w_ref, w_in_all, w_back_all, narrow, x_ref, cot_ref, rows_ref, lanes_ref,
-    qkv_ref, attend_ref, mixed_ref, residual_ref, d_qkv_ref,
+    qkv_ref, attend_ref, mixed_ref, residual_ref,
     send_ref, routed_ref, early_send, early_ref, noise_send, noise_all, router_ref,
-    hidden_ref, slope_ref, back_ref, out_ref, held,
-    w_grad_ref, pieces, piece_send, piece_line,
+    hidden_ref, slope_ref, back_ref, held,
+    wide_ref, back_grads, pair_ref, pieces, piece_send, piece_line,
     small_ref, small_plane, small_line_send, small_line,
-    own_sem, first_sems, plane_sems, in_sems, in_back_sems, route_sems, early_sems, noise_sems,
-    back_sems, out_sems, sum_send, sum_recv, w_sems, piece_sems, final_sems,
+    own_sem, first_sems, plane_sems, pair_sems, in_sems, in_back_sems, route_sems, early_sems, noise_sems,
+    back_sems, out_sems, sum_send, sum_recv, w_pair_sems, w_sems, piece_sems, final_sems,
     small_sems, small_line_sems,
 ):
     own_rows = tokens_ref.shape[0]
     wide = w_own_ref.shape[1]
     width = wide // 4
     heads = width // HD
-    slots = send_ref.shape[1]
+    slots = noise_send.shape[2]
+    pairs = experts * slots
     parts = w_in_all.shape[0]
     chunk = group * slots
     me_e, me_t = lax.axis_index("expert"), lax.axis_index("tensor")
     piece = D // experts
 
+    chips = experts // CORES
+    core = lax.rem(me_e, CORES)
+    half = chips * piece
+
     def rows_at(e):
-        return pl.ds(pl.multiple_of(e * piece, piece), piece)
+        at = lax.rem(e, CORES) * chips + e // CORES
+        return pl.ds(pl.multiple_of(at * piece, piece), piece)
+
+    def half_at(which):
+        return pl.ds(pl.multiple_of(which * half, half), half)
+
+    def chip_after(k):
+        return lax.rem(me_e + CORES * k, experts)
+
+    def chip_place(k, arriving):
+        return lax.rem(me_e + experts - CORES * k, experts) if arriving else me_e
 
     mine = rows_at(me_e)
 
@@ -329,33 +342,67 @@
             w_own_ref.at[mine], lambda owner: w_ref.at[owner, mine], first_sems, d, arriving
         )
 
-    def plane_copy(z, d, arriving):
+    def plane_copy(z, k, arriving):
         owner = lax.rem(me_t + tensor - z, tensor)
-        block = w_ref.at[owner, rows_at(place(d, arriving))]
+        block = w_ref.at[owner, rows_at(chip_place(k, arriving))]
         return remote(
-            block, block, plane_sems.at[0, z, d], plane_sems.at[1, z, d], "expert", after(d)
+            block, block, plane_sems.at[0, z, k], plane_sems.at[1, z, k], "expert", chip_after(k)
+        )
+
+    def pair_copy(z, arriving):
+        owner = lax.rem(me_t + tensor - z, tensor)
+        block = w_ref.at[owner, half_at(CORES - 1 - core if arriving else core)]
+        return remote(
+            block, block, pair_sems.at[0, z], pair_sems.at[1, z], "expert",
+            me_e + CORES - 1 - 2 * core,
+        )
+
+    def slot_rows(e):
+        return pl.ds(pl.multiple_of(e * slots, slots), slots)
+
+    def flat_copy(src, dst, sems, d, arriving):
+        return remote(
+            src.at[slot_rows(after(d))], dst.at[slot_rows(place(d, arriving))],
+            sems.at[0, d], sems.at[1, d], "expert", after(d),
         )
 
     def route_copy(d, arriving):
-        return swap_copy(send_ref, routed_ref, route_sems, d, arriving)
+        return flat_copy(send_ref, routed_ref, route_sems, d, arriving)
 
     def early_copy(d, arriving):
-        return swap_copy(early_send, early_ref, early_sems, d, arriving)
+        return flat_copy(early_send, early_ref, early_sems, d, arriving)
 
     def noise_copy(d, arriving):
         return swap_copy(noise_send, noise_all, noise_sems, d, arriving)
 
     def back_copy(d, arriving):
-        return swap_copy(early_send, back_ref, back_sems, d, arriving)
+        return flat_copy(early_send, back_ref, back_sems, d, arriving)
 
     def out_copy(d, arriving):
-        return swap_copy(send_ref, out_ref, out_sems, d, arriving)
-
-    def w_copy(t, d, arriving):
+        return flat_copy(send_ref, routed_ref, out_sems, d, arriving)
+
+    def columns(t):
+        return slice(t * wide, (t + 1) * wide)
+
+    def w_pair_copy(t):
         return remote(
-            w_grad_ref.at[t, rows_at(after(d))], pieces.at[place(d, arriving), t],
-            w_sems.at[0, t, d], w_sems.at[1, t, d], "expert", after(d),
-        )
+            wide_ref.at[half_at(CORES - 1 - core), columns(t)], pair_ref.at[t],
+            w_pair_sems.at[0, t], w_pair_sems.at[1, t], "expert", me_e + CORES - 1 - 2 * core,
+        )
+
+    def w_copy(t, k, arriving):
+        return remote(
+            wide_ref.at[rows_at(chip_after(k)), columns(t)],
+            pieces.at[chip_place(k, arriving) // CORES, t],
+            w_sems.at[0, t, k], w_sems.at[1, t, k], "expert", chip_after(k),
+        )
+
+    def share_pair_sum(t):
+        w_pair_copy(t).wait_recv()
+        ours = half_at(core)
+        pair_sum = wide_ref[ours, columns(t)].astype(F32) + pair_ref[t].astype(F32)
+        wide_ref[ours, columns(t)] = pair_sum.astype(BF)
+        each(chips, lambda k: w_copy(t, k, False).start())
 
     def piece_copy(d, arriving):
         src = piece_send.at[lax.rem(me_t + d, tensor)]
@@ -423,7 +470,7 @@
 
     def forward_piece(z):
         first_copy(z, True).wait_recv()
-        each(experts, lambda d: plane_copy(z, d, False).start())
+        each(chips, lambda k: plane_copy(z, k, False).start())
 
     each(tensor, forward_piece)
     for d in range(1, experts + 1):
@@ -432,12 +479,12 @@
         rows_of_e = mm(pick, cot_low).astype(BF)
         noise_of_e = mm(noise, pick, NT).astype(BF)
         if d < experts:
-            early_send[e] = rows_of_e
+            early_send[slot_rows(e), :] = rows_of_e
             noise_send[e] = noise_of_e
             early_copy(d, False).start()
             noise_copy(d, False).start()
         else:
-            early_ref[e] = rows_of_e
+            early_ref[slot_rows(e), :] = rows_of_e
             noise_all[e] = noise_of_e
     spread(tokens_ref[...].astype(F32), x_ref)
     x = x_ref[...]
@@ -446,9 +493,14 @@
     line_in.arrive(0)
     if tensor > 2:
         line_in.start(1)
-    line_back.start(0)
+
+    def forward_half(z):
+        each(chips, lambda k: plane_copy(z, k, True).wait_recv())
+        pair_copy(z, False).start()
+
+    each(tensor, forward_half)
     keep[0].wait()
-    each(tensor, lambda z: each(experts, lambda d: plane_copy(z, d, True).wait_recv()))
+    each(tensor, lambda z: pair_copy(z, True).wait_recv())
 
     lane = ids((SP, width), 1) // HD
     live = ids((SP, SP), 1) < SEQ
@@ -470,9 +522,6 @@
                 part = mm(attend, v)
                 mixed = part if mixed is None else jnp.where(lane == j, part, mixed)
             mixed_ref[t, rows, :] = mixed.astype(BF)
-        if t == tensor // 2 - 1 and tensor > 3:
-            line_in.arrive(1)
-            line_in.start(2)
     residual = x
     for t in range(tensor):
         residual = residual + mm(mixed_ref[t], w_ref[t, :, 3 * width : wide], NT)
@@ -483,21 +532,18 @@
         e = after(d)
         rows_of_e = mm(pick_of(e), normed2).astype(BF)
         if d < experts:
-            send_ref[e] = rows_of_e
+            send_ref[slot_rows(e), :] = rows_of_e
             route_copy(d, False).start()
         else:
-            routed_ref[e] = rows_of_e
-    done_in, done_back = (2 if tensor > 3 else 1), 0
-    for step in range(tensor - 1):
-        if step >= done_in:
-            line_in.arrive(step)
-            if step + 1 < tensor - 1:
-                line_in.start(step + 1)
-        if step < tensor - 2:
-            line_back.arrive(step)
-            line_back.start(step + 1)
-    if done_in > tensor - 2:
-        line_in.arrive(tensor - 2)
+            routed_ref[slot_rows(e), :] = rows_of_e
+    for step in range(1, tensor - 1):
+        line_in.arrive(step)
+        if step + 1 < tensor - 1:
+            line_in.start(step + 1)
+        if step == max(1, tensor - 3):
+            line_back.start(0)
+    if tensor == 2:
+        line_back.start(0)
     keep[1].wait()
 
     fold_from, fold_to = ids((noise_all.shape[1], LANES), 0), ids((noise_all.shape[1], LANES), 1)
@@ -510,11 +556,6 @@
     def block_rows(at):
         return pl.ds(pl.multiple_of(at * chunk, chunk), chunk)
 
-    def all_slots(ref, at):
-        if group == 1:
-            return ref[at]
-        return ref[pl.ds(at * group, group)].reshape(chunk, ref.shape[2])
-
     def hidden_units(turn, _):
         at = lax.rem(me_e // group + groups - turn, groups)
         for k in range(group):
@@ -526,13 +567,22 @@
                 early_copy(d, True).wait_recv()
                 noise_copy(d, True).wait_recv()
 
+        @pl.when(turn == groups // 2)
+        def _():
+            for step in range(0, tensor - 3):
+                line_back.arrive(step)
+                line_back.start(step + 1)
+
         rows = block_rows(at)
-        came = all_slots(routed_ref, at)
+        came = routed_ref[rows, :]
         added = [mm(noise_all[at * group + k], fold, TN) for k in range(group)]
         added = added[0] if group == 1 else jnp.concatenate(added, axis=0)
         logits = jnp.where(expert_lane < experts, mm(came, w_router_ref[...]) + added, -1e30)
         power = jnp.exp(logits - jnp.max(logits, -1, keepdims=True))
-        router_ref[rows, :] = power / jnp.sum(power, -1, keepdims=True)
+        router = power / jnp.sum(power, -1, keepdims=True)
+        router_ref[rows, :] = router
+        gate = jnp.sum(jnp.where(expert_lane == me_e, router, 0.0), -1, keepdims=True)
+        early_ref[rows, :] = (gate * early_ref[rows, :].astype(F32)).astype(BF)
         for f in range(parts):
             pre = mm(came, w_in_all[f])
             normal, density = gelu_parts(pre)
@@ -542,63 +592,8 @@
 
     lax.fori_loop(0, groups, hidden_units, 0)
 
-    line_back.arrive(tensor - 2)
-    keep[2].wait()
-
-    def early_sent(d):
-        early_copy(d, False).wait_send()
-        route_copy(d, False).wait_send()
-
-    each(experts, early_sent)
-
-    small_ref[...] = jnp.zeros_like(small_ref)
-
-    def expert_rows(turn, _):
-        at = lax.rem(me_e // group + groups - turn, groups)
-        rows = block_rows(at)
-        came = all_slots(routed_ref, at)
-        router = router_ref[rows, :]
-        own_lane = expert_lane == me_e
-        gate = jnp.sum(jnp.where(own_lane, router, 0.0), -1, keepdims=True)
-        cot = all_slots(early_ref, at).astype(F32)
-        d_exp = (gate * cot).astype(BF)
-        out = jnp.zeros((chunk, D), F32)
-        back = jnp.zeros((chunk, D), F32)
-        for f in range(parts):
-            w_b = w_back_all[f]
-            out = out + mm(hidden_ref[f, rows, :], w_b)
-            d_pre = (mm(d_exp, w_b, NT) * slope_ref[f, rows, :].astype(F32)).astype(BF)
-            slope_ref[f, rows, :] = d_pre
-            back = back + mm(d_pre, w_in_all[f], NT)
-        out = out.astype(BF).astype(F32)
-        d_gate = jnp.sum(cot * out, -1, keepdims=True)
-        d_logits = (d_gate * gate * (own_lane.astype(F32) - router)).astype(BF)
-        back = (back + mm(d_logits, w_router_ref[...], NT)).astype(BF)
-        out = (gate * out).astype(BF)
-        small_ref[0:experts, :] += mm(d_logits, came, TN)[0:experts]
-        for k in range(group):
-            e = at * group + k
-            part = slice(k * slots, (k + 1) * slots)
-            early_ref[e] = d_exp[part]
-            d = lax.rem(e + experts - me_e, experts)
-
-            @pl.when(d > 0)
-            def _(d=d, e=e, part=part):
-                send_ref[e] = out[part]
-                early_send[e] = back[part]
-                back_copy(d, False).start()
-
-            @pl.when(d == 0)
-            def _(e=e, part=part):
-                out_ref[e] = out[part]
-                back_ref[e] = back[part]
-
-        return 0
-
-    lax.fori_loop(0, groups, expert_rows, 0)
-
     def grads_at(block, part):
-        return slope_ref.at[block, part * D : (part + 1) * D]
+        return back_grads.at[block] if part else slope_ref.at[block, 0:D]
 
     sums = Sums(tensor, grads_at, held, sum_send, sum_recv)
     order = []
@@ -606,21 +601,111 @@
         for f in (tensor - 1 - step, step):
             if f not in order:
                 order.append(f)
-    for f in order:
-        for part, left, right in ((0, routed_ref, slope_ref), (1, early_ref, hidden_ref)):
-            in_grad_ref[...] = jnp.zeros_like(in_grad_ref)
-
-            def add_in(at, _, f=f, left=left, right=right):
-                in_grad_ref[...] += mm(all_slots(left, at), right[f, block_rows(at), :], TN)
-                return 0
-
-            lax.fori_loop(0, groups, add_in, 0)
-            grads_at(f, part)[...] = in_grad_ref[...].astype(BF)
-        for step in range(tensor - 1):
-            for way, block in ((0, tensor - 1 - step), (1, step)):
-                if block == f:
-                    sums.start_first(way, step)
-    each(experts, lambda d: out_copy(d, False).start())
+
+    def turn_rows(ref):
+        def body(at, _):
+            rows = pl.ds(pl.multiple_of(at * LANES, LANES), LANES)
+            wide_ref[:, rows] = ref[rows, :].T
+            return 0
+
+        lax.fori_loop(0, pairs // LANES, body, 0)
+
+    def weight_grads(part, right):
+        for f in order:
+            block = mm(wide_ref[:, 0:pairs], right[f, 0:pairs, :]).astype(BF)
+            grads_at(f, part)[...] = block
+            for step in range(tensor - 1):
+                for way, to in ((0, tensor - 1 - step), (1, step)):
+                    if to == f:
+                        sums.start_first(way, step, part)
+
+    turn_rows(early_ref)
+    weight_grads(1, hidden_ref)
+    turn_rows(routed_ref)
+
+    for step in range(max(tensor - 3, 0), tensor - 2):
+        line_back.arrive(step)
+        line_back.start(step + 1)
+    keep[2].wait()
+
+    def early_sent(d):
+        early_copy(d, False).wait_send()
+        route_copy(d, False).wait_send()
+
+    each(experts, early_sent)
+
+    small_ref[...] = jnp.zeros_like(small_ref)
+
+    def near(k):
+        def from_low(me):
+            below = (me - k + tensor) // tensor
+            return below * (me - k) + (1 - below) * k
+
+        low = 1 - (2 * me_t) // tensor
+        mirrored = tensor - 1 - from_low(tensor - 1 - me_t)
+        return low * from_low(me_t) + (1 - low) * mirrored
+
+    def unit_part(k, rows):
+        f = near(k)
+        w_b = w_back_all[f]
+        out = mm(hidden_ref[f, rows, :], w_b)
+        d_pre = (mm(early_ref[rows, :], w_b, NT) * slope_ref[f, rows, :].astype(F32)).astype(BF)
+        slope_ref[f, rows, :] = d_pre
+        return out, mm(d_pre, w_in_all[f], NT)
+
+    def near_rows(at, _):
+        rows = block_rows(at)
+        out, back = unit_part(0, rows)
+        for k in range(1, tensor - 1):
+            more_out, more_back = unit_part(k, rows)
+            out, back = out + more_out, back + more_back
+        send_ref[rows, :] = out.astype(BF)
+        early_send[rows, :] = back.astype(BF)
+        return 0
+
+    lax.fori_loop(0, groups, near_rows, 0)
+    line_steps = [(step, part) for part in (1, 0) for step in range(1, tensor - 1)]
+
+    def next_sum():
+        if line_steps:
+            sums.forward(*line_steps.pop(0))
+
+    next_sum()
+    line_back.arrive(tensor - 2)
+
+    def far_rows(turn, _):
+        at = lax.rem(me_e // group + groups - turn, groups)
+        rows = block_rows(at)
+        router = router_ref[rows, :]
+        own_lane = expert_lane == me_e
+        gate = jnp.sum(jnp.where(own_lane, router, 0.0), -1, keepdims=True)
+        out, back = unit_part(tensor - 1, rows)
+        out = (out + send_ref[rows, :].astype(F32)).astype(BF).astype(F32)
+        back = back + early_send[rows, :].astype(F32)
+        d_gate = jnp.sum(early_ref[rows, :].astype(F32) * out, -1, keepdims=True)
+        d_logits = (d_gate * (own_lane.astype(F32) - router)).astype(BF)
+        early_send[rows, :] = (back + mm(d_logits, w_router_ref[...], NT)).astype(BF)
+        send_ref[rows, :] = (gate * out).astype(BF)
+        small_ref[0:experts, :] += mm(d_logits, routed_ref[rows, :], TN)[0:experts]
+        for k in range(group):
+            e = at * group + k
+            d = lax.rem(e + experts - me_e, experts)
+
+            @pl.when(d > 0)
+            def _(d=d):
+                back_copy(d, False).start()
+
+            @pl.when(d == 0)
+            def _(e=e):
+                back_ref[slot_rows(e), :] = early_send[slot_rows(e), :]
+                routed_ref[slot_rows(e), :] = send_ref[slot_rows(e), :]
+
+        return 0
+
+    lax.fori_loop(0, groups, far_rows, 0)
+
+    weight_grads(0, slope_ref)
+    next_sum()
 
     each(experts, lambda d: back_copy(d, True).wait_recv())
     slots_of = rows_ref[:, 0:experts]
@@ -632,11 +717,10 @@
     cot_ref[...] = d_residual
     d_attention = d_residual.astype(BF)
     scaling = HD ** (-0.5)
-    line_steps = [(step, part) for step in range(1, tensor - 1) for part in (0, 1)]
     unit1, inverse1 = unit_norm(x_ref[...])
     normed1 = (unit1 * gain1_ref[...]).astype(BF)
     for t in range(tensor):
-        w_grad_ref[t, :, 3 * width : wide] = mm(d_attention, mixed_ref[t], TN).astype(BF)
+        wide_ref[:, t * wide + 3 * width : (t + 1) * wide] = mm(d_attention, mixed_ref[t], TN).astype(BF)
         d_mixed = mm(d_attention, w_ref[t, :, 3 * width : wide]).astype(BF)
         for i in range(images):
             rows = slice(i * SP, (i + 1) * SP)
@@ -660,33 +744,32 @@
                 dq = part_q if dq is None else jnp.where(own, part_q, dq)
                 dk = part_k if dk is None else dk + part_k
                 dv = part_v if dv is None else dv + part_v
-            d_qkv_ref[t, rows, 0:width] = dq.astype(BF)
-            d_qkv_ref[t, rows, width : 2 * width] = dk.astype(BF)
-            d_qkv_ref[t, rows, 2 * width : 3 * width] = dv.astype(BF)
-        w_grad_ref[t, :, 0 : 3 * width] = mm(normed1, d_qkv_ref[t], TN).astype(BF)
-        each(experts, lambda d, t=t: w_copy(t, d, False).start())
-        if t in (0, tensor // 2) and line_steps:
-            sums.forward(*line_steps.pop(0))
+            qkv_ref[t, rows, 0:width] = dq.astype(BF)
+            qkv_ref[t, rows, width : 2 * width] = dk.astype(BF)
+            qkv_ref[t, rows, 2 * width : 3 * width] = dv.astype(BF)
+        wide_ref[:, t * wide : t * wide + 3 * width] = mm(normed1, qkv_ref[t], TN).astype(BF)
+        w_pair_copy(t).start()
+        if t > 0:
+            share_pair_sum(t - 1)
+    share_pair_sum(tensor - 1)
+    next_sum()
     d_normed1 = None
     for t in range(tensor):
-        part = mm(d_qkv_ref[t], w_ref[t, :, 0 : 3 * width], NT)
+        part = mm(qkv_ref[t], w_ref[t, :, 0 : 3 * width], NT)
         d_normed1 = part if d_normed1 is None else d_normed1 + part
     d_rows, norm1 = norm_back(d_normed1, unit1, inverse1, gain1_ref[...])
     small_ref[experts : experts + 1, :] = norm1
     each(experts, lambda d: small_copy(d, False).start())
+    each(experts, lambda d: out_copy(d, False).start())
     small_plane[me_e] = small_ref[...]
     tokens_grad_ref[...] = compact(cot_ref[...] + d_rows)
 
-    each(experts, lambda d: out_copy(d, True).wait_recv())
-    output = residual_ref[...] + take_rows(slots_of, out_ref, experts)
-    output_ref[...] = compact(output).astype(BF)
-
     for t in range(tensor):
-        pieces[me_e, t] = w_grad_ref[t, mine, :]
+        pieces[me_e // CORES, t] = wide_ref[mine, columns(t)]
     for t in range(tensor):
-        each(experts, lambda d, t=t: w_copy(t, d, True).wait_recv())
+        each(chips, lambda k, t=t: w_copy(t, k, True).wait_recv())
         total = pieces[0, t].astype(F32)
-        for e in range(1, experts):
+        for e in range(1, chips):
             total = total + pieces[e, t].astype(F32)
         piece_send[t] = total.astype(BF)
     each(tensor, lambda d: piece_copy(d, False).start())
@@ -698,16 +781,18 @@
     small_line_send[...] = total
     each(tensor, lambda d: small_line_copy(d, False).start())
     small_line[me_t] = total
-    if line_steps:
-        sums.forward(*line_steps.pop(0))
     each(tensor, lambda d: piece_copy(d, True).wait_recv())
     total = piece_line[0].astype(F32)
     for t in range(1, tensor):
         total = total + piece_line[t].astype(F32)
     w_sum_ref[mine, :] = total.astype(BF)
     each(experts, lambda d: final_copy(d, False).start())
-    for step, part in line_steps:
-        sums.forward(step, part)
+    while line_steps:
+        next_sum()
+
+    each(experts, lambda d: out_copy(d, True).wait_recv())
+    output = residual_ref[...] + take_rows(slots_of, routed_ref, experts)
+    output_ref[...] = compact(output).astype(BF)
 
     each(tensor, lambda d: small_line_copy(d, True).wait_recv())
     total = small_line[0]
@@ -723,9 +808,9 @@
             came = held[way, tensor - 2, part].astype(F32)
             total = total + jnp.where(sums.hops(way) >= 1, came, jnp.zeros_like(came))
         if part == 0:
-            in_grad_ref[...] = total
+            in_grad_ref[...] = total.astype(BF)
         else:
-            back_grad_ref[...] = total.T
+            back_grad_ref[...] = total.T.astype(BF)
 
     sums.finish()
     line_in.finish()
@@ -735,8 +820,6 @@
         noise_copy(d, False).wait_send()
         back_copy(d, False).wait_send()
         out_copy(d, False).wait_send()
-        for t in range(tensor):
-            w_copy(t, d, False).wait_send()
         final_copy(d, False).wait_send()
         small_copy(d, False).wait_send()
 
@@ -746,9 +829,13 @@
         first_copy(d, False).wait_send()
         piece_copy(d, False).wait_send()
         small_line_copy(d, False).wait_send()
-        each(experts, lambda k: plane_copy(d, k, False).wait_send())
+        pair_copy(d, False).wait_send()
+        each(chips, lambda k: plane_copy(d, k, False).wait_send())
 
     each(tensor, sent_line)
+    for t in range(tensor):
+        w_pair_copy(t).wait_send()
+        each(chips, lambda k, t=t: w_copy(t, k, False).wait_send())
 
 
 def per_device(
@@ -761,7 +848,7 @@
     rows = images * SP
     capacity = (2 * own_rows * TOP + experts - 1) // experts
     slots = up(capacity, TILE)
-    group = max(1, 128 // slots)
+    group = max(g for g in range(1, experts + 1) if experts % g == 0 and g * slots <= 2 * SP)
     width = w_out.shape[0]
     hidden = w_in.shape[2]
     heads = tensor * width // HD
@@ -781,8 +868,8 @@
             shape((own_rows, D), F32),
             shape((D, 4 * width)),
             shape((small_rows, D), F32),
-            shape((D, hidden), F32),
-            shape((hidden, D), F32),
+            shape((D, hidden)),
+            shape((hidden, D)),
         ),
         scratch=(
             bf(tensor, D, 4 * width),
@@ -797,21 +884,21 @@
             bf(images, heads, SP, SP),
             bf(tensor, rows, width),
             f32(rows, D),
-            bf(tensor, rows, 3 * width),
-            bf(experts, slots, D),
-            bf(experts, slots, D),
-            bf(experts, slots, D),
-            bf(experts, slots, D),
+            bf(pairs, D),
+            bf(pairs, D),
+            bf(pairs, D),
+            bf(pairs, D),
             bf(experts, noise_rows, slots),
             bf(experts, noise_rows, slots),
             f32(pairs, LANES),
             bf(tensor, pairs, hidden),
-            bf(tensor, max(pairs, 2 * D), hidden),
-            bf(experts, slots, D),
-            bf(experts, slots, D),
+            bf(tensor, max(pairs, D), hidden),
+            bf(pairs, D),
             bf(2, tensor - 1, 2, D, hidden),
-            bf(tensor, D, 4 * width),
-            bf(experts, tensor, piece, 4 * width),
+            bf(D, max(pairs, tensor * 4 * width)),
+            bf(tensor, D, hidden),
+            bf(tensor, D // CORES, 4 * width),
+            bf(experts // CORES, tensor, piece, 4 * width),
             bf(tensor, piece, 4 * width),
             bf(tensor, piece, 4 * width),
             f32(small_rows, D),
@@ -820,7 +907,8 @@
             f32(tensor, small_rows, D),
             dma((3,)),
             dma((2, tensor)),
-            dma((2, tensor, experts)),
+            dma((2, tensor, experts // CORES)),
+            dma((2, tensor)),
             dma((2, 2, tensor - 1)),
             dma((2, 2, tensor - 1)),
             dma((2, experts)),
@@ -830,7 +918,8 @@
             dma((2, experts)),
             dma((2, tensor - 1, 2)),
             dma((2, tensor - 1, 2)),
-            dma((2, tensor, experts)),
+            dma((2, tensor)),
+            dma((2, tensor, experts // CORES)),
             dma((2, tensor)),
             dma((2, experts)),
             dma((2, experts)),
@@ -852,8 +941,8 @@
         w_sum[:, 3 * width :].T,
         small[experts + 1],
         small[:experts].T,
-        grad_in[None],
-        grad_back[None],
+        grad_in.astype(F32)[None],
+        grad_back.astype(F32)[None],
     )
 
 

time: 220 us -> 177 us (0.80)
  Pallas kernels: 204 us -> 160 us
    pallas_call x1, Pallas kernels: 204 us -> 160 us  [run(): pl.pallas_call(body, out_shape=out_shape, in_specs=[spec(place, far_in, p...]
    unnamed x29 -> x27, local copies, waits for them, and re-layouts: 9.24 us -> 7.6 us
where the time goes in v5:
time: 177 us; the launch traced here: 176 us
  Pallas kernels  160 us (90%)
  local copies, waits for them, and re-layouts  12.6 us (7%)
  other arithmetic  2.57 us (1%)
    pallas_call x1, Pallas kernels, run(): pl.pallas_call(body, out_shape=out_shape, in_specs=[spec(place, far_in, p...  160 us
    unnamed x27, local copies, waits for them, and re-layouts  7.6 us

profile of v5, /device:TPU:0, one launch (start us, length us, event | category | flops | bytes accessed | tf_op | source)
XLA Modules:
  0.0 176.1 jit_solution(8575437802817154293)
XLA Ops:
  0.6 0.0 copy-start.7
  0.7 0.0 copy-start.6
  0.7 1.0 copy.29
  1.7 0.0 copy-done.7
  1.7 0.0 copy-start.5
  1.7 0.2 copy.27
  1.9 0.7 pad.4.w_router_ref
  2.6 0.0 copy-done.6
  2.6 0.0 copy-start.8
  2.6 0.8 copy.32.noise_ref
  3.4 0.0 copy-done.8
  3.4 0.8 copy.31.routes_ref
  4.2 0.0 copy-done.5
  4.2 0.2 copy.28
  4.4 0.2 copy.30
  4.6 0.8 pad_maximum_fusion.w_own_ref
  5.5 160.2 %shard_map.178 = (bf16[394,512]{1,0:T(8,128)(2,1)}, f32[394,512]{1,0:T(8,128)}, bf16[512,512]{1,0:T(8,128)(2,1)}, f32[16,512]{1,0:T(8,128)}, bf16[512,512]{1,0:T(8,128)(2,1)}, /*index=5*/bf16[512,512]{1,0:T(8,128)(2,1)}) custom-call(s32[394,2]{1,0:T(8,128)} %copy.31.routes_ref, bf16[394,512]{1,0:T(8,128)(2,1)} %tokens_ref.1, bf16[394,512]{1,0:T(8,128)(2,1)} %cotangent_ref.1, ...), custom_call_target="tpu_custom_call" | custom-call | tf_op jit(solution)/shard_map/pallas_call | solution.py:50
  165.7 1.4 fusion
  167.1 1.3 slice_bitcast_fusion.1
  168.4 1.0 slice.20
  169.4 0.3 copy.33
  169.7 0.0 copy-start
  169.7 1.1 copy.34
  170.9 0.0 copy-done
  170.9 0.1 convert_element_type.4
  171.0 0.0 copy-start.2
  171.0 0.0 copy-start.3
  171.1 0.8 copy.35
  171.9 0.1 copy-done.2
  172.0 0.3 copy-done.3
  172.3 0.0 copy-start.4
  172.3 1.6 bitcast_convert_fusion
  173.9 0.0 copy-start.1
  173.9 0.0 copy-done.4
  173.9 0.8 copy.38
  174.7 0.5 copy-done.1
  175.2 0.9 copy.39
  (1 shorter events, 0.0 us)
Async XLA Ops:
  0.6 1.1 copy-start.7
  0.7 1.9 %copy-start.6 = (f32[394,8]{0,1:T(8,128)S(1)}, f32[394,8]{0,1:T(8,128)}, u32[]{:S(2)}) copy-start(f32[394,8]{0,1:T(8,128)} %param.17) | copy-start | bytes 37828
  1.7 2.5 %copy-start.5 = (bf16[512,3,128]{2,0,1:T(8,128)(2,1)S(1)}, bf16[512,3,128]{2,0,1:T(8,128)(2,1)}, u32[]{:S(2)}) copy-start(bf16[512,3,128]{2,0,1:T(8,128)(2,1)} %param.13) | copy-start | bytes 1179652
  2.6 0.8 copy-start.8
  169.7 1.2 copy-start
  171.0 1.0 copy-start.2
  171.0 1.3 copy-start.3
  172.3 1.6 copy-start.4
  173.9 1.3 copy-start.1

commit v6 on v5

--- a/solution.py
+++ b/solution.py
@@ -85,12 +85,12 @@
     return lax.broadcasted_iota(jnp.int32, shape_of, dim)
 
 
-def slots_by_row(routes, experts):
-    rows = routes.shape[0]
-    which = ids((rows, experts), 1)
-    named = (routes[:, 0:1] == which) | (routes[:, 1:2] == which)
-    before = (ids((rows, rows), 1) < ids((rows, rows), 0)).astype(F32).astype(BF)
-    rank = mm(before, named.astype(F32).astype(BF))
+def slots_by_lane(routes, experts):
+    rows = routes.shape[1]
+    which = ids((experts, rows), 0).astype(F32)
+    named = (routes[0:1] == which) | (routes[1:2] == which)
+    before = (ids((rows, rows), 0) < ids((rows, rows), 1)).astype(F32).astype(BF)
+    rank = mm(named.astype(F32).astype(BF), before)
     return jnp.where(named, rank, -1.0)
 
 
@@ -275,10 +275,10 @@
 
 def block_kernel(
     experts, tensor, images, group,
-    routes_ref, tokens_ref, cotangent_ref, noise_ref, gain1_ref, gain2_ref, w_router_ref,
-    w_own_ref, w_in_own, w_back_own,
+    routes_ref, tokens_ref, cotangent_ref, noise_ref, gain1_ref, gain2_ref, router_own,
+    w_out_own, w_qkv_own, w_in_own, w_back_own,
     output_ref, tokens_grad_ref, w_sum_ref, small_sum_ref, in_grad_ref, back_grad_ref,
-    w_ref, w_in_all, w_back_all, narrow, x_ref, cot_ref, rows_ref, lanes_ref,
+    w_ref, w_router_ref, w_in_all, w_back_all, narrow, x_ref, cot_ref, rows_ref, lanes_ref,
     qkv_ref, attend_ref, mixed_ref, residual_ref,
     send_ref, routed_ref, early_send, early_ref, noise_send, noise_all, router_ref,
     hidden_ref, slope_ref, back_ref, held,
@@ -289,8 +289,8 @@
     small_sems, small_line_sems,
 ):
     own_rows = tokens_ref.shape[0]
-    wide = w_own_ref.shape[1]
-    width = wide // 4
+    width = w_out_own.shape[0]
+    wide = 4 * width
     heads = width // HD
     slots = noise_send.shape[2]
     pairs = experts * slots
@@ -337,21 +337,23 @@
             "tensor", lax.rem(me_t + d, tensor),
         )
 
-    def first_copy(d, arriving):
+    def first_copy(which, d, arriving):
+        parts_of = (slice(0, 3), slice(3, 4))[which]
+        src = w_ref.at[me_t, parts_of, mine] if which else w_qkv_own.at[:, mine]
         return line_copy(
-            w_own_ref.at[mine], lambda owner: w_ref.at[owner, mine], first_sems, d, arriving
+            src, lambda owner: w_ref.at[owner, parts_of, mine], first_sems.at[which], d, arriving
         )
 
     def plane_copy(z, k, arriving):
         owner = lax.rem(me_t + tensor - z, tensor)
-        block = w_ref.at[owner, rows_at(chip_place(k, arriving))]
+        block = w_ref.at[owner, :, rows_at(chip_place(k, arriving))]
         return remote(
             block, block, plane_sems.at[0, z, k], plane_sems.at[1, z, k], "expert", chip_after(k)
         )
 
     def pair_copy(z, arriving):
         owner = lax.rem(me_t + tensor - z, tensor)
-        block = w_ref.at[owner, half_at(CORES - 1 - core if arriving else core)]
+        block = w_ref.at[owner, :, half_at(CORES - 1 - core if arriving else core)]
         return remote(
             block, block, pair_sems.at[0, z], pair_sems.at[1, z], "expert",
             me_e + CORES - 1 - 2 * core,
@@ -424,12 +426,14 @@
         )
 
     greet((("expert", experts), ("tensor", tensor)))
-    each(tensor, lambda d: first_copy(d, False).start())
+    each(tensor, lambda d: first_copy(0, d, False).start())
     line_in = Line(tensor, w_in_own, w_in_all, in_sems.at[0], in_sems.at[1])
     line_back = Line(tensor, w_back_own, w_back_all, in_back_sems.at[0], in_back_sems.at[1])
+    w_ref[me_t, 3] = w_out_own[...].T
+    each(tensor, lambda d: first_copy(1, d, False).start())
     line_in.start(0)
     keep = [
-        pltpu.make_async_copy(w_own_ref, w_ref.at[me_t], own_sem.at[0]),
+        pltpu.make_async_copy(w_qkv_own, w_ref.at[me_t, 0:3], own_sem.at[0]),
         pltpu.make_async_copy(w_in_own, w_in_all.at[me_t], own_sem.at[1]),
         pltpu.make_async_copy(w_back_own, w_back_all.at[me_t], own_sem.at[2]),
     ]
@@ -450,8 +454,14 @@
             narrow[i * SEQ : (i + 1) * SEQ, :] = padded[i * SP : i * SP + SEQ, :]
         return narrow[0:own_rows, :]
 
-    spread(noise_ref[...], rows_ref)
-    noise = rows_ref[...].T[0:experts, :]
+    def spread_lanes(packed, fill):
+        gap = jnp.full((packed.shape[0], SP - SEQ), fill, F32)
+        blocks = []
+        for i in range(images):
+            blocks += [packed[:, i * SEQ : (i + 1) * SEQ], gap]
+        return jnp.concatenate(blocks, axis=1)
+
+    noise = spread_lanes(noise_ref[...], 0.0)
     high = noise.astype(BF).astype(F32)
     middle = (noise - high).astype(BF).astype(F32)
     low = noise - high - middle
@@ -459,8 +469,14 @@
     if noise_send.shape[1] > 3 * experts:
         noise_parts.append(jnp.zeros((noise_send.shape[1] - 3 * experts, noise.shape[1]), F32))
     noise = jnp.concatenate(noise_parts, axis=0).astype(BF)
-    spread(slots_by_row(routes_ref[...], experts), rows_ref, -1.0)
-    lanes_ref[...] = rows_ref[...].T[0:experts, :]
+    slots_by = slots_by_lane(spread_lanes(routes_ref[...].astype(F32), -1.0), experts)
+    lanes_ref[...] = slots_by
+    no_slots = jnp.zeros((LANES - experts, slots_by.shape[1]), F32)
+    rows_ref[...] = jnp.concatenate([slots_by, no_slots], axis=0).T
+    no_router = jnp.zeros((LANES - experts, D), F32)
+    w_router_ref[...] = jnp.concatenate(
+        [router_own[...].astype(F32), no_router], axis=0
+    ).astype(BF)
     spread(cotangent_ref[...].astype(F32), cot_ref)
     cot_low = cot_ref[...].astype(BF)
     spot = ids((slots, lanes_ref.shape[1]), 0).astype(F32)
@@ -469,7 +485,8 @@
         return (spot == lanes_ref[pl.ds(e, 1), :]).astype(F32).astype(BF)
 
     def forward_piece(z):
-        first_copy(z, True).wait_recv()
+        first_copy(0, z, True).wait_recv()
+        first_copy(1, z, True).wait_recv()
         each(chips, lambda k: plane_copy(z, k, False).start())
 
     each(tensor, forward_piece)
@@ -502,10 +519,13 @@
     keep[0].wait()
     each(tensor, lambda z: pair_copy(z, True).wait_recv())
 
+    def qkv_weights(t):
+        return jnp.concatenate([w_ref[t, c] for c in range(3)], axis=1)
+
     lane = ids((SP, width), 1) // HD
     live = ids((SP, SP), 1) < SEQ
     for t in range(tensor):
-        qkv_ref[t] = mm(normed1, w_ref[t, :, 0 : 3 * width]).astype(BF)
+        qkv_ref[t] = mm(normed1, qkv_weights(t)).astype(BF)
         for i in range(images):
             rows = slice(i * SP, (i + 1) * SP)
             q = qkv_ref[t, rows, 0:width]
@@ -524,7 +544,7 @@
             mixed_ref[t, rows, :] = mixed.astype(BF)
     residual = x
     for t in range(tensor):
-        residual = residual + mm(mixed_ref[t], w_ref[t, :, 3 * width : wide], NT)
+        residual = residual + mm(mixed_ref[t], w_ref[t, 3], NT)
     residual_ref[...] = residual
     unit2, inverse2 = unit_norm(residual)
     normed2 = (unit2 * gain2_ref[...]).astype(BF)
@@ -577,7 +597,7 @@
         came = routed_ref[rows, :]
         added = [mm(noise_all[at * group + k], fold, TN) for k in range(group)]
         added = added[0] if group == 1 else jnp.concatenate(added, axis=0)
-        logits = jnp.where(expert_lane < experts, mm(came, w_router_ref[...]) + added, -1e30)
+        logits = jnp.where(expert_lane < experts, mm(came, w_router_ref[...], NT) + added, -1e30)
         power = jnp.exp(logits - jnp.max(logits, -1, keepdims=True))
         router = power / jnp.sum(power, -1, keepdims=True)
         router_ref[rows, :] = router
@@ -684,7 +704,7 @@
         back = back + early_send[rows, :].astype(F32)
         d_gate = jnp.sum(early_ref[rows, :].astype(F32) * out, -1, keepdims=True)
         d_logits = (d_gate * (own_lane.astype(F32) - router)).astype(BF)
-        early_send[rows, :] = (back + mm(d_logits, w_router_ref[...], NT)).astype(BF)
+        early_send[rows, :] = (back + mm(d_logits, w_router_ref[...])).astype(BF)
         send_ref[rows, :] = (gate * out).astype(BF)
         small_ref[0:experts, :] += mm(d_logits, routed_ref[rows, :], TN)[0:experts]
         for k in range(group):
@@ -721,7 +741,7 @@
     normed1 = (unit1 * gain1_ref[...]).astype(BF)
     for t in range(tensor):
         wide_ref[:, t * wide + 3 * width : (t + 1) * wide] = mm(d_attention, mixed_ref[t], TN).astype(BF)
-        d_mixed = mm(d_attention, w_ref[t, :, 3 * width : wide]).astype(BF)
+        d_mixed = mm(d_attention, w_ref[t, 3]).astype(BF)
         for i in range(images):
             rows = slice(i * SP, (i + 1) * SP)
             q = qkv_ref[t, rows, 0:width]
@@ -755,7 +775,7 @@
     next_sum()
     d_normed1 = None
     for t in range(tensor):
-        part = mm(qkv_ref[t], w_ref[t, :, 0 : 3 * width], NT)
+        part = mm(qkv_ref[t], qkv_weights(t), NT)
         d_normed1 = part if d_normed1 is None else d_normed1 + part
     d_rows, norm1 = norm_back(d_normed1, unit1, inverse1, gain1_ref[...])
     small_ref[experts : experts + 1, :] = norm1
@@ -826,7 +846,8 @@
     each(experts, sent)
 
     def sent_line(d):
-        first_copy(d, False).wait_send()
+        first_copy(0, d, False).wait_send()
+        first_copy(1, d, False).wait_send()
         piece_copy(d, False).wait_send()
         small_line_copy(d, False).wait_send()
         pair_copy(d, False).wait_send()
@@ -836,6 +857,24 @@
     for t in range(tensor):
         w_pair_copy(t).wait_send()
         each(chips, lambda k, t=t: w_copy(t, k, False).wait_send())
+
+
+def finish_kernel(
+    experts, output_in, tokens_in, w_sum_ref, small_ref, in_ref, back_ref,
+    output_ref, tokens_ref, norm1_ref, qkv_ref, out_ref, norm2_ref, router_ref,
+    in_grad_ref, back_grad_ref,
+):
+    output_ref[...] = output_in[...]
+    tokens_ref[...] = tokens_in[...]
+    width = out_ref.shape[0]
+    for c in range(3):
+        qkv_ref[c] = w_sum_ref[:, c * width : (c + 1) * width].astype(F32)
+    out_ref[...] = w_sum_ref[:, 3 * width : 4 * width].T.astype(F32)
+    router_ref[...] = small_ref[0:experts, :]
+    norm1_ref[...] = small_ref[experts : experts + 1, :]
+    norm2_ref[...] = small_ref[experts + 1 : experts + 2, :]
+    in_grad_ref[...] = in_ref[...].astype(F32)
+    back_grad_ref[...] = back_ref[...].astype(F32)
 
 
 def per_device(
@@ -859,8 +898,6 @@
     dma = pltpu.SemaphoreType.DMA
     bf, f32 = (lambda *dims: pltpu.VMEM(dims, BF)), (lambda *dims: pltpu.VMEM(dims, F32))
 
-    w_own = jnp.concatenate([w_qkv.reshape(D, 3 * width), w_out.T], axis=1)
-    w_router_wide = jnp.pad(w_router, ((0, 0), (0, LANES - experts)))
     output, grad_tokens, w_sum, small, grad_in, grad_back = call(
         functools.partial(block_kernel, experts, tensor, images, group),
         (
@@ -872,7 +909,8 @@
             shape((hidden, D)),
         ),
         scratch=(
-            bf(tensor, D, 4 * width),
+            bf(tensor, 4, D, width),
+            bf(LANES, D),
             bf(tensor, D, hidden),
             bf(tensor, hidden, D),
             f32(up(own_rows, TILE), D),
@@ -906,7 +944,7 @@
             f32(small_rows, D),
             f32(tensor, small_rows, D),
             dma((3,)),
-            dma((2, tensor)),
+            dma((2, 2, tensor)),
             dma((2, tensor, experts // CORES)),
             dma((2, tensor)),
             dma((2, 2, tensor - 1)),
@@ -925,24 +963,37 @@
             dma((2, experts)),
             dma((2, tensor)),
         ),
-        far_in=(7, 8, 9),
+        far_in=(8, 9, 10),
         collective_id=0,
         has_side_effects=True,
     )(
-        routes, tokens, cotangent, noise, norm1_gain.reshape(1, D), norm2_gain.reshape(1, D),
-        w_router_wide, w_own, w_in[0], w_back[0],
+        routes.T, tokens, cotangent, noise.T, norm1_gain.reshape(1, D), norm2_gain.reshape(1, D),
+        w_router.T, w_out, w_qkv.transpose(1, 0, 2), w_in[0], w_back[0],
     )
-    w_sum = w_sum.astype(F32)
+    output, grad_tokens, norm1, grad_qkv, grad_out, norm2, router, grad_in, grad_back = call(
+        functools.partial(finish_kernel, experts),
+        (
+            shape((own_rows, D)),
+            shape((own_rows, D), F32),
+            shape((1, D), F32),
+            shape((3, D, width), F32),
+            shape((width, D), F32),
+            shape((1, D), F32),
+            shape((experts, D), F32),
+            shape((D, hidden), F32),
+            shape((hidden, D), F32),
+        ),
+    )(output, grad_tokens, w_sum, small, grad_in, grad_back)
     return (
         output,
         grad_tokens,
-        small[experts],
-        w_sum[:, : 3 * width].reshape(D, 3, width),
-        w_sum[:, 3 * width :].T,
-        small[experts + 1],
-        small[:experts].T,
-        grad_in.astype(F32)[None],
-        grad_back.astype(F32)[None],
+        norm1.reshape(D),
+        grad_qkv.transpose(1, 0, 2),
+        grad_out,
+        norm2.reshape(D),
+        router.T,
+        grad_in[None],
+        grad_back[None],
     )
 
 

time: 177 us -> 165 us (0.932)
  local copies, waits for them, and re-layouts: 12.6 us -> 0 us
  Pallas kernels: 160 us -> 165 us
  other arithmetic: 2.57 us -> 0 us
    unnamed x27 -> x0, local copies, waits for them, and re-layouts: 7.6 us -> none
    pallas_call x1 -> x2, Pallas kernels: 160 us -> 165 us  [run(): pl.pallas_call(body, out_shape=out_shape, in_specs=[spec(place, far_in, p...]
    slice x3 -> x0, local copies, waits for them, and re-layouts: 2.69 us -> none  [the longest x1 1.38 us: per_device(): small[experts + 1]]
where the time goes in v6:
time: 165 us
  Pallas kernels  165 us (100%)
    pallas_call x2, Pallas kernels, run(): pl.pallas_call(body, out_shape=out_shape, in_specs=[spec(place, far_in, p...  165 us

profile of v6, /device:TPU:0, one launch (start us, length us, event | category | flops | bytes accessed | tf_op | source)
XLA Modules:
  0.0 165.2 jit_solution(12736263266298681428)
XLA Ops:
  0.6 160.6 %shard_map.178 = (bf16[394,512]{1,0:T(8,128)(2,1)}, f32[394,512]{1,0:T(8,128)}, bf16[512,512]{1,0:T(8,128)(2,1)}, f32[16,512]{1,0:T(8,128)}, bf16[512,512]{1,0:T(8,128)(2,1)}, /*index=5*/bf16[512,512]{1,0:T(8,128)(2,1)}) custom-call(s32[2,394]{1,0:T(2,128)} %bitcast.19, bf16[394,512]{1,0:T(8,128)(2,1)} %tokens_ref.1, bf16[394,512]{1,0:T(8,128)(2,1)} %cotangent_ref.1, ...), custom_call_target="tpu_custom_call" | custom-call | tf_op jit(solution)/shard_map/pallas_call | solution.py:50
  161.3 3.9 %shard_map.179 = (bf16[394,512]{1,0:T(8,128)(2,1)}, f32[394,512]{1,0:T(8,128)}, f32[1,512]{1,0:T(1,128)}, f32[3,512,128]{2,1,0:T(8,128)}, f32[128,512]{1,0:T(8,1...) custom-call(bf16[394,512]{1,0:T(8,128)(2,1)} %get-tuple-element.24.output_in, ...), custom_call_target="tpu_custom_call" | custom-call | tf_op jit(solution)/shard_map/pallas_call | solution.py:50

commit v7 on v6

--- a/solution.py
+++ b/solution.py
@@ -15,6 +15,8 @@
 LANES = 128
 TILE = 16
 EPSILON = 1e-06
+DENSITY = 0.3989422804014327
+TAIL = 0.5 / DENSITY
 BF = jnp.bfloat16
 F32 = jnp.float32
 VMEM_BYTES = 62 * 1024 * 1024
@@ -188,15 +190,18 @@
 
 
 def gelu_parts(pre):
-    density = jnp.exp(pre * pre * -0.5)
-    size = jnp.abs(pre) * (0.5**0.5)
-    t = 1.0 / (1.0 + 0.3275911 * size)
+    density = jnp.exp2(pre * pre * (-0.5 * 1.4426950408889634)) * DENSITY
+    t = pl.reciprocal(1.0 + jnp.abs(pre * (0.3275911 * 0.5**0.5)), approx=True)
     series = t * (
-        0.254829592
-        + t * (-0.284496736 + t * (1.421413741 + t * (-1.453152027 + t * 1.061405429)))
+        0.254829592 * TAIL
+        + t
+        * (
+            -0.284496736 * TAIL
+            + t * (1.421413741 * TAIL + t * (-1.453152027 * TAIL + t * (1.061405429 * TAIL)))
+        )
     )
-    tail = 0.5 * series * density
-    return jnp.where(pre < 0, tail, 1.0 - tail), density * 0.3989422804014327
+    tail = series * density
+    return jnp.where(pre < 0, tail, 1.0 - tail), density
 
 
 class Sums:
@@ -405,10 +410,21 @@
         pair_sum = wide_ref[ours, columns(t)].astype(F32) + pair_ref[t].astype(F32)
         wide_ref[ours, columns(t)] = pair_sum.astype(BF)
         each(chips, lambda k: w_copy(t, k, False).start())
+        pieces[me_e // CORES, t] = wide_ref[mine, columns(t)]
+
+    def plane_sum(t):
+        each(chips, lambda k: w_copy(t, k, True).wait_recv())
+        total = pieces[0, t].astype(F32)
+        for e in range(1, chips):
+            total = total + pieces[e, t].astype(F32)
+        return total.astype(BF)
+
+    def send_piece(t):
+        piece_send[t] = plane_sum(t)
+        piece_copy(t + 1, False).start()
 
     def piece_copy(d, arriving):
-        src = piece_send.at[lax.rem(me_t + d, tensor)]
-        return line_copy(src, lambda owner: piece_line.at[owner], piece_sems, d, arriving)
+        return line_copy(piece_send.at[d - 1], lambda owner: piece_line.at[owner], piece_sems, d, arriving)
 
     def final_copy(d, arriving):
         block = w_sum_ref.at[rows_at(place(d, arriving))]
@@ -603,11 +619,29 @@
         router_ref[rows, :] = router
         gate = jnp.sum(jnp.where(expert_lane == me_e, router, 0.0), -1, keepdims=True)
         early_ref[rows, :] = (gate * early_ref[rows, :].astype(F32)).astype(BF)
-        for f in range(parts):
-            pre = mm(came, w_in_all[f])
+        half_rows, block = chunk // 2, min(256, w_in_all.shape[2])
+
+        def spot_of(r):
+            return pl.ds(pl.multiple_of(at * chunk + r * half_rows, TILE), half_rows)
+
+        cuts = [
+            (f, n, r)
+            for f in range(parts)
+            for n in range(0, w_in_all.shape[2], block)
+            for r in range(2)
+        ]
+
+        def pre_of(f, n, r):
+            return mm(routed_ref[spot_of(r), :], w_in_all[f, :, n : n + block])
+
+        ahead = pre_of(*cuts[0])
+        for number, (f, n, r) in enumerate(cuts):
+            pre = ahead
+            if number + 1 < len(cuts):
+                ahead = pre_of(*cuts[number + 1])
             normal, density = gelu_parts(pre)
-            hidden_ref[f, rows, :] = (pre * normal).astype(BF)
-            slope_ref[f, rows, :] = (normal + pre * density).astype(BF)
+            hidden_ref[f, spot_of(r), n : n + block] = (pre * normal).astype(BF)
+            slope_ref[f, spot_of(r), n : n + block] = (normal + pre * density).astype(BF)
         return 0
 
     lax.fori_loop(0, groups, hidden_units, 0)
@@ -634,7 +668,7 @@
         for f in order:
             block = mm(wide_ref[:, 0:pairs], right[f, 0:pairs, :]).astype(BF)
             grads_at(f, part)[...] = block
-            for step in range(tensor - 1):
+            for step in range(tensor - 1 if part else 1):
                 for way, to in ((0, tensor - 1 - step), (1, step)):
                     if to == f:
                         sums.start_first(way, step, part)
@@ -694,7 +728,7 @@
     line_back.arrive(tensor - 2)
 
     def far_rows(turn, _):
-        at = lax.rem(me_e // group + groups - turn, groups)
+        at = lax.rem(me_e // group + 1 + turn, groups)
         rows = block_rows(at)
         router = router_ref[rows, :]
         own_lane = expert_lane == me_e
@@ -739,8 +773,10 @@
     scaling = HD ** (-0.5)
     unit1, inverse1 = unit_norm(x_ref[...])
     normed1 = (unit1 * gain1_ref[...]).astype(BF)
-    for t in range(tensor):
-        wide_ref[:, t * wide + 3 * width : (t + 1) * wide] = mm(d_attention, mixed_ref[t], TN).astype(BF)
+    for turn in range(tensor):
+        t = lax.rem(me_t + 1 + turn, tensor)
+        first = turn * wide
+        wide_ref[:, first + 3 * width : first + wide] = mm(d_attention, mixed_ref[t], TN).astype(BF)
         d_mixed = mm(d_attention, w_ref[t, 3]).astype(BF)
         for i in range(images):
             rows = slice(i * SP, (i + 1) * SP)
@@ -767,33 +803,41 @@
             qkv_ref[t, rows, 0:width] = dq.astype(BF)
             qkv_ref[t, rows, width : 2 * width] = dk.astype(BF)
             qkv_ref[t, rows, 2 * width : 3 * width] = dv.astype(BF)
-        wide_ref[:, t * wide : t * wide + 3 * width] = mm(normed1, qkv_ref[t], TN).astype(BF)
-        w_pair_copy(t).start()
-        if t > 0:
-            share_pair_sum(t - 1)
+        wide_ref[:, first : first + 3 * width] = mm(normed1, qkv_ref[t], TN).astype(BF)
+        w_pair_copy(turn).start()
+        if turn > 0:
+            share_pair_sum(turn - 1)
+        if turn > 2:
+            send_piece(turn - 3)
     share_pair_sum(tensor - 1)
     next_sum()
+    sent = max(tensor - 3, 0)
+    for turn in range(sent, tensor - 2):
+        send_piece(turn)
+    for step in range(1, tensor - 2):
+        for way in (0, 1):
+            sums.start_first(way, step, 0)
     d_normed1 = None
     for t in range(tensor):
         part = mm(qkv_ref[t], qkv_weights(t), NT)
         d_normed1 = part if d_normed1 is None else d_normed1 + part
     d_rows, norm1 = norm_back(d_normed1, unit1, inverse1, gain1_ref[...])
     small_ref[experts : experts + 1, :] = norm1
+    send_piece(tensor - 2)
     each(experts, lambda d: small_copy(d, False).start())
     each(experts, lambda d: out_copy(d, False).start())
+    for way in (0, 1):
+        sums.start_first(way, tensor - 2, 0)
     small_plane[me_e] = small_ref[...]
     tokens_grad_ref[...] = compact(cot_ref[...] + d_rows)
 
-    for t in range(tensor):
-        pieces[me_e // CORES, t] = wide_ref[mine, columns(t)]
-    for t in range(tensor):
-        each(chips, lambda k, t=t: w_copy(t, k, True).wait_recv())
-        total = pieces[0, t].astype(F32)
-        for e in range(1, chips):
-            total = total + pieces[e, t].astype(F32)
-        piece_send[t] = total.astype(BF)
-    each(tensor, lambda d: piece_copy(d, False).start())
-    piece_line[me_t] = piece_send[me_t]
+    piece_line[me_t] = plane_sum(tensor - 1)
+    each(tensor, lambda d: piece_copy(d, True).wait_recv())
+    total = piece_line[0].astype(F32)
+    for t in range(1, tensor):
+        total = total + piece_line[t].astype(F32)
+    w_sum_ref[mine, :] = total.astype(BF)
+    each(experts, lambda d: final_copy(d, False).start())
     each(experts, lambda d: small_copy(d, True).wait_recv())
     total = small_plane[0]
     for e in range(1, experts):
@@ -801,12 +845,6 @@
     small_line_send[...] = total
     each(tensor, lambda d: small_line_copy(d, False).start())
     small_line[me_t] = total
-    each(tensor, lambda d: piece_copy(d, True).wait_recv())
-    total = piece_line[0].astype(F32)
-    for t in range(1, tensor):
-        total = total + piece_line[t].astype(F32)
-    w_sum_ref[mine, :] = total.astype(BF)
-    each(experts, lambda d: final_copy(d, False).start())
     while line_steps:
         next_sum()
 
@@ -821,7 +859,7 @@
     small_sum_ref[...] = total
     each(experts, lambda d: final_copy(d, True).wait_recv())
 
-    for part in (0, 1):
+    for part in (1, 0):
         sums.last(part)
         total = grads_at(me_t, part)[...].astype(F32)
         for way in (0, 1):

time: 165 us -> 161 us (0.976)
  Pallas kernels: 165 us -> 160 us
    pallas_call x2, Pallas kernels: 165 us -> 160 us  [run(): pl.pallas_call(body, out_shape=out_shape, in_specs=[spec(place, far_in, p...]
where the time goes in v7:
time: 161 us
  Pallas kernels  160 us (99%)
    pallas_call x2, Pallas kernels, run(): pl.pallas_call(body, out_shape=out_shape, in_specs=[spec(place, far_in, p...  160 us

profile of v7, /device:TPU:0, one launch (start us, length us, event | category | flops | bytes accessed | tf_op | source)
XLA Modules:
  0.0 161.1 jit_solution(9558191477108747697)
XLA Ops:
  0.6 156.6 %shard_map.178 = (bf16[394,512]{1,0:T(8,128)(2,1)}, f32[394,512]{1,0:T(8,128)}, bf16[512,512]{1,0:T(8,128)(2,1)}, f32[16,512]{1,0:T(8,128)}, bf16[512,512]{1,0:T(8,128)(2,1)}, /*index=5*/bf16[512,512]{1,0:T(8,128)(2,1)}) custom-call(s32[2,394]{1,0:T(2,128)} %bitcast.19, bf16[394,512]{1,0:T(8,128)(2,1)} %tokens_ref.1, bf16[394,512]{1,0:T(8,128)(2,1)} %cotangent_ref.1, ...), custom_call_target="tpu_custom_call" | custom-call | tf_op jit(solution)/shard_map/pallas_call | solution.py:52
  157.2 3.9 %shard_map.179 = (bf16[394,512]{1,0:T(8,128)(2,1)}, f32[394,512]{1,0:T(8,128)}, f32[1,512]{1,0:T(1,128)}, f32[3,512,128]{2,1,0:T(8,128)}, f32[128,512]{1,0:T(8,1...) custom-call(bf16[394,512]{1,0:T(8,128)(2,1)} %get-tuple-element.24.output_in, ...), custom_call_target="tpu_custom_call" | custom-call | tf_op jit(solution)/shard_map/pallas_call | solution.py:52

commit v8 on v7

--- a/solution.py
+++ b/solution.py
@@ -137,12 +137,12 @@
     )
 
 
-def each(size, step):
+def each(size, step, first=1):
     def body(d, _):
         step(d)
         return 0
 
-    lax.fori_loop(1, size, body, 0)
+    lax.fori_loop(first, size, body, 0)
 
 
 class Line:
@@ -426,9 +426,18 @@
     def piece_copy(d, arriving):
         return line_copy(piece_send.at[d - 1], lambda owner: piece_line.at[owner], piece_sems, d, arriving)
 
-    def final_copy(d, arriving):
-        block = w_sum_ref.at[rows_at(place(d, arriving))]
-        return remote(block, block, final_sems.at[0, d], final_sems.at[1, d], "expert", after(d))
+    def final_copy(k, arriving):
+        block = w_sum_ref.at[rows_at(chip_place(k, arriving))]
+        return remote(
+            block, block, final_sems.at[0, k], final_sems.at[1, k], "expert", chip_after(k)
+        )
+
+    def final_pair_copy(arriving):
+        block = w_sum_ref.at[half_at(CORES - 1 - core if arriving else core)]
+        return remote(
+            block, block, final_sems.at[0, 0], final_sems.at[1, 0], "expert",
+            me_e + CORES - 1 - 2 * core,
+        )
 
     def small_copy(d, arriving):
         return remote(
@@ -762,6 +771,7 @@
     next_sum()
 
     each(experts, lambda d: back_copy(d, True).wait_recv())
+    out_copy(experts // 2, False).start()
     slots_of = rows_ref[:, 0:experts]
     d_normed2 = take_rows(slots_of, back_ref, experts)
     unit2, inverse2 = unit_norm(residual_ref[...])
@@ -810,13 +820,9 @@
         if turn > 2:
             send_piece(turn - 3)
     share_pair_sum(tensor - 1)
-    next_sum()
     sent = max(tensor - 3, 0)
     for turn in range(sent, tensor - 2):
         send_piece(turn)
-    for step in range(1, tensor - 2):
-        for way in (0, 1):
-            sums.start_first(way, step, 0)
     d_normed1 = None
     for t in range(tensor):
         part = mm(qkv_ref[t], qkv_weights(t), NT)
@@ -824,10 +830,15 @@
     d_rows, norm1 = norm_back(d_normed1, unit1, inverse1, gain1_ref[...])
     small_ref[experts : experts + 1, :] = norm1
     send_piece(tensor - 2)
+    for step in range(1, tensor - 2):
+        for way in (0, 1):
+            sums.start_first(way, step, 0)
     each(experts, lambda d: small_copy(d, False).start())
-    each(experts, lambda d: out_copy(d, False).start())
+    each(experts // 2, lambda d: out_copy(d, False).start())
+    each(experts, lambda d: out_copy(d, False).start(), experts // 2 + 1)
     for way in (0, 1):
         sums.start_first(way, tensor - 2, 0)
+    next_sum()
     small_plane[me_e] = small_ref[...]
     tokens_grad_ref[...] = compact(cot_ref[...] + d_rows)
 
@@ -837,7 +848,7 @@
     for t in range(1, tensor):
         total = total + piece_line[t].astype(F32)
     w_sum_ref[mine, :] = total.astype(BF)
-    each(experts, lambda d: final_copy(d, False).start())
+    each(chips, lambda k: final_copy(k, False).start())
     each(experts, lambda d: small_copy(d, True).wait_recv())
     total = small_plane[0]
     for e in range(1, experts):
@@ -849,6 +860,8 @@
         next_sum()
 
     each(experts, lambda d: out_copy(d, True).wait_recv())
+    each(chips, lambda k: final_copy(k, True).wait_recv())
+    final_pair_copy(False).start()
     output = residual_ref[...] + take_rows(slots_of, routed_ref, experts)
     output_ref[...] = compact(output).astype(BF)
 
@@ -857,7 +870,7 @@
     for t in range(1, tensor):
         total = total + small_line[t]
     small_sum_ref[...] = total
-    each(experts, lambda d: final_copy(d, True).wait_recv())
+    final_pair_copy(True).wait_recv()
 
     for part in (1, 0):
         sums.last(part)
@@ -878,7 +891,6 @@
         noise_copy(d, False).wait_send()
         back_copy(d, False).wait_send()
         out_copy(d, False).wait_send()
-        final_copy(d, False).wait_send()
         small_copy(d, False).wait_send()
 
     each(experts, sent)
@@ -892,6 +904,8 @@
         each(chips, lambda k: plane_copy(d, k, False).wait_send())
 
     each(tensor, sent_line)
+    each(chips, lambda k: final_copy(k, False).wait_send())
+    final_pair_copy(False).wait_send()
     for t in range(tensor):
         w_pair_copy(t).wait_send()
         each(chips, lambda k, t=t: w_copy(t, k, False).wait_send())
@@ -997,7 +1011,7 @@
             dma((2, tensor)),
             dma((2, tensor, experts // CORES)),
             dma((2, tensor)),
-            dma((2, experts)),
+            dma((2, experts // CORES)),
             dma((2, experts)),
             dma((2, tensor)),
         ),

time: 161 us -> 160 us (level)
  no operation moved by 1% of the time
where the time goes in v8:
time: 160 us
  Pallas kernels  160 us (100%)
    pallas_call x2, Pallas kernels, run(): pl.pallas_call(body, out_shape=out_shape, in_specs=[spec(place, far_in, p...  160 us

profile of v8, /device:TPU:0, one launch (start us, length us, event | category | flops | bytes accessed | tf_op | source)
XLA Modules:
  0.0 160.2 jit_solution(7535769836732750244)
XLA Ops:
  0.6 155.7 %shard_map.178 = (bf16[394,512]{1,0:T(8,128)(2,1)}, f32[394,512]{1,0:T(8,128)}, bf16[512,512]{1,0:T(8,128)(2,1)}, f32[16,512]{1,0:T(8,128)}, bf16[512,512]{1,0:T(8,128)(2,1)}, /*index=5*/bf16[512,512]{1,0:T(8,128)(2,1)}) custom-call(s32[2,394]{1,0:T(2,128)} %bitcast.19, bf16[394,512]{1,0:T(8,128)(2,1)} %tokens_ref.1, bf16[394,512]{1,0:T(8,128)(2,1)} %cotangent_ref.1, ...), custom_call_target="tpu_custom_call" | custom-call | tf_op jit(solution)/shard_map/pallas_call | solution.py:52
  156.3 3.9 %shard_map.179 = (bf16[394,512]{1,0:T(8,128)(2,1)}, f32[394,512]{1,0:T(8,128)}, f32[1,512]{1,0:T(1,128)}, f32[3,512,128]{2,1,0:T(8,128)}, f32[128,512]{1,0:T(8,1...) custom-call(bf16[394,512]{1,0:T(8,128)(2,1)} %get-tuple-element.24.output_in, ...), custom_call_target="tpu_custom_call" | custom-call | tf_op jit(solution)/shard_map/pallas_call | solution.py:52

commit v9 on v8

--- a/solution.py
+++ b/solution.py
@@ -386,7 +386,7 @@
         return flat_copy(early_send, back_ref, back_sems, d, arriving)
 
     def out_copy(d, arriving):
-        return flat_copy(send_ref, routed_ref, out_sems, d, arriving)
+        return flat_copy(send_ref, early_ref, out_sems, d, arriving)
 
     def columns(t):
         return slice(t * wide, (t + 1) * wide)
@@ -749,7 +749,7 @@
         d_logits = (d_gate * (own_lane.astype(F32) - router)).astype(BF)
         early_send[rows, :] = (back + mm(d_logits, w_router_ref[...])).astype(BF)
         send_ref[rows, :] = (gate * out).astype(BF)
-        small_ref[0:experts, :] += mm(d_logits, routed_ref[rows, :], TN)[0:experts]
+        router_ref[rows, :] = d_logits.astype(F32)
         for k in range(group):
             e = at * group + k
             d = lax.rem(e + experts - me_e, experts)
@@ -761,28 +761,34 @@
             @pl.when(d == 0)
             def _(e=e):
                 back_ref[slot_rows(e), :] = early_send[slot_rows(e), :]
-                routed_ref[slot_rows(e), :] = send_ref[slot_rows(e), :]
+                early_ref[slot_rows(e), :] = send_ref[slot_rows(e), :]
 
         return 0
 
     lax.fori_loop(0, groups, far_rows, 0)
 
     weight_grads(0, slope_ref)
-    next_sum()
-
+
+    def router_part(at, _):
+        rows = block_rows(at)
+        d_logits = router_ref[rows, :].astype(BF)
+        small_ref[0:experts, :] += mm(d_logits, routed_ref[rows, :], TN)[0:experts]
+        return 0
+
+    lax.fori_loop(0, groups, router_part, 0)
+    unit1, inverse1 = unit_norm(x_ref[...])
+    normed1 = (unit1 * gain1_ref[...]).astype(BF)
+    unit2, inverse2 = unit_norm(residual_ref[...])
     each(experts, lambda d: back_copy(d, True).wait_recv())
     out_copy(experts // 2, False).start()
     slots_of = rows_ref[:, 0:experts]
     d_normed2 = take_rows(slots_of, back_ref, experts)
-    unit2, inverse2 = unit_norm(residual_ref[...])
     d_rows, norm2 = norm_back(d_normed2, unit2, inverse2, gain2_ref[...])
     small_ref[experts + 1 : experts + 2, :] = norm2
     d_residual = cot_ref[...] + d_rows
     cot_ref[...] = d_residual
     d_attention = d_residual.astype(BF)
     scaling = HD ** (-0.5)
-    unit1, inverse1 = unit_norm(x_ref[...])
-    normed1 = (unit1 * gain1_ref[...]).astype(BF)
     for turn in range(tensor):
         t = lax.rem(me_t + 1 + turn, tensor)
         first = turn * wide
@@ -817,6 +823,8 @@
         w_pair_copy(turn).start()
         if turn > 0:
             share_pair_sum(turn - 1)
+        if turn == 0:
+            next_sum()
         if turn > 2:
             send_piece(turn - 3)
     share_pair_sum(tensor - 1)
@@ -862,7 +870,7 @@
     each(experts, lambda d: out_copy(d, True).wait_recv())
     each(chips, lambda k: final_copy(k, True).wait_recv())
     final_pair_copy(False).start()
-    output = residual_ref[...] + take_rows(slots_of, routed_ref, experts)
+    output = residual_ref[...] + take_rows(slots_of, early_ref, experts)
     output_ref[...] = compact(output).astype(BF)
 
     each(tensor, lambda d: small_line_copy(d, True).wait_recv())

time: 160 us -> 160 us (level)
  no operation moved by 1% of the time
where the time goes in v9:
time: 160 us; the launch traced here: 159 us
  Pallas kernels  159 us (99%)
    pallas_call x2, Pallas kernels, run(): pl.pallas_call(body, out_shape=out_shape, in_specs=[spec(place, far_in, p...  159 us

profile of v9, /device:TPU:0, one launch (start us, length us, event | category | flops | bytes accessed | tf_op | source)
XLA Modules:
  0.0 159.4 jit_solution(7706430323719754743)
XLA Ops:
  0.6 154.9 %shard_map.178 = (bf16[394,512]{1,0:T(8,128)(2,1)}, f32[394,512]{1,0:T(8,128)}, bf16[512,512]{1,0:T(8,128)(2,1)}, f32[16,512]{1,0:T(8,128)}, bf16[512,512]{1,0:T(8,128)(2,1)}, /*index=5*/bf16[512,512]{1,0:T(8,128)(2,1)}) custom-call(s32[2,394]{1,0:T(2,128)} %bitcast.19, bf16[394,512]{1,0:T(8,128)(2,1)} %tokens_ref.1, bf16[394,512]{1,0:T(8,128)(2,1)} %cotangent_ref.1, ...), custom_call_target="tpu_custom_call" | custom-call | tf_op jit(solution)/shard_map/pallas_call | solution.py:52
  155.5 3.9 %shard_map.179 = (bf16[394,512]{1,0:T(8,128)(2,1)}, f32[394,512]{1,0:T(8,128)}, f32[1,512]{1,0:T(1,128)}, f32[3,512,128]{2,1,0:T(8,128)}, f32[128,512]{1,0:T(8,1...) custom-call(bf16[394,512]{1,0:T(8,128)(2,1)} %get-tuple-element.24.output_in, ...), custom_call_target="tpu_custom_call" | custom-call | tf_op jit(solution)/shard_map/pallas_call | solution.py:52

commit v10 on v9

--- a/solution.py
+++ b/solution.py
@@ -737,7 +737,8 @@
     line_back.arrive(tensor - 2)
 
     def far_rows(turn, _):
-        at = lax.rem(me_e // group + 1 + turn, groups)
+        ours, across = me_e // group, groups // 2
+        at = 2 * lax.rem(ours // 2 + 1 + turn // 2, across) + lax.rem(ours + 1 + turn, 2)
         rows = block_rows(at)
         router = router_ref[rows, :]
         own_lane = expert_lane == me_e

time: 160 us -> 160 us (level)
  no operation moved by 1% of the time
where the time goes in v10:
time: 160 us
  Pallas kernels  159 us (99%)
    pallas_call x2, Pallas kernels, run(): pl.pallas_call(body, out_shape=out_shape, in_specs=[spec(place, far_in, p...  159 us

profile of v10, /device:TPU:0, one launch (start us, length us, event | category | flops | bytes accessed | tf_op | source)
XLA Modules:
  0.0 159.8 jit_solution(17123724002032818325)
XLA Ops:
  0.6 155.2 %shard_map.178 = (bf16[394,512]{1,0:T(8,128)(2,1)}, f32[394,512]{1,0:T(8,128)}, bf16[512,512]{1,0:T(8,128)(2,1)}, f32[16,512]{1,0:T(8,128)}, bf16[512,512]{1,0:T(8,128)(2,1)}, /*index=5*/bf16[512,512]{1,0:T(8,128)(2,1)}) custom-call(s32[2,394]{1,0:T(2,128)} %bitcast.19, bf16[394,512]{1,0:T(8,128)(2,1)} %tokens_ref.1, bf16[394,512]{1,0:T(8,128)(2,1)} %cotangent_ref.1, ...), custom_call_target="tpu_custom_call" | custom-call | tf_op jit(solution)/shard_map/pallas_call | solution.py:52
  155.9 3.9 %shard_map.179 = (bf16[394,512]{1,0:T(8,128)(2,1)}, f32[394,512]{1,0:T(8,128)}, f32[1,512]{1,0:T(1,128)}, f32[3,512,128]{2,1,0:T(8,128)}, f32[128,512]{1,0:T(8,1...) custom-call(bf16[394,512]{1,0:T(8,128)(2,1)} %get-tuple-element.24.output_in, ...), custom_call_target="tpu_custom_call" | custom-call | tf_op jit(solution)/shard_map/pallas_call | solution.py:52
